TPU v7x, 128 devices: a whole 4x4x4 slice. The times are simulated.
128 devices in a mesh: fsdp: 16 (over x, z_lo, core), tp: 8 (over y, z_hi).
Axes of the slice: x: 4, y: 4, z: 4 (z_hi: 2, z_lo: 2; z = z_hi * 2 + z_lo), core: 2. Of those that a mesh axis runs over, the one named last changes fastest.
Arguments:
- tokens: bfloat16 [20480, 1024], P(('fsdp', 'tp')), may hold values from -6 to 6
- gain_attn: float32 [1024], replicated, may hold values from 0.25 to 1.75
- w_qkv: bfloat16 [1024, 3, 1024], P('fsdp', None, 'tp'), may hold values from -0.1875 to 0.1875
- w_out: bfloat16 [1024, 1024], P('fsdp', 'tp'), may hold values from -6 to 6
- gain_mlp: float32 [1024], replicated, may hold values from 0.25 to 1.75
- w_in: bfloat16 [1024, 2, 2624], P('fsdp', None, 'tp'), may hold values from -0.1875 to 0.1875
- w_down: bfloat16 [1024, 2624], P('fsdp', 'tp'), may hold values from -0.125 to 0.125
- cotangent: bfloat16 [20480, 1024], P(('fsdp', 'tp')), may hold values from -6 to 6
Outputs:
- layer_out: bfloat16 [20480, 1024], P(('fsdp', 'tp'))
- grad_tokens: bfloat16 [20480, 1024], P(('fsdp', 'tp'))
- grad_gain_attn: float32 [1024], replicated
- grad_w_qkv: float32 [1024, 3, 1024], P('fsdp', None, 'tp')
- grad_w_out: float32 [1024, 1024], P('fsdp', 'tp')
- grad_gain_mlp: float32 [1024], replicated
- grad_w_in: float32 [1024, 2, 2624], P('fsdp', None, 'tp')
- grad_w_down: float32 [1024, 2624], P('fsdp', 'tp')
All inputs are finite; a program needn't handle non-finite values.
Results may differ from a plain program's by a relative error of at most 0.029.
Values may be sent and summed in bfloat16 or wider, within the bound.
No kernel may reach another device: no remote copies, remote signals or barrier semaphores. Data moves between devices by JAX's collectives and lax.ppermute only.
A program may use at most 128 MiB of HBM per device.

v0:
```python
import jax
import jax.numpy as jnp
from jax import lax
from jax.sharding import PartitionSpec as P

HD = 64
LEN = 1280
QBLOCK = 640


EPSILON = 1e-05
THETA = 160000.0


def normalize(values):
    centre = values - jnp.mean(values, axis=-1, keepdims=True)
    scaling = lax.rsqrt(jnp.mean(centre * centre, axis=-1, keepdims=True) + EPSILON)
    return (centre * scaling, scaling)


def norm_back(grad_normed, normed_hat, scaling, gain):
    grad_hat = grad_normed * gain
    mean_grad = jnp.mean(grad_hat, axis=-1, keepdims=True)
    mean_proj = jnp.mean(grad_hat * normed_hat, axis=-1, keepdims=True)
    return (
        scaling * (grad_hat - mean_grad - normed_hat * mean_proj),
        jnp.sum(grad_normed * normed_hat, axis=0),
    )


def rope_tables(length, head_size):
    half = head_size // 2
    freqs = THETA ** (-jnp.arange(half, dtype=jnp.float32) * 2.0 / head_size)
    angles = jnp.arange(length, dtype=jnp.float32)[:, None] * freqs[None, :]
    return (jnp.cos(angles), jnp.sin(angles))


def rotate(values, cosine, sine):
    half = values.shape[-1] // 2
    first = values[..., :half]
    second = values[..., half:]
    cosine = cosine[:, None, :]
    sine = sine[:, None, :]
    return jnp.concatenate(
        [first * cosine - second * sine, second * cosine + first * sine], axis=-1
    )


def geglu(pair_in):
    return jax.nn.gelu(pair_in[:, 0], approximate=False) * pair_in[:, 1]


def on_device(tokens, gain_attn, w_qkv, w_out, gain_mlp, w_in, w_down, cotangent):
    score_scale = float(HD) ** (-0.5)
    resid = tokens.astype(jnp.float32)
    hat_attn, scale_attn = normalize(resid)
    normed_attn = (hat_attn * gain_attn).astype(jnp.bfloat16)
    full_qkv, full_out = (
        lax.all_gather(w_qkv, "fsdp", axis=0, tiled=True),
        lax.all_gather(w_out, "fsdp", axis=0, tiled=True),
    )
    rows_attn = lax.all_gather(normed_attn, "tp", axis=0, tiled=True)
    group_rows = rows_attn.shape[0]
    seq_count = group_rows // LEN
    local_width = full_out.shape[1]
    heads = local_width // HD
    pair_count = seq_count * heads
    block_count = LEN // QBLOCK
    qkv = jnp.einsum("td,dcj->tcj", rows_attn, full_qkv, preferred_element_type=jnp.float32)
    cosine, sine = rope_tables(LEN, HD)

    def split_heads(array):
        return array.reshape(seq_count, LEN, heads, HD)

    def to_pairs(array):
        return array.transpose(0, 2, 1, 3).reshape(pair_count, LEN, HD)

    def from_pairs(array):
        return array.reshape(seq_count, heads, LEN, HD).transpose(0, 2, 1, 3)

    queries = rotate(split_heads(qkv[:, 0]), cosine, sine).astype(jnp.bfloat16)
    keys = rotate(split_heads(qkv[:, 1]), cosine, sine).astype(jnp.bfloat16)
    value_rows = split_heads(qkv[:, 2]).astype(jnp.bfloat16)
    pair_q = to_pairs(queries).reshape(pair_count, block_count, QBLOCK, HD)
    pair_k = to_pairs(keys)
    pair_v = to_pairs(value_rows)

    def attend(item):
        query_blocks, key_rows, val_rows = item

        def one_block(query_block):
            scores = (
                jnp.einsum("qd,kd->qk", query_block, key_rows, preferred_element_type=jnp.float32)
                * score_scale
            )
            row_peak = jnp.max(scores, axis=1, keepdims=True)
            exponent = jnp.exp(scores - row_peak)
            row_total = jnp.sum(exponent, axis=1, keepdims=True)
            probability = (exponent / row_total).astype(jnp.bfloat16)
            block_out = jnp.dot(probability, val_rows, preferred_element_type=jnp.float32)
            return (block_out, row_peak + jnp.log(row_total))

        return lax.map(one_block, query_blocks)

    mixed, logsum = lax.map(attend, (pair_q, pair_k, pair_v))
    attn_mixed = (
        from_pairs(mixed.reshape(pair_count, LEN, HD))
        .reshape(group_rows, local_width)
        .astype(jnp.bfloat16)
    )
    row_block = attn_mixed
    attn_sum = lax.psum_scatter(
        jnp.einsum("tj,ej->te", row_block, full_out, preferred_element_type=jnp.float32).astype(
            jnp.bfloat16
        ),
        "tp",
        scatter_dimension=0,
        tiled=True,
    ).astype(jnp.float32)
    resid_mid = resid + attn_sum
    hat_mlp, scale_mlp = normalize(resid_mid)
    normed_mlp = (hat_mlp * gain_mlp).astype(jnp.bfloat16)
    full_in, full_down = (
        lax.all_gather(w_in, "fsdp", axis=0, tiled=True),
        lax.all_gather(w_down, "fsdp", axis=0, tiled=True),
    )
    rows_mlp = lax.all_gather(normed_mlp, "tp", axis=0, tiled=True)
    hidden_in = jnp.einsum("td,dcf->tcf", rows_mlp, full_in, preferred_element_type=jnp.float32)
    activated = geglu(hidden_in).astype(jnp.bfloat16)
    row_block = activated
    mlp_sum = lax.psum_scatter(
        jnp.einsum("tf,ef->te", row_block, full_down, preferred_element_type=jnp.float32).astype(
            jnp.bfloat16
        ),
        "tp",
        scatter_dimension=0,
        tiled=True,
    ).astype(jnp.float32)
    layer_out = (resid_mid + mlp_sum).astype(jnp.bfloat16)
    back_all = lax.all_gather(cotangent, "tp", axis=0, tiled=True)
    grad_act = jnp.dot(back_all, full_down, preferred_element_type=jnp.float32)
    grad_down = jnp.einsum("te,tf->ef", back_all, activated, preferred_element_type=jnp.float32)
    pull_geglu = jax.vjp(geglu, hidden_in)[1]
    grad_hidden = pull_geglu(grad_act)[0].astype(jnp.bfloat16)
    grad_in = jnp.einsum("td,tcf->dcf", rows_mlp, grad_hidden, preferred_element_type=jnp.float32)
    row_block = grad_hidden
    grad_normed_mlp = lax.psum_scatter(
        jnp.einsum("tcf,dcf->td", row_block, full_in, preferred_element_type=jnp.float32).astype(
            jnp.bfloat16
        ),
        "tp",
        scatter_dimension=0,
        tiled=True,
    ).astype(jnp.float32)
    grad_mid_norm, gain_mlp_part = norm_back(grad_normed_mlp, hat_mlp, scale_mlp, gain_mlp)
    grad_mid = cotangent.astype(jnp.float32) + grad_mid_norm
    back_attn = lax.all_gather(grad_mid.astype(jnp.bfloat16), "tp", axis=0, tiled=True)
    grad_out = jnp.einsum("te,tj->ej", back_attn, attn_mixed, preferred_element_type=jnp.float32)
    grad_mixed = jnp.dot(back_attn, full_out, preferred_element_type=jnp.float32).astype(
        jnp.bfloat16
    )
    pair_grad = to_pairs(split_heads(grad_mixed)).reshape(pair_count, block_count, QBLOCK, HD)

    def attend_back(item):
        query_blocks, key_rows, val_rows, grad_blocks, logsum_blocks = item

        def one_block(carry, block_item):
            grad_keys, grad_vals = carry
            query_block, grad_block, logsum_block = block_item
            scores = (
                jnp.einsum("qd,kd->qk", query_block, key_rows, preferred_element_type=jnp.float32)
                * score_scale
            )
            probability = jnp.exp(scores - logsum_block)
            grad_probs = jnp.einsum(
                "qd,kd->qk", grad_block, val_rows, preferred_element_type=jnp.float32
            )
            inner = jnp.sum(grad_probs * probability, axis=1, keepdims=True)
            grad_scores = (probability * (grad_probs - inner)).astype(jnp.bfloat16)
            grad_query = (
                jnp.dot(grad_scores, key_rows, preferred_element_type=jnp.float32) * score_scale
            )
            grad_keys = (
                grad_keys
                + jnp.einsum(
                    "qk,qd->kd", grad_scores, query_block, preferred_element_type=jnp.float32
                )
                * score_scale
            )
            grad_vals = grad_vals + jnp.einsum(
                "qk,qd->kd",
                probability.astype(jnp.bfloat16),
                grad_block,
                preferred_element_type=jnp.float32,
            )
            return ((grad_keys, grad_vals), grad_query)

        zero_rows = jnp.zeros((LEN, HD), jnp.float32)
        totals, grad_queries = lax.scan(
            one_block, (zero_rows, zero_rows), (query_blocks, grad_blocks, logsum_blocks)
        )
        return (grad_queries, totals[0], totals[1])

    grad_q, grad_k, grad_v = lax.map(attend_back, (pair_q, pair_k, pair_v, pair_grad, logsum))
    grad_q = rotate(from_pairs(grad_q.reshape(pair_count, LEN, HD)), cosine, -sine)
    grad_k = rotate(from_pairs(grad_k), cosine, -sine)
    grad_v = from_pairs(grad_v)
    grad_qkv = (
        jnp.stack([grad_q, grad_k, grad_v], axis=2)
        .reshape(group_rows, 3, local_width)
        .astype(jnp.bfloat16)
    )
    grad_qkv_w = jnp.einsum("td,tcj->dcj", rows_attn, grad_qkv, preferred_element_type=jnp.float32)
    row_block = grad_qkv
    grad_normed_attn = lax.psum_scatter(
        jnp.einsum("tcj,dcj->td", row_block, full_qkv, preferred_element_type=jnp.float32).astype(
            jnp.bfloat16
        ),
        "tp",
        scatter_dimension=0,
        tiled=True,
    ).astype(jnp.float32)
    grad_first, gain_attn_part = norm_back(grad_normed_attn, hat_attn, scale_attn, gain_attn)
    grad_tokens = (grad_mid + grad_first).astype(jnp.bfloat16)
    gain_attn_grad, gain_mlp_grad = lax.psum((gain_attn_part, gain_mlp_part), ("fsdp", "tp"))
    grad_qkv_w, grad_out, grad_in, grad_down = (
        lax.psum_scatter(
            grad_qkv_w.astype(jnp.bfloat16), "fsdp", scatter_dimension=0, tiled=True
        ).astype(jnp.float32),
        lax.psum_scatter(
            grad_out.astype(jnp.bfloat16), "fsdp", scatter_dimension=0, tiled=True
        ).astype(jnp.float32),
        lax.psum_scatter(
            grad_in.astype(jnp.bfloat16), "fsdp", scatter_dimension=0, tiled=True
        ).astype(jnp.float32),
        lax.psum_scatter(
            grad_down.astype(jnp.bfloat16), "fsdp", scatter_dimension=0, tiled=True
        ).astype(jnp.float32),
    )
    return (
        layer_out,
        grad_tokens,
        gain_attn_grad,
        grad_qkv_w,
        grad_out,
        gain_mlp_grad,
        grad_in,
        grad_down,
    )


def solution(mesh):
    in_specs = (
        P(("fsdp", "tp"), None),
        P(),
        P("fsdp", None, "tp"),
        P("fsdp", "tp"),
        P(),
        P("fsdp", None, "tp"),
        P("fsdp", "tp"),
        P(("fsdp", "tp"), None),
    )
    out_specs = (
        P(("fsdp", "tp"), None),
        P(("fsdp", "tp"), None),
        P(),
        P("fsdp", None, "tp"),
        P("fsdp", "tp"),
        P(),
        P("fsdp", None, "tp"),
        P("fsdp", "tp"),
    )
    return jax.shard_map(
        on_device, mesh=mesh, in_specs=in_specs, out_specs=out_specs, check_vma=False
    )
```

profile of v0, /device:TPU:0, one launch (start us, length us, event | category | flops | bytes accessed | tf_op | source)
XLA Modules:
  0.0 899.6 jit_solution(1874184017353979466)
XLA Ops:
  12.2 21.2 %all_gather.26 = bf16[1024,128]{1,0:T(8,128)(2,1)S(1)} all-gather(bf16[64,128]{1,0:T(8,128)(2,1)} %param.19), channel_id=1, replica_groups=mesh['fsdp'=16,'tp'=8] {'fsdp'}, dimensions={0}, use_global_device_ids=true | all-gather | bytes 278528 | tf_op jit(solution)/shard_map/all_gather | solution.py:60
  33.3 18.5 %all_gather.25 = bf16[1024,3,128]{2,0,1:T(8,128)(2,1)S(1)} all-gather(bf16[64,3,128]{2,0,1:T(8,128)(2,1)S(1)} %copy-done.36), channel_id=1, replica_groups=mesh['fsdp'=16,'tp'=8] {'fsdp'}, dimensions={0}, use_global_device_ids=true | all-gather | bytes 835584 | tf_op jit(solution)/shard_map/all_gather | solution.py:59
  53.2 21.6 %all-gather.6.cloned.1.call-done = bf16[1280,1024]{1,0:T(8,128)(2,1)} async-done(((bf16[160,1024]{1,0:T(8,128)(2,1)}), bf16[1280,1024]{1,0:T(8,128)(2,1)}) %all-gather.6.cloned.1.call-update) | async-done | bytes 2621456 | tf_op jit(solution)/shard_map/all_gather | solution.py:62
  79.2 10.7 %while.54 = (s32[]{:T(128)}, bf16[2,2,640,64]{2,3,1,0:T(8,128)(2,1)}, f32[2,2,640,1]{2,3,1,0:T(1,128)S(1)}, bf16[2,2,640,64]{3,2,1,0:T(8,128)(2,1)S(1)}, bf16[2,...) while((s32[]{:T(128)}, ...), condition=%wide.region_7.8_spmd, body=%wide.region_2.7_spmd.sunk | while | flops 215448960 | bytes 12165378 | solution.py:105
  79.3 4.5 while.57
  84.6 4.5 while.57
  95.4 74.1 %reduce-scatter.11.cloned.1.call-done = bf16[160,1024]{1,0:T(8,128)(2,1)} async-done(((bf16[1280,1024]{1,0:T(8,128)(2,1)}), bf16[160,1024]{1,0:T(8,128)(2,1)}) %reduce-scatter.11.cloned.1.call-update) | async-done | bytes 327696 | tf_op jit(solution)/shard_map/reduce_scatter | solution.py:112
  173.8 22.8 %all_gather.29 = bf16[1024,328]{1,0:T(8,128)(2,1)} all-gather(bf16[64,328]{1,0:T(8,128)(2,1)S(1)} %copy-done.37), channel_id=1, replica_groups=mesh['fsdp'=16,'tp'=8] {'fsdp'}, dimensions={0}, use_global_device_ids=true | all-gather | bytes 713728 | tf_op jit(solution)/shard_map/all_gather | solution.py:125
  196.6 34.0 %all-gather.12.cloned.1.call-done = bf16[1280,1024]{1,0:T(8,128)(2,1)} async-done(((bf16[160,1024]{1,0:T(8,128)(2,1)}), bf16[1280,1024]{1,0:T(8,128)(2,1)}) %all-gather.12.cloned.1.call-update) | async-done | bytes 2621456 | tf_op jit(solution)/shard_map/all_gather | solution.py:140
  230.6 4.2 fusion.96
  234.8 29.7 %all-gather.10.cloned.1.call-done = bf16[1024,2,328]{2,0,1:T(8,128)(2,1)} async-done(((bf16[64,2,328]{2,0,1:T(8,128)(2,1)}), bf16[1024,2,328]{2,0,1:T(8,128)(2,1)}) %all-gather.10.cloned.1.call-update) | async-done | bytes 1343504 | tf_op jit(solution)/shard_map/all_gather | solution.py:124
  264.5 61.8 %all-gather.8.cloned.1.call-done = bf16[1280,1024]{1,0:T(8,128)(2,1)} async-done(((bf16[160,1024]{1,0:T(8,128)(2,1)}), bf16[1280,1024]{1,0:T(8,128)(2,1)}) %all-gather.8.cloned.1.call-update) | async-done | bytes 2621456 | tf_op jit(solution)/shard_map/all_gather | solution.py:127
  326.3 4.3 fusion.28
  330.6 3.6 multiply_bitcast_fusion
  337.3 3.8 bitcast_convert_fusion.1
  341.2 76.8 %reduce-scatter.15.cloned.1.call-done = bf16[160,1024]{1,0:T(8,128)(2,1)} async-done(((bf16[1280,1024]{1,0:T(8,128)(2,1)}), bf16[160,1024]{1,0:T(8,128)(2,1)}) %reduce-scatter.15.cloned.1.call-update) | async-done | bytes 327696 | tf_op jit(solution)/shard_map/reduce_scatter | solution.py:147
  422.1 3.9 fusion.60
  428.7 6.4 fusion.34
  435.2 44.6 %all-gather.14.cloned.1.call-done = bf16[1280,1024]{1,0:T(8,128)(2,1)} async-done(((bf16[160,1024]{1,0:T(8,128)(2,1)}), bf16[1280,1024]{1,0:T(8,128)(2,1)}) %all-gather.14.cloned.1.call-update) | async-done | bytes 2621456 | tf_op jit(solution)/shard_map/all_gather | solution.py:157
  483.6 57.0 %while.56 = (s32[]{:T(128)}, f32[2,2,640,64]{2,1,3,0:T(2,128)}, f32[2,1280,64]{1,2,0:T(8,128)}, bf16[2,1280,64]{1,2,0:T(8,128)(2,1)}, bf16[2,2,640,64]{3,2,1,0:T...) while((s32[]{:T(128)}, f32[2,2,640,64]{2,1,3,0:T(2,128)}, ...), condition=%wide.region_19.20_spmd, body=%wide.region_15.19_spmd.sunk | while | flops 531291520 | bytes 50652384 | solution.py:204
  487.8 20.3 %while.58 = (s32[]{:T(128)}, f32[1280,64]{0,1:T(8,128)}, f32[1280,64]{0,1:T(8,128)}, f32[2,640,64]{1,2,0:T(8,128)}, bf16[2,640,64]{2,1,0:T(8,128)(2,1)}, /*index...) while((s32[]{:T(128)}, f32[1280,64]{0,1:T(8,128)}, ...), condition=%wide.region_18.18_spmd.clone, body=%wide.region_16.17_spmd.clone.sunk | while | flops 531291520 | bytes 39499592 | solution.py:199
  516.3 20.3 %while.58 = (s32[]{:T(128)}, f32[1280,64]{0,1:T(8,128)}, f32[1280,64]{0,1:T(8,128)}, f32[2,640,64]{1,2,0:T(8,128)}, bf16[2,640,64]{2,1,0:T(8,128)(2,1)}, /*index...) while((s32[]{:T(128)}, f32[1280,64]{0,1:T(8,128)}, ...), condition=%wide.region_18.18_spmd.clone, body=%wide.region_16.17_spmd.clone.sunk | while | flops 531291520 | bytes 39499592 | solution.py:199
  542.3 3.4 convolution_convert_fusion.4
  547.2 4.3 fusion.57
  551.5 3.0 bitcast_convert_fusion
  555.9 3.1 convolution_convert_fusion
  561.0 44.8 %reduce-scatter.23.cloned.1.call-done = bf16[64,2,328]{2,0,1:T(8,128)(2,1)} async-done(((bf16[1024,2,328]{2,0,1:T(8,128)(2,1)}), bf16[64,2,328]{2,0,1:T(8,128)(2,1)}) %reduce-scatter.23.cloned.1.call-update) | async-done | bytes 83984 | tf_op jit(solution)/shard_map/reduce_scatter | solution.py:233
  607.5 59.8 %reduce-scatter.21.cloned.1.call-done = bf16[64,128]{1,0:T(8,128)(2,1)} async-done(((bf16[1024,128]{1,0:T(8,128)(2,1)}), bf16[64,128]{1,0:T(8,128)(2,1)}) %reduce-scatter.21.cloned.1.call-update) | async-done | bytes 16400 | tf_op jit(solution)/shard_map/reduce_scatter | solution.py:230
  668.6 61.0 %reduce-scatter.19.cloned.1.call-done = bf16[64,3,128]{2,0,1:T(8,128)(2,1)} async-done(((bf16[1024,3,128]{2,0,1:T(8,128)(2,1)}), bf16[64,3,128]{2,0,1:T(8,128)(2,1)}) %reduce-scatter.19.cloned.1.call-update) | async-done | bytes 49168 | tf_op jit(solution)/shard_map/reduce_scatter | solution.py:227
  731.1 78.8 %reduce-scatter.17.cloned.1.call-done = bf16[160,1024]{1,0:T(8,128)(2,1)} async-done(((bf16[1280,1024]{1,0:T(8,128)(2,1)}), bf16[160,1024]{1,0:T(8,128)(2,1)}) %reduce-scatter.17.cloned.1.call-update) | async-done | bytes 327696 | tf_op jit(solution)/shard_map/reduce_scatter | solution.py:215
  811.3 66.8 %all-reduce.2 = (f32[1024]{0:T(1024)}, f32[1024]{0:T(1024)}) all-reduce(f32[1024]{0:T(1024)S(1)} %get-tuple-element.278, f32[1024]{0:T(1024)S(1)} %copy-done.47), channel_id=1, replica_groups=mesh['fsdp'=16,'tp'=8] {'fsdp','tp'}, use_global_device_ids=true, to_apply=%region_24.25 | all-reduce | flops 2048 | bytes 16384 | tf_op jit(solution)/shard_map/psum | solution.py:225
  878.1 12.4 %reduce-scatter.13.cloned.1.call-done = bf16[160,1024]{1,0:T(8,128)(2,1)} async-done(((bf16[1280,1024]{1,0:T(8,128)(2,1)}), bf16[160,1024]{1,0:T(8,128)(2,1)}) %reduce-scatter.13.cloned.1.call-update) | async-done | bytes 327696 | tf_op jit(solution)/shard_map/reduce_scatter | solution.py:131
  (320 shorter events, 115.6 us)
Async XLA Ops:
  7.2 67.6 %all-gather.6.cloned.1.call-start = ((), (), s32[]{:S(2)}) async-start(), calls=%async_computation.8 | async-start | bytes 2949120 | tf_op jit(solution)/shard_map/all_gather | solution.py:62
  12.1 157.4 %reduce-scatter.11.cloned.1.call-start = ((), (), s32[]{:S(2)}) async-start(), calls=%async_computation.9 | async-start | bytes 2949120 | tf_op jit(solution)/shard_map/reduce_scatter | solution.py:112
  93.8 78.1 %copy-start.34 = (f32[1024]{0:T(1024)S(1)}, f32[1024]{0:T(1024)}, u32[]{:S(2)}) copy-start(f32[1024]{0:T(1024)} %param.20) | copy-start | bytes 12292
  93.8 80.0 %copy-start.37 = (bf16[64,328]{1,0:T(8,128)(2,1)S(1)}, bf16[64,328]{1,0:T(8,128)(2,1)}, u32[]{:S(2)}) copy-start(bf16[64,328]{1,0:T(8,128)(2,1)} %param.22) | copy-start | bytes 125956
  93.8 136.8 %all-gather.12.cloned.1.call-start = ((), (), s32[]{:S(2)}) async-start(), calls=%async_computation.13 | async-start | bytes 2949120 | tf_op jit(solution)/shard_map/all_gather | solution.py:140
  94.6 169.9 %all-gather.10.cloned.1.call-start = ((), (), s32[]{:S(2)}) async-start(), calls=%async_computation.11 | async-start | bytes 1671168 | tf_op jit(solution)/shard_map/all_gather | solution.py:124
  95.3 230.9 %all-gather.8.cloned.1.call-start = ((), (), s32[]{:S(2)}) async-start(), calls=%async_computation.10 | async-start | bytes 2949120 | tf_op jit(solution)/shard_map/all_gather | solution.py:127
  170.7 249.3 %copy-start.39 = (f32[160]{0:T(256)}, f32[160]{0:T(256)S(1)}, u32[]{:S(2)}) copy-start(f32[160]{0:T(256)S(1)} %broadcast_multiply_fusion.4) | copy-start | bytes 1924
  171.9 248.1 %copy-start.43 = (f32[160]{0:T(256)}, f32[160]{0:T(256)S(1)}, u32[]{:S(2)}) copy-start(f32[160]{0:T(256)S(1)} %add_rsqrt_fusion) | copy-start | bytes 1924
  173.8 244.2 %reduce-scatter.15.cloned.1.call-start = ((), (), s32[]{:S(2)}) async-start(), calls=%async_computation.14 | async-start | bytes 2949120 | tf_op jit(solution)/shard_map/reduce_scatter | solution.py:147
  341.1 76.9 %copy-start.13 = (bf16[160,1024]{1,0:T(8,128)(2,1)S(1)}, bf16[160,1024]{1,0:T(8,128)(2,1)}, u32[]{:S(2)}) copy-start(bf16[160,1024]{1,0:T(8,128)(2,1)} %reduce-scatter.11.cloned.1.call-done) | copy-start | bytes 983044
  341.1 78.9 %copy-start.18 = (bf16[160,1024]{1,0:T(8,128)(2,1)S(1)}, bf16[160,1024]{1,0:T(8,128)(2,1)}, u32[]{:S(2)}) copy-start(bf16[160,1024]{1,0:T(8,128)(2,1)} %param.23) | copy-start | bytes 983044
  341.1 138.7 %all-gather.14.cloned.1.call-start = ((), (), s32[]{:S(2)}) async-start(), calls=%async_computation.15 | async-start | bytes 2949120 | tf_op jit(solution)/shard_map/all_gather | solution.py:157
  422.1 137.1 %reduce-scatter.25.cloned.1.call-start = ((), (), s32[]{:S(2)}) async-start(), calls=%async_computation.20 | async-start | bytes 835584
  428.4 177.4 %reduce-scatter.23.cloned.1.call-start = ((), (), s32[]{:S(2)}) async-start(), calls=%async_computation.19 | async-start | bytes 1671168 | tf_op jit(solution)/shard_map/reduce_scatter | solution.py:233
  435.1 232.2 %reduce-scatter.21.cloned.1.call-start = ((), (), s32[]{:S(2)}) async-start(), calls=%async_computation.18 | async-start | bytes 278528 | tf_op jit(solution)/shard_map/reduce_scatter | solution.py:230
  545.7 183.9 %reduce-scatter.19.cloned.1.call-start = ((), (), s32[]{:S(2)}) async-start(), calls=%async_computation.17 | async-start | bytes 835584 | tf_op jit(solution)/shard_map/reduce_scatter | solution.py:227
  551.5 258.4 %reduce-scatter.17.cloned.1.call-start = ((), (), s32[]{:S(2)}) async-start(), calls=%async_computation.16 | async-start | bytes 2949120 | tf_op jit(solution)/shard_map/reduce_scatter | solution.py:215
  554.6 336.0 %reduce-scatter.13.cloned.1.call-start = ((), (), s32[]{:S(2)}) async-start(), calls=%async_computation.12 | async-start | bytes 2949120 | tf_op jit(solution)/shard_map/reduce_scatter | solution.py:131
  559.1 250.8 %copy-start.6 = (bf16[160,1024]{1,0:T(8,128)(2,1)S(1)}, bf16[160,1024]{1,0:T(8,128)(2,1)}, u32[]{:S(2)}) copy-start(bf16[160,1024]{1,0:T(8,128)(2,1)} %param.16) | copy-start | bytes 983044
  559.1 250.8 %copy-start.38 = (f32[1024]{0:T(1024)S(1)}, f32[1024]{0:T(1024)}, u32[]{:S(2)}) copy-start(f32[1024]{0:T(1024)} %param.17) | copy-start | bytes 12292
  559.1 250.8 %copy-start.42 = (f32[160]{0:T(256)S(1)}, f32[160]{0:T(256)}, u32[]{:S(2)}) copy-start(f32[160]{0:T(256)} %copy-done.41) | copy-start | bytes 1924
  559.1 250.8 %copy-start.46 = (f32[160]{0:T(256)S(1)}, f32[160]{0:T(256)}, u32[]{:S(2)}) copy-start(f32[160]{0:T(256)} %copy-done.45) | copy-start | bytes 1924
  559.1 252.2 %copy-start.47 = (f32[1024]{0:T(1024)S(1)}, f32[1024]{0:T(1024)}, u32[]{:S(2)}) copy-start(f32[1024]{0:T(1024)} %get-tuple-element.276) | copy-start | bytes 12292
  559.1 331.5 %copy-start.14 = (bf16[160,1024]{1,0:T(8,128)(2,1)S(1)}, bf16[160,1024]{1,0:T(8,128)(2,1)}, u32[]{:S(2)}) copy-start(bf16[160,1024]{1,0:T(8,128)(2,1)} %reduce-scatter.11.cloned.1.call-done) | copy-start | bytes 983044
  559.1 331.5 %copy-start.19 = (bf16[160,1024]{1,0:T(8,128)(2,1)S(1)}, bf16[160,1024]{1,0:T(8,128)(2,1)}, u32[]{:S(2)}) copy-start(bf16[160,1024]{1,0:T(8,128)(2,1)} %param.23) | copy-start | bytes 983044
  559.1 331.4 %copy-start.20 = (bf16[160,1024]{1,0:T(8,128)(2,1)S(1)}, bf16[160,1024]{1,0:T(8,128)(2,1)}, u32[]{:S(2)}) copy-start(bf16[160,1024]{1,0:T(8,128)(2,1)} %reduce-scatter.15.cloned.1.call-done) | copy-start | bytes 983044
  559.1 331.4 %copy-start.35 = (f32[1024]{0:T(1024)S(1)}, f32[1024]{0:T(1024)}, u32[]{:S(2)}) copy-start(f32[1024]{0:T(1024)} %param.20) | copy-start | bytes 12292
  559.1 331.4 %copy-start.40 = (f32[160]{0:T(256)S(1)}, f32[160]{0:T(256)}, u32[]{:S(2)}) copy-start(f32[160]{0:T(256)} %copy-done.39) | copy-start | bytes 1924
  559.1 331.4 %copy-start.44 = (f32[160]{0:T(256)S(1)}, f32[160]{0:T(256)}, u32[]{:S(2)}) copy-start(f32[160]{0:T(256)} %copy-done.43) | copy-start | bytes 1924
  559.1 331.4 %copy-start.49 = (f32[160]{0:T(256)S(1)}, f32[160]{0:T(256)}, u32[]{:S(2)}) copy-start(f32[160]{0:T(256)} %copy-done.48) | copy-start | bytes 1924
  559.2 331.4 %copy-start.51 = (f32[160]{0:T(256)S(1)}, f32[160]{0:T(256)}, u32[]{:S(2)}) copy-start(f32[160]{0:T(256)} %copy-done.50) | copy-start | bytes 1924
  (61 other events, 304.0 us)
Sparse Core Ops, SparseCore 0:
  12.2 62.5 all-gather.5
  93.9 75.5 reduce-scatter.10
  171.8 58.7 all-gather.11
  232.7 31.7 all-gather.9
  267.2 58.9 all-gather.7
  341.3 76.6 reduce-scatter.14
  422.2 57.5 all-gather.13
  482.2 59.7 reduce-scatter.24
  544.5 61.2 reduce-scatter.22
  608.6 58.6 reduce-scatter.20
  669.8 59.7 reduce-scatter.18
  733.3 76.5 reduce-scatter.16
  813.7 76.7 reduce-scatter.12
where the time goes:
time: 901 us; the launch traced here: 900 us
  waiting for transfers between devices  600 us (67%)
  blocking collectives  129 us (14%)
  matrix products  81 us (9%)
  local copies, waits for them, and re-layouts  36.7 us (4%)
  other arithmetic  36.1 us (4%)
  between operations  14.5 us (2%)
    reduce_scatter x1, waiting for transfers between devices, on_device(): lax.psum_scatter(jnp.einsum('tcj,dcj->td', row_block, full_qkv, preferred...  78.8 us
    reduce_scatter x1, waiting for transfers between devices, on_device(): lax.psum_scatter(jnp.einsum('tcf,dcf->td', row_block, full_in, preferred_...  76.8 us
    reduce_scatter x1, waiting for transfers between devices, on_device(): lax.psum_scatter(jnp.einsum('tj,ej->te', row_block, full_out, preferred_e...  74.1 us
    psum x1, blocking collectives, on_device(): lax.psum((gain_attn_part, gain_mlp_part), ('fsdp', 'tp'))  66.8 us
    all_gather x1, waiting for transfers between devices, on_device(): rows_mlp = lax.all_gather(normed_mlp, 'tp', axis=0, tiled=True)  61.8 us
    reduce_scatter x1, waiting for transfers between devices, on_device(): lax.psum_scatter(grad_qkv_w.astype(jnp.bfloat16), 'fsdp', scatter_dimensi...  61 us
    reduce_scatter x1, waiting for transfers between devices, on_device(): lax.psum_scatter(grad_out.astype(jnp.bfloat16), 'fsdp', scatter_dimension...  59.8 us
    reduce_scatter x1, waiting for transfers between devices, on_device(): lax.psum_scatter(grad_in.astype(jnp.bfloat16), 'fsdp', scatter_dimension=...  44.8 us
  transfers between devices with their start and end apart: 13, of which 12 were waited for; matrix products, arithmetic and copies ran while one was open for 12% of the time, Pallas kernels for 0%

commit v1 on v0

v1 whole, which is shorter than its diff:
```python
import functools

import jax
import jax.numpy as jnp
from jax import lax
from jax.experimental import pallas as pl
from jax.experimental.pallas import tpu as pltpu
from jax.sharding import Mesh
from jax.sharding import PartitionSpec as P

HD = 64
LEN = 1280
EPSILON = 1e-05
THETA = 160000.0
ROWS = 160
WIDTH = 1024
FFB = 328
PAD = 384
QB = 256
VMEM = 60 * 1024 * 1024

AXES = ("x", "zl", "c", "yh", "yl", "zh")
FS = ("x", "zl", "c")
TP = ("yh", "yl", "zh")
MLP_AX = ("yh", "yl")
PRE_AX = ("zh",)
M = 4
PRE = 2
F32 = jnp.float32
BF16 = jnp.bfloat16


def exchange(value, axes, count, mask):
    return lax.ppermute(value, axes, [(i, i ^ mask) for i in range(count)])


def gather_by_mask(value, axes, count):
    return [value] + [exchange(value, axes, count, m) for m in range(1, count)]


def scatter_by_mask(parts, axes, count):
    return [parts[0]] + [exchange(parts[m], axes, count, m) for m in range(1, count)]


def total(parts):
    result = parts[0].astype(F32)
    for part in parts[1:]:
        result = result + part.astype(F32)
    return result


def normalize(values):
    centre = values - jnp.mean(values, axis=-1, keepdims=True)
    scaling = lax.rsqrt(jnp.mean(centre * centre, axis=-1, keepdims=True) + EPSILON)
    return (centre * scaling, scaling)


def norm_back(grad_normed, normed_hat, scaling, gain):
    grad_hat = grad_normed * gain
    mean_grad = jnp.mean(grad_hat, axis=-1, keepdims=True)
    mean_proj = jnp.mean(grad_hat * normed_hat, axis=-1, keepdims=True)
    return (
        scaling * (grad_hat - mean_grad - normed_hat * mean_proj),
        jnp.sum(grad_normed * normed_hat, axis=0),
    )


def rope_tables():
    me = lax.axis_index(TP)
    block = jnp.bitwise_xor(jnp.arange(8, dtype=jnp.int32), me)
    places = (block[:, None] * ROWS + jnp.arange(ROWS, dtype=jnp.int32)[None, :]).reshape(LEN)
    half = HD // 2
    freqs = THETA ** (-jnp.arange(half, dtype=F32) * 2.0 / HD)
    angles = places.astype(F32)[:, None] * freqs[None, :]
    cosine, sine = jnp.cos(angles), jnp.sin(angles)
    return (
        jnp.concatenate([cosine] * 4, axis=1),
        jnp.concatenate([-sine, sine, -sine, sine], axis=1),
    )


def dot(a, b, ca, cb):
    return lax.dot_general(a, b, (((ca,), (cb,)), ((), ())), preferred_element_type=F32)


def swap_halves(values):
    lane = lax.broadcasted_iota(jnp.int32, values.shape, 1)
    first = (lane // 32) % 2 == 0
    return jnp.where(first, pltpu.roll(values, 96, 1), pltpu.roll(values, 32, 1))


def head_mask(values, head):
    lane = lax.broadcasted_iota(jnp.int32, values.shape, 1)
    return jnp.where((lane // HD) == head, values, jnp.zeros_like(values))


def attend_kernel(*refs):
    row_refs = refs[:8]
    w_ref, cos_ref, sin_ref, q_ref, k_ref, v_ref, mixed_ref, lse_ref, rows, proj = refs[8:]
    for r in range(8):
        rows[r * ROWS : (r + 1) * ROWS, :] = row_refs[r][...]
    for c in range(3):
        proj[...] = dot(rows[...], w_ref[c], 1, 0)
        if c == 2:
            v_ref[...] = proj[...].astype(BF16)
        else:
            value = proj[...]
            value = value * cos_ref[...] + swap_halves(value) * sin_ref[...]
            if c == 0:
                q_ref[...] = value.astype(BF16) * jnp.asarray(0.125, BF16)
            else:
                k_ref[...] = value.astype(BF16)

    def block(i, carry):
        at = pl.ds(pl.multiple_of(i * QB, QB), QB)
        query = q_ref[at, :]
        outs = []
        sums = []
        for head in range(2):
            scores = dot(head_mask(query, head), k_ref[...], 1, 1)
            peak = jnp.max(scores, axis=1, keepdims=True)
            exponent = jnp.exp(scores - peak)
            row_sum = jnp.sum(exponent, axis=1, keepdims=True)
            out = dot(exponent.astype(BF16), v_ref[...], 1, 0)
            outs.append(out / row_sum)
            sums.append(jnp.broadcast_to(peak + jnp.log(row_sum), (QB, 2 * HD)))
        lane = lax.broadcasted_iota(jnp.int32, (QB, 2 * HD), 1)
        mixed_ref[at, :] = jnp.where(lane < HD, outs[0], outs[1]).astype(BF16)
        lse_ref[at, :] = jnp.where(lane < HD, sums[0], sums[1])
        return carry

    lax.fori_loop(0, LEN // QB, block, 0)


def attend(row_blocks, w_qkv, cosine, sine):
    wide = jax.ShapeDtypeStruct((LEN, 2 * HD), BF16)
    return pl.pallas_call(
        attend_kernel,
        out_shape=[wide, wide, wide, wide, jax.ShapeDtypeStruct((LEN, 2 * HD), F32)],
        scratch_shapes=[pltpu.VMEM((LEN, WIDTH), BF16), pltpu.VMEM((LEN, 2 * HD), F32)],
        compiler_params=pltpu.CompilerParams(vmem_limit_bytes=VMEM),
        cost_estimate=pl.CostEstimate(
            flops=6_000_000_000, bytes_accessed=8_000_000, transcendentals=3_300_000
        ),
        name="attend",
    )(*row_blocks, w_qkv, cosine, sine)


def attend_back_kernel(
    q_ref, k_ref, v_ref, lse_ref, g_ref, cos_ref, sin_ref, out_ref, key_sum, val_sum
):
    key_sum[...] = jnp.zeros_like(key_sum)
    val_sum[...] = jnp.zeros_like(val_sum)

    def block(i, carry):
        at = pl.ds(pl.multiple_of(i * QB, QB), QB)
        query = q_ref[at, :]
        grad = g_ref[at, :]
        grad_query = jnp.zeros((QB, 2 * HD), F32)
        for head in range(2):
            query_h = head_mask(query, head)
            grad_h = head_mask(grad, head)
            scores = dot(query_h, k_ref[...], 1, 1)
            probs = jnp.exp(scores - lse_ref[at, head * HD : head * HD + 1])
            grad_probs = dot(grad_h, v_ref[...], 1, 1)
            inner = jnp.sum(grad_probs * probs, axis=1, keepdims=True)
            grad_scores = (probs * (grad_probs - inner)).astype(BF16)
            grad_query = grad_query + dot(grad_scores, head_mask(k_ref[...], head), 1, 0)
            key_sum[...] += dot(query_h, grad_scores, 0, 0)
            val_sum[...] += dot(grad_h, probs.astype(BF16), 0, 0)
        grad_query = grad_query * 0.125
        cosine, sine = cos_ref[at, :], sin_ref[at, :]
        out_ref[0, at, :] = (grad_query * cosine - swap_halves(grad_query) * sine).astype(BF16)
        return carry

    lax.fori_loop(0, LEN // QB, block, 0)
    grad_key = key_sum[...].T
    out_ref[1] = (grad_key * cos_ref[...] - swap_halves(grad_key) * sin_ref[...]).astype(BF16)
    out_ref[2] = val_sum[...].T.astype(BF16)


def attend_back(q, k, v, lse, grad_mixed, cosine, sine):
    return pl.pallas_call(
        attend_back_kernel,
        out_shape=jax.ShapeDtypeStruct((3, LEN, 2 * HD), BF16),
        scratch_shapes=[pltpu.VMEM((2 * HD, LEN), F32), pltpu.VMEM((2 * HD, LEN), F32)],
        compiler_params=pltpu.CompilerParams(vmem_limit_bytes=VMEM),
        cost_estimate=pl.CostEstimate(
            flops=12_000_000_000, bytes_accessed=8_000_000, transcendentals=3_300_000
        ),
        name="attend_back",
    )(q, k, v, lse, grad_mixed, cosine, sine)


def mlp_kernel(*refs):
    row_refs, back_refs = refs[:M], refs[M : 2 * M]
    w_ref, act_ref, gh_ref, dn_ref, rows, back, dn = refs[2 * M :]
    step = pl.program_id(0)

    @pl.when(step == 0)
    def _():
        for r in range(M):
            rows[r * ROWS : (r + 1) * ROWS, :] = row_refs[r][...]
            back[r * ROWS : (r + 1) * ROWS, :] = back_refs[r][...]
        dn[...] = jnp.zeros_like(dn)

    w_act = w_ref[:, 0].reshape(WIDTH, PAD)
    w_gate = w_ref[:, 1].reshape(WIDTH, PAD)
    w_down = w_ref[:, 2].reshape(WIDTH, PAD)
    a_in = dot(rows[...], w_act, 1, 0)
    gate = dot(rows[...], w_gate, 1, 0)
    grad_act = dot(back[...], w_down, 1, 0)
    cdf = 0.5 * (1.0 + lax.erf(a_in * (0.5**0.5)))
    gelu = a_in * cdf
    slope = cdf + a_in * (jnp.exp(-0.5 * a_in * a_in) * 0.3989422804014327)
    act_ref[0] = (gelu * gate).astype(BF16)
    g_act = (grad_act * gate * slope).astype(BF16)
    g_gate = (grad_act * gelu).astype(BF16)
    gh_ref[0, 0] = g_act
    gh_ref[0, 1] = g_gate
    dn[...] += dot(g_act, w_act, 1, 1) + dot(g_gate, w_gate, 1, 1)

    @pl.when(step == PRE - 1)
    def _():
        for r in range(M):
            dn_ref[r] = dn[r * ROWS : (r + 1) * ROWS, :].astype(BF16)


def mlp(row_blocks, back_blocks, weights):
    group = M * ROWS
    whole = pl.BlockSpec((ROWS, WIDTH), lambda p: (0, 0))
    return pl.pallas_call(
        mlp_kernel,
        grid=(PRE,),
        in_specs=[whole] * (2 * M) + [pl.BlockSpec((16, 3, 64, PAD), lambda p: (0, p, 0, 0))],
        out_specs=[
            pl.BlockSpec((1, group, PAD), lambda p: (p, 0, 0)),
            pl.BlockSpec((1, 2, group, PAD), lambda p: (p, 0, 0, 0)),
            pl.BlockSpec((M, ROWS, WIDTH), lambda p: (0, 0, 0)),
        ],
        out_shape=[
            jax.ShapeDtypeStruct((PRE, group, PAD), BF16),
            jax.ShapeDtypeStruct((PRE, 2, group, PAD), BF16),
            jax.ShapeDtypeStruct((M, ROWS, WIDTH), BF16),
        ],
        scratch_shapes=[
            pltpu.VMEM((group, WIDTH), BF16),
            pltpu.VMEM((group, WIDTH), BF16),
            pltpu.VMEM((group, WIDTH), F32),
        ],
        compiler_params=pltpu.CompilerParams(vmem_limit_bytes=VMEM),
        cost_estimate=pl.CostEstimate(
            flops=10_000_000_000, bytes_accessed=10_000_000, transcendentals=1_000_000
        ),
        name="mlp",
    )(*row_blocks, *back_blocks, weights)


def mlp_grads_kernel(*refs):
    row_refs, back_refs = refs[:M], refs[M : 2 * M]
    w_ref, act_ref, gh_ref, grad_ref, sum_ref, rows, back, sums = refs[2 * M :]
    step = pl.program_id(0)

    @pl.when(step == 0)
    def _():
        for r in range(M):
            rows[:, r * ROWS : (r + 1) * ROWS] = row_refs[r][...].T
            back[:, r * ROWS : (r + 1) * ROWS] = back_refs[r][...].T
        sums[...] = jnp.zeros_like(sums)

    grad_ref[:, 0] = dot(rows[...], gh_ref[0, 0], 1, 0).astype(BF16).reshape(16, 64, PAD)
    grad_ref[:, 1] = dot(rows[...], gh_ref[0, 1], 1, 0).astype(BF16).reshape(16, 64, PAD)
    grad_ref[:, 2] = dot(back[...], act_ref[0], 1, 0).astype(BF16).reshape(16, 64, PAD)
    sums[...] += dot(act_ref[0], w_ref[:, 0].reshape(WIDTH, PAD), 1, 1)

    @pl.when(step == PRE - 1)
    def _():
        for r in range(M):
            sum_ref[r] = sums[r * ROWS : (r + 1) * ROWS, :].astype(BF16)


def mlp_grads(row_blocks, back_blocks, weights, act, grad_hidden):
    group = M * ROWS
    whole = pl.BlockSpec((ROWS, WIDTH), lambda p: (0, 0))
    return pl.pallas_call(
        mlp_grads_kernel,
        grid=(PRE,),
        in_specs=[whole] * (2 * M)
        + [
            pl.BlockSpec((16, 1, 64, PAD), lambda p: (0, 3 * p + 2, 0, 0)),
            pl.BlockSpec((1, group, PAD), lambda p: (p, 0, 0)),
            pl.BlockSpec((1, 2, group, PAD), lambda p: (p, 0, 0, 0)),
        ],
        out_specs=[
            pl.BlockSpec((16, 3, 64, PAD), lambda p: (0, p, 0, 0)),
            pl.BlockSpec((M, ROWS, WIDTH), lambda p: (0, 0, 0)),
        ],
        out_shape=[
            jax.ShapeDtypeStruct((16, 3 * PRE, 64, PAD), BF16),
            jax.ShapeDtypeStruct((M, ROWS, WIDTH), BF16),
        ],
        scratch_shapes=[
            pltpu.VMEM((WIDTH, group), BF16),
            pltpu.VMEM((WIDTH, group), BF16),
            pltpu.VMEM((group, WIDTH), F32),
        ],
        compiler_params=pltpu.CompilerParams(vmem_limit_bytes=VMEM),
        cost_estimate=pl.CostEstimate(
            flops=8_000_000_000, bytes_accessed=12_000_000, transcendentals=0
        ),
        name="mlp_grads",
    )(*row_blocks, *back_blocks, weights, act, grad_hidden)


def halve(value, axis, axes_count_mask):
    bit = lax.axis_index(axis)
    size = value.shape[0] // 2
    keep = lax.dynamic_slice_in_dim(value, bit * size, size, 0)
    send = lax.dynamic_slice_in_dim(value, (1 - bit) * size, size, 0)
    got = lax.ppermute(send, axis, [(0, 1), (1, 0)])
    return keep.astype(F32) + got.astype(F32)


def reduce_over_fsdp(partial):
    width = partial.shape[1]
    array = partial.reshape(4, 2, 2, 64, width).transpose(2, 1, 0, 3, 4)
    array = halve(array, "c", 2)[0]
    array = halve(array.astype(BF16), "zl", 2)[0]
    array = array.astype(BF16)
    me = lax.axis_index("x")
    parts = [
        lax.dynamic_index_in_dim(array, jnp.bitwise_xor(me, m), 0, keepdims=False)
        for m in range(4)
    ]
    return total(scatter_by_mask(parts, ("x",), 4))


def on_device(tokens, gain_attn, w_qkv, w_out, gain_mlp, w_in, w_down, cotangent):
    mlp_shard = jnp.concatenate([w_in, w_down[:, None, :]], axis=1).transpose(1, 0, 2)
    mlp_shard = jnp.pad(mlp_shard, ((0, 0), (0, 0), (0, PAD - FFB)))
    mlp_shards = gather_by_mask(mlp_shard, PRE_AX, PRE)
    out_shards = gather_by_mask(w_out, TP, 8)
    out_wide = jnp.concatenate(out_shards + [jnp.zeros_like(w_out)], axis=1)
    out_wide = out_wide.reshape(64, 3, PAD).transpose(1, 0, 2)
    shards = jnp.concatenate(mlp_shards + [out_wide], axis=0)
    weights = lax.all_gather(shards, FS, axis=0, tiled=False)
    full_qkv = lax.all_gather(w_qkv.transpose(1, 0, 2), FS, axis=1, tiled=True)
    cosine, sine = rope_tables()

    resid = tokens.astype(F32)
    hat_attn, scale_attn = normalize(resid)
    normed_attn = (hat_attn * gain_attn).astype(BF16)
    rows_attn = gather_by_mask(normed_attn, TP, 8)
    q, k, v, mixed, lse = attend(rows_attn, full_qkv, cosine, sine)
    mixed_parts = scatter_by_mask(list(mixed.reshape(8, ROWS, 2 * HD)), TP, 8)
    mixed_own = jnp.concatenate(mixed_parts, axis=1)
    full_out = [weights[:, 3 * PRE + b].reshape(WIDTH, PAD) for b in range(3)]
    full_out = jnp.concatenate(full_out, axis=1)[:, :WIDTH]
    attn_sum = dot(mixed_own, full_out, 1, 1)
    resid_mid = resid + attn_sum
    hat_mlp, scale_mlp = normalize(resid_mid)
    normed_mlp = (hat_mlp * gain_mlp).astype(BF16)

    back_blocks = gather_by_mask(cotangent, MLP_AX, M)
    row_blocks = gather_by_mask(normed_mlp, MLP_AX, M)
    act, grad_hidden, dn_parts = mlp(row_blocks, back_blocks, weights)
    grad_normed_mlp = total(scatter_by_mask(list(dn_parts), MLP_AX, M))
    grads, sum_parts = mlp_grads(row_blocks, back_blocks, weights, act, grad_hidden)
    grads = lax.psum_scatter(grads, FS, scatter_dimension=0, tiled=False)
    mlp_sum = total(scatter_by_mask(list(sum_parts), MLP_AX, M))
    layer_out = (resid_mid + mlp_sum).astype(BF16)

    grad_mid_norm, gain_mlp_part = norm_back(grad_normed_mlp, hat_mlp, scale_mlp, gain_mlp)
    grad_mid = cotangent.astype(F32) + grad_mid_norm
    grad_attn = grad_mid.astype(BF16)
    grad_mixed = dot(grad_attn, full_out, 1, 0).astype(BF16)
    grad_out = dot(grad_attn, mixed_own, 0, 0).astype(BF16)
    gm_parts = [grad_mixed[:, 2 * HD * m : 2 * HD * (m + 1)] for m in range(8)]
    gm_own = jnp.concatenate(scatter_by_mask(gm_parts, TP, 8), axis=0)
    grad_qkv = attend_back(q, k, v, lse, gm_own, cosine, sine)

    dn_attn = sum(dot(grad_qkv[c], full_qkv[c], 1, 1) for c in range(3)).astype(BF16)
    dn_attn_parts = list(dn_attn.reshape(8, ROWS, WIDTH))
    grad_normed_attn = total(scatter_by_mask(dn_attn_parts, TP, 8))
    rows_all = jnp.concatenate(rows_attn, axis=0)
    grad_qkv_w = jnp.concatenate([dot(rows_all, grad_qkv[c], 0, 0) for c in range(3)], axis=1)

    grad_out = reduce_over_fsdp(grad_out).astype(BF16)
    grad_out = total(
        scatter_by_mask([grad_out[:, 2 * HD * m : 2 * HD * (m + 1)] for m in range(8)], TP, 8)
    )
    grad_qkv_w = reduce_over_fsdp(grad_qkv_w.astype(BF16)).reshape(64, 3, 2 * HD)

    grad_parts = [grads[3 * p : 3 * p + 3] for p in range(PRE)]
    grad_mlp = total(scatter_by_mask(grad_parts, PRE_AX, PRE))
    grad_in = grad_mlp[:2, :, :FFB].transpose(1, 0, 2)
    grad_down = grad_mlp[2, :, :FFB]

    grad_first, gain_attn_part = norm_back(grad_normed_attn, hat_attn, scale_attn, gain_attn)
    grad_tokens = (grad_mid + grad_first).astype(BF16)
    gains = jnp.stack([gain_attn_part, gain_mlp_part])
    for axis in AXES:
        if axis == "x":
            gains = gains + lax.ppermute(gains, "x", [(0, 1), (1, 0), (2, 3), (3, 2)])
            gains = gains + lax.ppermute(gains, "x", [(0, 3), (1, 2), (2, 1), (3, 0)])
        else:
            gains = gains + lax.ppermute(gains, axis, [(0, 1), (1, 0)])
    return (
        layer_out,
        grad_tokens,
        gains[0],
        grad_qkv_w,
        grad_out,
        gains[1],
        grad_in,
        grad_down,
    )


def solution(mesh):
    fine = Mesh(mesh.devices.reshape(4, 2, 2, 2, 2, 2), AXES)
    in_specs = (
        P(AXES, None),
        P(),
        P(FS, None, TP),
        P(FS, TP),
        P(),
        P(FS, None, TP),
        P(FS, TP),
        P(AXES, None),
    )
    out_specs = (
        P(AXES, None),
        P(AXES, None),
        P(),
        P(FS, None, TP),
        P(FS, TP),
        P(),
        P(FS, None, TP),
        P(FS, TP),
    )
    return jax.shard_map(
        on_device, mesh=fine, in_specs=in_specs, out_specs=out_specs, check_vma=False
    )
```

time: 901 us -> 404 us (0.45)
  waiting for transfers between devices: 600 us -> 111 us
  starting transfers between devices: 1.02 us -> 122 us
  blocking collectives: 129 us -> 36.9 us
  matrix products: 81 us -> 10.8 us
  Pallas kernels: 0 us -> 50.7 us
  other arithmetic: 36.1 us -> 17.9 us
    reduce_scatter x7 -> x1, waiting for transfers between devices: 408 us -> 0.01 us  [on_device(): grads = lax.psum_scatter(grads, FS, scatter_dimension=0, tiled=False)]
    all_gather x5 -> x1, waiting for transfers between devices: 192 us -> 0.02 us  [on_device(): weights = lax.all_gather(shards, FS, axis=0, tiled=False)]
    ppermute x0 -> x73, starting transfers between devices: none -> 122 us  [the longest x62 109 us: exchange(): return lax.ppermute(value, axes, [(i, i ^ mask) for i in range(count)])]
    ppermute x0 -> x73, waiting for transfers between devices: none -> 111 us  [the longest x62 84.9 us: exchange(): return lax.ppermute(value, axes, [(i, i ^ mask) for i in range(count)])]
    dot_general x40 -> x9, matrix products: 81 us -> 10.8 us  [dot(): lax.dot_general(a, b, (((ca,), (cb,)), ((), ())), preferred_element_type=...]
    psum x1 -> x0, blocking collectives: 66.8 us -> none  [on_device(): lax.psum((gain_attn_part, gain_mlp_part), ('fsdp', 'tp'))]
    pallas_call x0 -> x4, Pallas kernels: none -> 50.7 us  [the longest x1 14 us: attend_back(): pl.pallas_call(attend_back_kernel, out_shape=jax.ShapeDtypeStruct((3, LEN...]
    all_gather x3 -> x1, blocking collectives: 62.5 us -> 36.9 us  [on_device(): full_qkv = lax.all_gather(w_qkv.transpose(1, 0, 2), FS, axis=1, tiled=True)]
  transfers between devices with their start and end apart: 13 -> 75, of which waited for: 12 -> 30; matrix products, arithmetic and copies ran while one was open for 12% -> 12% of each run, Pallas kernels for 0% -> 10%
where the time goes in v1:
time: 404 us; the launch traced here: 396 us
  starting transfers between devices  122 us (30%)
  waiting for transfers between devices  111 us (27%)
  Pallas kernels  50.7 us (13%)
  blocking collectives  36.9 us (9%)
  local copies, waits for them, and re-layouts  32.3 us (8%)
  other arithmetic  17.9 us (4%)
  between operations  15.3 us (4%)
  matrix products  10.8 us (3%)
    ppermute x62, starting transfers between devices, exchange(): return lax.ppermute(value, axes, [(i, i ^ mask) for i in range(count)])  109 us
    ppermute x62, waiting for transfers between devices, exchange(): return lax.ppermute(value, axes, [(i, i ^ mask) for i in range(count)])  84.9 us
    all_gather x1, blocking collectives, on_device(): full_qkv = lax.all_gather(w_qkv.transpose(1, 0, 2), FS, axis=1, tiled=True)  36.9 us
    unnamed x98, local copies, waits for them, and re-layouts  15.9 us
    pallas_call x1, Pallas kernels, attend_back(): pl.pallas_call(attend_back_kernel, out_shape=jax.ShapeDtypeStruct((3, LEN...  14 us
    pallas_call x1, Pallas kernels, mlp_grads(): pl.pallas_call(mlp_grads_kernel, grid=(PRE,), in_specs=[whole] * (2 * M)...  12.7 us
    pallas_call x1, Pallas kernels, attend(): pl.pallas_call(attend_kernel, out_shape=[wide, wide, wide, wide, jax.Shap...  12.4 us
    pallas_call x1, Pallas kernels, mlp(): pl.pallas_call(mlp_kernel, grid=(PRE,), in_specs=[whole] * (2 * M) + [pl....  11.7 us
  transfers between devices with their start and end apart: 75, of which 30 were waited for; matrix products, arithmetic and copies ran while one was open for 12% of the time, Pallas kernels for 10%

profile of v1, /device:TPU:0, one launch (start us, length us, event | category | flops | bytes accessed | tf_op | source)
XLA Modules:
  0.0 396.3 jit_solution(6878780523820707226)
XLA Ops:
  7.2 3.2 collective-permute-start.20
  10.4 3.9 collective-permute-start.19
  17.2 3.1 collective-permute-start.15
  27.2 3.0 collective-permute-start.21
  31.4 3.4 collective-permute-done.21
  44.2 3.5 collective-permute-start.4
  54.4 12.5 %collective-permute-done.6.refs_7_ = bf16[160,1024]{1,0:T(8,128)(2,1)S(1)} collective-permute-done((bf16[160,1024]{1,0:T(8,128)(2,1)}, bf16[160,1024]{1,0:T(8,128)(2,1)S(1)}, u32[]{:S(2)}, u32[]{:S(2)}) %collective-permute-start.6) | collective-permute-done | bytes 327712 | tf_op jit(solution)/shard_map/ppermute | solution.py:34
  70.6 36.9 %all_gather.9.refs_8_ = bf16[3,1024,128]{2,1,0:T(8,128)(2,1)} all-gather(bf16[3,64,128]{2,1,0:T(8,128)(2,1)S(1)} %bitcast.155), channel_id=1, replica_groups=mesh['x'=4,'zl'=2,'c'=2,'yh'=2,'yl'=2,'zh'=2] {'x','zl','c'}, dimensions={1}, use_global_device_ids=true | all-gather | bytes 835584 | tf_op jit(solution)/shard_map/all_gather | solution.py:347
  112.9 12.4 %attend.1 = (bf16[1280,128]{1,0:T(8,128)(2,1)}, bf16[1280,128]{1,0:T(8,128)(2,1)}, bf16[1280,128]{1,0:T(8,128)(2,1)}, bf16[1280,128]{1,0:T(8,128)(2,1)}, f32[1280,128]{1,0:T(8,128)}) custom-call(bf16[160,1024]{1,0:T(8,128)(2,1)} %get-tuple-element.75.refs_0_, bf16[160,1024]{1,0:T(8,128)(2,1)} %copy-done.24, bf16[160,1024]{1,0:T(8,128)(2,1)} %copy-done.23, ...), custom_call_target="tpu_custom_call" | custom-call | flops 6000000000 | bytes 8000000 | tf_op jit(solution)/shard_map/attend/pallas_call | solution.py:137
  126.3 3.0 collective-permute-start.13
  134.9 3.9 collective-permute-done.8
  139.9 5.3 %collective-permute-done.9 = bf16[160,128]{1,0:T(8,128)(2,1)S(1)} collective-permute-done((bf16[160,128]{1,0:T(8,128)(2,1)S(1)}, bf16[160,128]{1,0:T(8,128)(2,1)S(1)}, u32[]{:S(2)}, u32[]{:S(2)}) %collective-permute-start.9) | collective-permute-done | bytes 40992 | tf_op jit(solution)/shard_map/ppermute | solution.py:34
  146.1 4.6 %collective-permute-done.10 = bf16[160,128]{1,0:T(8,128)(2,1)S(1)} collective-permute-done((bf16[160,128]{1,0:T(8,128)(2,1)S(1)}, bf16[160,128]{1,0:T(8,128)(2,1)S(1)}, u32[]{:S(2)}, u32[]{:S(2)}) %collective-permute-start.10) | collective-permute-done | bytes 40992 | tf_op jit(solution)/shard_map/ppermute | solution.py:34
  152.9 5.8 %collective-permute-done.11 = bf16[160,128]{1,0:T(8,128)(2,1)S(1)} collective-permute-done((bf16[160,128]{1,0:T(8,128)(2,1)S(1)}, bf16[160,128]{1,0:T(8,128)(2,1)S(1)}, u32[]{:S(2)}, u32[]{:S(2)}) %collective-permute-start.11) | collective-permute-done | bytes 40992 | tf_op jit(solution)/shard_map/ppermute | solution.py:34
  160.1 3.8 collective-permute-done.12
  175.9 3.5 collective-permute-done.24.refs_3_
  180.4 11.7 %mlp.1 = (bf16[2,640,384]{2,1,0:T(8,128)(2,1)}, bf16[2,2,640,384]{3,2,1,0:T(8,128)(2,1)}, bf16[4,160,1024]{2,1,0:T(8,128)(2,1)}) custom-call(bf16[160,1024]{1,0:T(8,128)(2,1)} %copy-done.25, bf16[160,1024]{1,0:T(8,128)(2,1)} %collective-permute-done.22.refs_1_, bf16[160,1024]{1,0:T(8,128)(2,1)} %copy-done.34, bf16[160,1024]{1,0:T(8,128)(2,1)} %copy-done.33, ...), custom_call_target="tpu_custom_call" | custom-call | flops 10000000000 | bytes 10000000 | tf_op jit(solution)/shard_map/mlp/pallas_call | solution.py:232
  198.6 12.7 %mlp_grads.1 = (bf16[16,6,64,384]{3,2,1,0:T(8,128)(2,1)}, bf16[4,160,1024]{2,1,0:T(8,128)(2,1)}) custom-call(bf16[160,1024]{1,0:T(8,128)(2,1)} %copy-done.25, bf16[160,1024]{1,0:T(8,128)(2,1)} %collective-permute-done.22.refs_1_, bf16[160,1024]{1,0:T(8,128)(2,1)} %copy-done.34, bf16[160,1024]{1,0:T(8,128)(2,1)} %copy-done.33, bf16[160,1024]{1,0:T(8,128)(2,1)} %refs_4_.3, ...), custom_call_target="tpu_custom_call" | custom-call | flops 8000000000 | bytes 12000000 | tf_op jit(solution)/shard_map/mlp_grads/pallas_call | solution.py:285
  219.8 4.8 %collective-permute-done.30 = bf16[160,1024]{1,0:T(8,128)(2,1)S(1)} collective-permute-done((bf16[160,1024]{1,0:T(8,128)(2,1)S(1)}, bf16[160,1024]{1,0:T(8,128)(2,1)S(1)}, u32[]{:S(2)}, u32[]{:S(2)}) %collective-permute-start.30) | collective-permute-done | bytes 327712 | tf_op jit(solution)/shard_map/ppermute | solution.py:34
  239.6 3.7 collective-permute-done.35
  245.2 4.7 %collective-permute-done.36 = bf16[160,128]{1,0:T(8,128)(2,1)S(1)} collective-permute-done((bf16[160,128]{1,0:T(8,128)(2,1)S(1)}, bf16[160,128]{1,0:T(8,128)(2,1)S(1)}, u32[]{:S(2)}, u32[]{:S(2)}) %collective-permute-start.36) | collective-permute-done | bytes 40992 | tf_op jit(solution)/shard_map/ppermute | solution.py:34
  250.7 14.0 %attend_back.1 = bf16[3,1280,128]{2,1,0:T(8,128)(2,1)} custom-call(bf16[1280,128]{1,0:T(8,128)(2,1)} %get-tuple-element.23.q_ref, bf16[1280,128]{1,0:T(8,128)(2,1)} %get-tuple-element.24.k_ref, bf16[1280,128]{1,0:T(8,128)(2,1)} %get-tuple-element.25.v_ref, f32[1280,128]{1,0:T(8,128)} %get-tuple-element.26.lse_ref, bf16[1280,128]{1,0:T(8,128)(2,1)} %copy-done.29, ...), custom_call_target="tpu_custom_call" | custom-call | flops 12000000000 | bytes 8000000 | tf_op jit(solution)/shard_map/attend_back/pallas_call | solution.py:183
  276.1 4.4 %copy.48 = bf16[1024,1280]{1,0:T(8,128)(2,1)} copy(bf16[1024,1280]{0,1:T(8,128)(2,1)} %bitcast.25) | data formatting | bytes 5242880 | tf_op jit(solution)/shard_map/dot_general | solution.py:83
  285.8 3.3 collective-permute-start.44
  289.1 10.8 %collective-permute-done.41 = bf16[160,1024]{1,0:T(8,128)(2,1)} collective-permute-done((bf16[160,1024]{1,0:T(8,128)(2,1)}, bf16[160,1024]{1,0:T(8,128)(2,1)}, u32[]{:S(2)}, u32[]{:S(2)}) %collective-permute-start.41) | collective-permute-done | bytes 327712 | tf_op jit(solution)/shard_map/ppermute | solution.py:34
  305.5 4.0 %collective-permute-done.43 = bf16[160,1024]{1,0:T(8,128)(2,1)S(1)} collective-permute-done((bf16[160,1024]{1,0:T(8,128)(2,1)S(1)}, bf16[160,1024]{1,0:T(8,128)(2,1)S(1)}, u32[]{:S(2)}, u32[]{:S(2)}) %collective-permute-start.43) | collective-permute-done | bytes 327712 | tf_op jit(solution)/shard_map/ppermute | solution.py:34
  321.5 3.3 collective-permute-start.50
  328.7 4.1 %collective-permute-done.52 = f32[2,1024]{1,0:T(2,128)S(1)} collective-permute-done((f32[2,1024]{1,0:T(2,128)S(1)}, f32[2,1024]{1,0:T(2,128)S(1)}, u32[]{:S(2)}, u32[]{:S(2)}) %collective-permute-start.52) | collective-permute-done | bytes 8224 | tf_op jit(solution)/shard_map/ppermute | solution.py:407
  333.0 3.4 collective-permute-done.53
  345.0 10.1 %collective-permute-done.61 = bf16[1,4,64,1024]{3,2,1,0:T(8,128)(2,1)S(1)} collective-permute-done((bf16[1,4,64,1024]{3,2,1,0:T(8,128)(2,1)S(1)}, bf16[1,4,64,1024]{3,2,1,0:T(8,128)(2,1)S(1)}, u32[]{:S(2)}, u32[]{:S(2)}) %collective-permute-start.61) | collective-permute-done | bytes 524320 | tf_op jit(solution)/shard_map/ppermute | solution.py:320
  373.0 3.0 collective-permute-start.68
  382.8 3.8 collective-permute-done.72
  (300 shorter events, 167.6 us)
Async XLA Ops:
  7.2 156.7 %all-gather.3.cloned.1.call-start = ((), (), s32[]{:S(2)}) async-start(), calls=%async_computation.2 | async-start | bytes 7520256 | tf_op jit(solution)/shard_map/all_gather | solution.py:346
  7.2 24.2 %collective-permute-start.20 = (bf16[64,128]{1,0:T(8,128)(2,1)}, bf16[64,128]{1,0:T(8,128)(2,1)S(1)}, u32[]{:S(2)}, u32[]{:S(2)}) collective-permute-start(bf16[64,128]{1,0:T(8,128)(2,1)} %param.11), channel_id=1, source_target_pairs={{0,6},{1,7},{2,4},{3,5},{4,2},{5,3},{6,0},{7,1},{8,14},{9,15},{10,... | collective-permute-start | bytes 49160 | tf_op jit(solution)/shard_map/ppermute | solution.py:34
  10.4 21.0 %collective-permute-start.19 = (bf16[64,128]{1,0:T(8,128)(2,1)}, bf16[64,128]{1,0:T(8,128)(2,1)S(1)}, u32[]{:S(2)}, u32[]{:S(2)}) collective-permute-start(bf16[64,128]{1,0:T(8,128)(2,1)} %param.11), channel_id=1, source_target_pairs={{0,5},{1,4},{2,7},{3,6},{4,1},{5,0},{6,3},{7,2},{8,13},{9,12},{10,... | collective-permute-start | bytes 49160 | tf_op jit(solution)/shard_map/ppermute | solution.py:34
  14.3 17.0 %collective-permute-start.18 = (bf16[64,128]{1,0:T(8,128)(2,1)}, bf16[64,128]{1,0:T(8,128)(2,1)S(1)}, u32[]{:S(2)}, u32[]{:S(2)}) collective-permute-start(bf16[64,128]{1,0:T(8,128)(2,1)} %param.11), channel_id=1, source_target_pairs={{0,4},{1,5},{2,6},{3,7},{4,0},{5,1},{6,2},{7,3},{8,12},{9,13},{10,... | collective-permute-start | bytes 49160 | tf_op jit(solution)/shard_map/ppermute | solution.py:34
  17.2 13.0 %collective-permute-start.17 = (bf16[64,128]{1,0:T(8,128)(2,1)}, bf16[64,128]{1,0:T(8,128)(2,1)S(1)}, u32[]{:S(2)}, u32[]{:S(2)}) collective-permute-start(bf16[64,128]{1,0:T(8,128)(2,1)} %param.11), channel_id=1, source_target_pairs={{0,3},{1,2},{2,1},{3,0},{4,7},{5,6},{6,5},{7,4},{8,11},{9,10},{10,... | collective-permute-start | bytes 49160 | tf_op jit(solution)/shard_map/ppermute | solution.py:34
  38.9 340.0 %reduce-scatter.2.cloned.1.call-start = ((), (), s32[]{:S(2)}) async-start(), calls=%async_computation.1 | async-start | bytes 5013504 | tf_op jit(solution)/shard_map/reduce_scatter | solution.py:369
  40.4 26.5 %collective-permute-start.6 = (bf16[160,1024]{1,0:T(8,128)(2,1)}, bf16[160,1024]{1,0:T(8,128)(2,1)S(1)}, u32[]{:S(2)}, u32[]{:S(2)}) collective-permute-start(bf16[160,1024]{1,0:T(8,128)(2,1)} %get-tuple-element.75.refs_0_), channel_id=1, source_target_pairs={{0,7},{1,6},{2,5},{3,4},{4,3},{5,2},{6,1},{7,0},{8,15},{9,14},{10,... | collective-permute-start | bytes 983048 | tf_op jit(solution)/shard_map/ppermute | solution.py:34
  43.0 26.0 %collective-permute-start.5 = (bf16[160,1024]{1,0:T(8,128)(2,1)}, bf16[160,1024]{1,0:T(8,128)(2,1)S(1)}, u32[]{:S(2)}, u32[]{:S(2)}) collective-permute-start(bf16[160,1024]{1,0:T(8,128)(2,1)} %get-tuple-element.75.refs_0_), channel_id=1, source_target_pairs={{0,6},{1,7},{2,4},{3,5},{4,2},{5,3},{6,0},{7,1},{8,14},{9,15},{10,... | collective-permute-start | bytes 983048 | tf_op jit(solution)/shard_map/ppermute | solution.py:34
  44.2 63.3 %collective-permute-start.4 = (bf16[160,1024]{1,0:T(8,128)(2,1)}, bf16[160,1024]{1,0:T(8,128)(2,1)S(1)}, u32[]{:S(2)}, u32[]{:S(2)}) collective-permute-start(bf16[160,1024]{1,0:T(8,128)(2,1)} %get-tuple-element.75.refs_0_), channel_id=1, source_target_pairs={{0,5},{1,4},{2,7},{3,6},{4,1},{5,0},{6,3},{7,2},{8,13},{9,12},{10,... | collective-permute-start | bytes 983048 | tf_op jit(solution)/shard_map/ppermute | solution.py:34
  47.7 61.5 %collective-permute-start.3 = (bf16[160,1024]{1,0:T(8,128)(2,1)}, bf16[160,1024]{1,0:T(8,128)(2,1)}, u32[]{:S(2)}, u32[]{:S(2)}) collective-permute-start(bf16[160,1024]{1,0:T(8,128)(2,1)} %get-tuple-element.75.refs_0_), channel_id=1, source_target_pairs={{0,4},{1,5},{2,6},{3,7},{4,0},{5,1},{6,2},{7,3},{8,12},{9,13},{10,... | collective-permute-start | bytes 983048 | tf_op jit(solution)/shard_map/ppermute | solution.py:34
  49.5 60.1 %collective-permute-start.2 = (bf16[160,1024]{1,0:T(8,128)(2,1)}, bf16[160,1024]{1,0:T(8,128)(2,1)}, u32[]{:S(2)}, u32[]{:S(2)}) collective-permute-start(bf16[160,1024]{1,0:T(8,128)(2,1)} %get-tuple-element.75.refs_0_), channel_id=1, source_target_pairs={{0,3},{1,2},{2,1},{3,0},{4,7},{5,6},{6,5},{7,4},{8,11},{9,10},{10,... | collective-permute-start | bytes 983048 | tf_op jit(solution)/shard_map/ppermute | solution.py:34
  66.8 45.2 %collective-permute-start.1 = (bf16[160,1024]{1,0:T(8,128)(2,1)}, bf16[160,1024]{1,0:T(8,128)(2,1)S(1)}, u32[]{:S(2)}, u32[]{:S(2)}) collective-permute-start(bf16[160,1024]{1,0:T(8,128)(2,1)} %get-tuple-element.75.refs_0_), channel_id=1, source_target_pairs={{0,2},{1,3},{2,0},{3,1},{4,6},{5,7},{6,4},{7,5},{8,10},{9,11},{10,... | collective-permute-start | bytes 983048 | tf_op jit(solution)/shard_map/ppermute | solution.py:34
  69.0 43.1 %collective-permute-start = (bf16[160,1024]{1,0:T(8,128)(2,1)}, bf16[160,1024]{1,0:T(8,128)(2,1)S(1)}, u32[]{:S(2)}, u32[]{:S(2)}) collective-permute-start(bf16[160,1024]{1,0:T(8,128)(2,1)} %get-tuple-element.75.refs_0_), channel_id=1, source_target_pairs={{0,1},{1,0},{2,3},{3,2},{4,5},{5,4},{6,7},{7,6},{8,9},{9,8},{10,11... | collective-permute-start | bytes 983048 | tf_op jit(solution)/shard_map/ppermute | solution.py:34
  107.5 61.5 %collective-permute-start.27 = (bf16[160,1024]{1,0:T(8,128)(2,1)}, bf16[160,1024]{1,0:T(8,128)(2,1)S(1)}, u32[]{:S(2)}, u32[]{:S(2)}) collective-permute-start(bf16[160,1024]{1,0:T(8,128)(2,1)} %refs_4_.3), channel_id=1, source_target_pairs={{0,6},{2,4},{4,2},{6,0},{1,7},{3,5},{5,3},{7,1},{8,14},{10,12},{12... | collective-permute-start | bytes 983048 | tf_op jit(solution)/shard_map/ppermute | solution.py:34
  109.2 66.7 %collective-permute-start.26 = (bf16[160,1024]{1,0:T(8,128)(2,1)}, bf16[160,1024]{1,0:T(8,128)(2,1)S(1)}, u32[]{:S(2)}, u32[]{:S(2)}) collective-permute-start(bf16[160,1024]{1,0:T(8,128)(2,1)} %refs_4_.3), channel_id=1, source_target_pairs={{0,4},{2,6},{4,0},{6,2},{1,5},{3,7},{5,1},{7,3},{8,12},{10,14},{12... | collective-permute-start | bytes 983048 | tf_op jit(solution)/shard_map/ppermute | solution.py:34
  109.6 66.3 %collective-permute-start.25 = (bf16[160,1024]{1,0:T(8,128)(2,1)}, bf16[160,1024]{1,0:T(8,128)(2,1)S(1)}, u32[]{:S(2)}, u32[]{:S(2)}) collective-permute-start(bf16[160,1024]{1,0:T(8,128)(2,1)} %refs_4_.3), channel_id=1, source_target_pairs={{0,2},{2,0},{4,6},{6,4},{1,3},{3,1},{5,7},{7,5},{8,10},{10,8},{12,... | collective-permute-start | bytes 983048 | tf_op jit(solution)/shard_map/ppermute | solution.py:34
  126.3 37.6 %collective-permute-start.13 = (bf16[160,128]{1,0:T(8,128)(2,1)S(1)}, bf16[160,128]{1,0:T(8,128)(2,1)S(1)}, u32[]{:S(2)}, u32[]{:S(2)}) collective-permute-start(bf16[160,128]{1,0:T(8,128)(2,1)S(1)} %get-tuple-element.109), channel_id=1, source_target_pairs={{0,7},{1,6},{2,5},{3,4},{4,3},{5,2},{6,1},{7,0},{8,15},{9,14},{10,... | collective-permute-start | bytes 122888 | tf_op jit(solution)/shard_map/ppermute | solution.py:34
  194.3 19.9 %collective-permute-start.31 = (bf16[160,1024]{1,0:T(8,128)(2,1)}, bf16[160,1024]{1,0:T(8,128)(2,1)}, u32[]{:S(2)}, u32[]{:S(2)}) collective-permute-start(bf16[160,1024]{1,0:T(8,128)(2,1)} %get-tuple-element.90), channel_id=1, source_target_pairs={{0,2},{2,0},{4,6},{6,4},{1,3},{3,1},{5,7},{7,5},{8,10},{10,8},{12,... | collective-permute-start | bytes 983048 | tf_op jit(solution)/shard_map/ppermute | solution.py:34
  194.3 22.5 %collective-permute-start.33 = (bf16[160,1024]{1,0:T(8,128)(2,1)}, bf16[160,1024]{1,0:T(8,128)(2,1)}, u32[]{:S(2)}, u32[]{:S(2)}) collective-permute-start(bf16[160,1024]{1,0:T(8,128)(2,1)} %get-tuple-element.91), channel_id=1, source_target_pairs={{0,6},{2,4},{4,2},{6,0},{1,7},{3,5},{5,3},{7,1},{8,14},{10,12},{12... | collective-permute-start | bytes 983048 | tf_op jit(solution)/shard_map/ppermute | solution.py:34
  195.8 21.0 %collective-permute-start.32 = (bf16[160,1024]{1,0:T(8,128)(2,1)}, bf16[160,1024]{1,0:T(8,128)(2,1)}, u32[]{:S(2)}, u32[]{:S(2)}) collective-permute-start(bf16[160,1024]{1,0:T(8,128)(2,1)} %get-tuple-element.92), channel_id=1, source_target_pairs={{0,4},{2,6},{4,0},{6,2},{1,5},{3,7},{5,1},{7,3},{8,12},{10,14},{12... | collective-permute-start | bytes 983048 | tf_op jit(solution)/shard_map/ppermute | solution.py:34
  230.0 19.9 %collective-permute-start.40 = (bf16[160,128]{1,0:T(8,128)(2,1)S(1)}, bf16[160,128]{1,0:T(8,128)(2,1)S(1)}, u32[]{:S(2)}, u32[]{:S(2)}) collective-permute-start(bf16[160,128]{1,0:T(8,128)(2,1)S(1)} %get-tuple-element.101), channel_id=1, source_target_pairs={{0,7},{1,6},{2,5},{3,4},{4,3},{5,2},{6,1},{7,0},{8,15},{9,14},{10,... | collective-permute-start | bytes 122888 | tf_op jit(solution)/shard_map/ppermute | solution.py:34
  232.8 17.1 %collective-permute-start.39 = (bf16[160,128]{1,0:T(8,128)(2,1)S(1)}, bf16[160,128]{1,0:T(8,128)(2,1)S(1)}, u32[]{:S(2)}, u32[]{:S(2)}) collective-permute-start(bf16[160,128]{1,0:T(8,128)(2,1)S(1)} %get-tuple-element.102), channel_id=1, source_target_pairs={{0,6},{1,7},{2,4},{3,5},{4,2},{5,3},{6,0},{7,1},{8,14},{9,15},{10,... | collective-permute-start | bytes 122888 | tf_op jit(solution)/shard_map/ppermute | solution.py:34
  234.6 15.3 %collective-permute-start.38 = (bf16[160,128]{1,0:T(8,128)(2,1)S(1)}, bf16[160,128]{1,0:T(8,128)(2,1)S(1)}, u32[]{:S(2)}, u32[]{:S(2)}) collective-permute-start(bf16[160,128]{1,0:T(8,128)(2,1)S(1)} %get-tuple-element.103), channel_id=1, source_target_pairs={{0,5},{1,4},{2,7},{3,6},{4,1},{5,0},{6,3},{7,2},{8,13},{9,12},{10,... | collective-permute-start | bytes 122888 | tf_op jit(solution)/shard_map/ppermute | solution.py:34
  270.7 29.2 %collective-permute-start.41 = (bf16[160,1024]{1,0:T(8,128)(2,1)}, bf16[160,1024]{1,0:T(8,128)(2,1)}, u32[]{:S(2)}, u32[]{:S(2)}) collective-permute-start(bf16[160,1024]{1,0:T(8,128)(2,1)} %get-tuple-element.81), channel_id=1, source_target_pairs={{0,1},{1,0},{2,3},{3,2},{4,5},{5,4},{6,7},{7,6},{8,9},{9,8},{10,11... | collective-permute-start | bytes 983048 | tf_op jit(solution)/shard_map/ppermute | solution.py:34
  272.7 28.1 %collective-permute-start.47 = (bf16[160,1024]{1,0:T(8,128)(2,1)}, bf16[160,1024]{1,0:T(8,128)(2,1)}, u32[]{:S(2)}, u32[]{:S(2)}) collective-permute-start(bf16[160,1024]{1,0:T(8,128)(2,1)} %get-tuple-element.82), channel_id=1, source_target_pairs={{0,7},{1,6},{2,5},{3,4},{4,3},{5,2},{6,1},{7,0},{8,15},{9,14},{10,... | collective-permute-start | bytes 983048 | tf_op jit(solution)/shard_map/ppermute | solution.py:34
  282.5 22.8 %collective-permute-start.46 = (bf16[160,1024]{1,0:T(8,128)(2,1)S(1)}, bf16[160,1024]{1,0:T(8,128)(2,1)S(1)}, u32[]{:S(2)}, u32[]{:S(2)}) collective-permute-start(bf16[160,1024]{1,0:T(8,128)(2,1)S(1)} %copy-done.16), channel_id=1, source_target_pairs={{0,6},{1,7},{2,4},{3,5},{4,2},{5,3},{6,0},{7,1},{8,14},{9,15},{10,... | collective-permute-start | bytes 983048 | tf_op jit(solution)/shard_map/ppermute | solution.py:34
  284.2 21.3 %collective-permute-start.45 = (bf16[160,1024]{1,0:T(8,128)(2,1)S(1)}, bf16[160,1024]{1,0:T(8,128)(2,1)S(1)}, u32[]{:S(2)}, u32[]{:S(2)}) collective-permute-start(bf16[160,1024]{1,0:T(8,128)(2,1)S(1)} %copy-done.15), channel_id=1, source_target_pairs={{0,5},{1,4},{2,7},{3,6},{4,1},{5,0},{6,3},{7,2},{8,13},{9,12},{10,... | collective-permute-start | bytes 983048 | tf_op jit(solution)/shard_map/ppermute | solution.py:34
  285.8 19.7 %collective-permute-start.44 = (bf16[160,1024]{1,0:T(8,128)(2,1)S(1)}, bf16[160,1024]{1,0:T(8,128)(2,1)S(1)}, u32[]{:S(2)}, u32[]{:S(2)}) collective-permute-start(bf16[160,1024]{1,0:T(8,128)(2,1)S(1)} %copy-done.14), channel_id=1, source_target_pairs={{0,4},{1,5},{2,6},{3,7},{4,0},{5,1},{6,2},{7,3},{8,12},{9,13},{10,... | collective-permute-start | bytes 983048 | tf_op jit(solution)/shard_map/ppermute | solution.py:34
  305.3 36.3 %collective-permute-start.60 = (bf16[1,2,4,64,1024]{4,3,2,1,0:T(8,128)(2,1)S(1)}, bf16[1,2,4,64,1024]{4,3,2,1,0:T(8,128)(2,1)S(1)}, u32[]{:S(2)}, u32[]{:S(2)}) collective-permute-start(bf16[1,2,4,64,1024]{4,3,2,1,0:T(8,128)(2,1)S(1)} %bitcast.138), channel_id=1, source_target_pairs={{0,8},{8,0},{1,9},{9,1},{2,10},{10,2},{3,11},{11,3},{4,12},{12,4},... | collective-permute-start | bytes 3145736 | tf_op jit(solution)/shard_map/ppermute | solution.py:320
  326.5 18.3 %collective-permute-start.55 = (bf16[1,2,4,64,384]{4,3,0,1,2:T(8,128)(2,1)S(1)}, bf16[1,2,4,64,384]{4,3,0,1,2:T(8,128)(2,1)S(1)}, u32[]{:S(2)}, u32[]{:S(2)}) collective-permute-start(bf16[1,2,4,64,384]{4,3,0,1,2:T(8,128)(2,1)S(1)} %dynamic-slice_bitcast_fusion.1), channel_id=1, source_target_pairs={{0,8},{8,0},{1,9},{9,1},{2,10},{10,2},{3,11},{11,3},{4,12},{12,4},... | collective-permute-start | bytes 1179656 | tf_op jit(solution)/shard_map/ppermute | solution.py:320
  342.1 13.0 %collective-permute-start.61 = (bf16[1,4,64,1024]{3,2,1,0:T(8,128)(2,1)S(1)}, bf16[1,4,64,1024]{3,2,1,0:T(8,128)(2,1)S(1)}, u32[]{:S(2)}, u32[]{:S(2)}) collective-permute-start(bf16[1,4,64,1024]{3,2,1,0:T(8,128)(2,1)S(1)} %dynamic-slice_bitcast_fusion), channel_id=1, source_target_pairs={{0,16},{16,0},{1,17},{17,1},{2,18},{18,2},{3,19},{19,3},{4,20},{20... | collective-permute-start | bytes 1572872 | tf_op jit(solution)/shard_map/ppermute | solution.py:320
  344.9 14.6 %collective-permute-start.56 = (bf16[1,4,64,384]{3,2,1,0:T(8,128)(2,1)S(1)}, bf16[1,4,64,384]{3,2,1,0:T(8,128)(2,1)S(1)}, u32[]{:S(2)}, u32[]{:S(2)}) collective-permute-start(bf16[1,4,64,384]{3,2,1,0:T(8,128)(2,1)S(1)} %dynamic-slice_bitcast_fusion.2), channel_id=1, source_target_pairs={{0,16},{16,0},{1,17},{17,1},{2,18},{18,2},{3,19},{19,3},{4,20},{20... | collective-permute-start | bytes 589832 | tf_op jit(solution)/shard_map/ppermute | solution.py:320
  (78 other events, 657.4 us)
Sparse Core Ops, SparseCore 0:
  39.0 73.6 all-gather.2
  211.4 87.1 reduce-scatter.1

commit v2 on v1

v2 whole, which is shorter than its diff:
```python
import jax
import jax.numpy as jnp
from jax import lax
from jax.experimental import pallas as pl
from jax.experimental.pallas import tpu as pltpu
from jax.sharding import Mesh
from jax.sharding import PartitionSpec as P

HD = 64
LEN = 1280
EPSILON = 1e-05
THETA = 160000.0
ROWS = 160
WIDTH = 1024
FFB = 328
PAD = 384
QB = 256
SENT = 176
VMEM = 60 * 1024 * 1024

AXES = ("x", "zl", "c", "yh", "yl", "zh")
FS = ("x", "zl", "c")
TP = ("yh", "yl", "zh")
MLP_AX = ("yh", "yl")
PRE_AX = ("zh",)
M = 4
PRE = 2
F32 = jnp.float32
BF16 = jnp.bfloat16


def exchange(value, axes, count, mask):
    return lax.ppermute(value, axes, [(i, i ^ mask) for i in range(count)])


def gather_by_mask(value, axes, count):
    return [value] + [exchange(value, axes, count, m) for m in range(1, count)]


def scatter_by_mask(parts, axes, count):
    return [parts[0]] + [exchange(parts[m], axes, count, m) for m in range(1, count)]


def total(parts):
    result = parts[0].astype(F32)
    for part in parts[1:]:
        result = result + part.astype(F32)
    return result


def normalize(values):
    centre = values - jnp.mean(values, axis=-1, keepdims=True)
    scaling = lax.rsqrt(jnp.mean(centre * centre, axis=-1, keepdims=True) + EPSILON)
    return (centre * scaling, scaling)


def norm_back(grad_normed, normed_hat, scaling, gain):
    grad_hat = grad_normed * gain
    mean_grad = jnp.mean(grad_hat, axis=-1, keepdims=True)
    mean_proj = jnp.mean(grad_hat * normed_hat, axis=-1, keepdims=True)
    return (
        scaling * (grad_hat - mean_grad - normed_hat * mean_proj),
        jnp.sum(grad_normed * normed_hat, axis=0),
    )


def rope_tables():
    half = HD // 2
    freqs = THETA ** (-jnp.arange(half, dtype=F32) * 2.0 / HD)
    angles = jnp.arange(LEN, dtype=F32)[:, None] * freqs[None, :]
    cosine, sine = jnp.cos(angles), jnp.sin(angles)
    return (
        jnp.concatenate([cosine] * 4, axis=1),
        jnp.concatenate([-sine, sine, -sine, sine], axis=1),
    )


def dot(a, b, ca, cb):
    return lax.dot_general(a, b, (((ca,), (cb,)), ((), ())), preferred_element_type=F32)


def swap_halves(values):
    lane = lax.broadcasted_iota(jnp.int32, values.shape, 1)
    first = (lane // 32) % 2 == 0
    return jnp.where(first, pltpu.roll(values, 96, 1), pltpu.roll(values, 32, 1))


def head_mask(values, head):
    lane = lax.broadcasted_iota(jnp.int32, values.shape, 1)
    return jnp.where((lane // HD) == head, values, jnp.zeros_like(values))


def attend_kernel(
    rows_ref, w_ref, cos_ref, sin_ref, q_ref, k_ref, v_ref, mixed_ref, lse_ref, proj
):
    proj[...] = dot(rows_ref[...].reshape(LEN, WIDTH), w_ref[...].reshape(WIDTH, PAD), 1, 0)
    cosine, sine = cos_ref[...], sin_ref[...]
    value = proj[:, : 2 * HD]
    value = value * cosine + swap_halves(value) * sine
    q_ref[...] = value.astype(BF16) * jnp.asarray(0.125, BF16)
    value = proj[:, 2 * HD : 4 * HD]
    k_ref[...] = (value * cosine + swap_halves(value) * sine).astype(BF16)
    v_ref[...] = proj[:, 4 * HD :].astype(BF16)

    def block(i, carry):
        at = pl.ds(pl.multiple_of(i * QB, QB), QB)
        query = q_ref[at, :]
        outs = []
        sums = []
        for head in range(2):
            scores = dot(head_mask(query, head), k_ref[...], 1, 1)
            peak = jnp.max(scores, axis=1, keepdims=True)
            exponent = jnp.exp(scores - peak)
            row_sum = jnp.sum(exponent, axis=1, keepdims=True)
            out = dot(exponent.astype(BF16), v_ref[...], 1, 0)
            outs.append(out / row_sum)
            sums.append(jnp.broadcast_to(peak + jnp.log(row_sum), (QB, 2 * HD)))
        lane = lax.broadcasted_iota(jnp.int32, (QB, 2 * HD), 1)
        mixed_ref[at, :] = jnp.where(lane < HD, outs[0], outs[1]).astype(BF16)
        lse_ref[at, :] = jnp.where(lane < HD, sums[0], sums[1])
        return carry

    lax.fori_loop(0, LEN // QB, block, 0)


def whole(*shape):
    return pl.BlockSpec(shape, lambda i: (0,) * len(shape))


ROWS_SPEC = pl.BlockSpec((8, ROWS, WIDTH), lambda i: (0, 0, 0))
QKV_SPEC = pl.BlockSpec((16, 1, 64, PAD), lambda i: (0, 3, 0, 0))


def attend(rows, weights, cosine, sine):
    wide = jax.ShapeDtypeStruct((LEN, 2 * HD), BF16)
    return pl.pallas_call(
        attend_kernel,
        grid=(1,),
        in_specs=[ROWS_SPEC, QKV_SPEC, whole(LEN, 2 * HD), whole(LEN, 2 * HD)],
        out_specs=[whole(LEN, 2 * HD)] * 5,
        out_shape=[wide, wide, wide, wide, jax.ShapeDtypeStruct((LEN, 2 * HD), F32)],
        scratch_shapes=[pltpu.VMEM((LEN, PAD), F32)],
        compiler_params=pltpu.CompilerParams(vmem_limit_bytes=VMEM),
        cost_estimate=pl.CostEstimate(
            flops=6_000_000_000, bytes_accessed=8_000_000, transcendentals=3_300_000
        ),
        name="attend",
    )(rows, weights, cosine, sine)


def attend_back_kernel(me_ref, *refs):
    q_ref, k_ref, v_ref, lse_ref, g_ref, cos_ref, sin_ref, w_ref, out_ref = refs[:9]
    dn_refs = refs[9:17]
    key_sum, val_sum, dn = refs[17:]
    key_sum[...] = jnp.zeros_like(key_sum)
    val_sum[...] = jnp.zeros_like(val_sum)

    def block(i, carry):
        at = pl.ds(pl.multiple_of(i * QB, QB), QB)
        query = q_ref[at, :]
        grad = g_ref[at, :]
        grad_query = jnp.zeros((QB, 2 * HD), F32)
        for head in range(2):
            query_h = head_mask(query, head)
            grad_h = head_mask(grad, head)
            scores = dot(query_h, k_ref[...], 1, 1)
            probs = jnp.exp(scores - lse_ref[at, head * HD : head * HD + 1])
            grad_probs = dot(grad_h, v_ref[...], 1, 1)
            inner = jnp.sum(grad_probs * probs, axis=1, keepdims=True)
            grad_scores = (probs * (grad_probs - inner)).astype(BF16)
            grad_query = grad_query + dot(grad_scores, head_mask(k_ref[...], head), 1, 0)
            key_sum[...] += dot(query_h, grad_scores, 0, 0)
            val_sum[...] += dot(grad_h, probs.astype(BF16), 0, 0)
        grad_query = grad_query * 0.125
        cosine, sine = cos_ref[at, :], sin_ref[at, :]
        grad_query = grad_query * cosine - swap_halves(grad_query) * sine
        out_ref[at, : 2 * HD] = grad_query.astype(BF16)
        return carry

    lax.fori_loop(0, LEN // QB, block, 0)
    grad_key = key_sum[...].T
    grad_key = grad_key * cos_ref[...] - swap_halves(grad_key) * sin_ref[...]
    out_ref[:, 2 * HD : 4 * HD] = grad_key.astype(BF16)
    out_ref[:, 4 * HD :] = val_sum[...].T.astype(BF16)
    dn[...] = dot(out_ref[...], w_ref[...].reshape(WIDTH, PAD), 1, 1).astype(BF16)
    me = me_ref[0]
    for m in range(8):
        at = pl.multiple_of(jnp.bitwise_xor(me, m) * ROWS, ROWS)
        dn_refs[m][...] = dn[pl.ds(at, ROWS), :]


def attend_back(me, q, k, v, lse, grad_mixed, cosine, sine, weights):
    return pl.pallas_call(
        attend_back_kernel,
        grid=(1,),
        in_specs=[pl.BlockSpec(memory_space=pltpu.SMEM)]
        + [whole(LEN, 2 * HD)] * 7
        + [QKV_SPEC],
        out_specs=[whole(LEN, PAD)] + [whole(ROWS, WIDTH)] * 8,
        out_shape=[jax.ShapeDtypeStruct((LEN, PAD), BF16)]
        + [jax.ShapeDtypeStruct((ROWS, WIDTH), BF16)] * 8,
        scratch_shapes=[
            pltpu.VMEM((2 * HD, LEN), F32),
            pltpu.VMEM((2 * HD, LEN), F32),
            pltpu.VMEM((LEN, WIDTH), BF16),
        ],
        compiler_params=pltpu.CompilerParams(vmem_limit_bytes=VMEM),
        cost_estimate=pl.CostEstimate(
            flops=12_000_000_000, bytes_accessed=8_000_000, transcendentals=3_300_000
        ),
        name="attend_back",
    )(me, q, k, v, lse, grad_mixed, cosine, sine, weights)


def qkv_grads_kernel(rows_ref, g_ref, out_ref, turned):
    for r in range(8):
        turned[:, r * ROWS : (r + 1) * ROWS] = rows_ref[r].T
    out_ref[...] = dot(turned[...], g_ref[...], 1, 0).astype(BF16).reshape(16, 64, PAD)


def qkv_grads(rows, grad_qkv):
    return pl.pallas_call(
        qkv_grads_kernel,
        grid=(1,),
        in_specs=[ROWS_SPEC, whole(LEN, PAD)],
        out_specs=whole(16, 64, PAD),
        out_shape=jax.ShapeDtypeStruct((16, 64, PAD), BF16),
        scratch_shapes=[pltpu.VMEM((WIDTH, LEN), BF16)],
        compiler_params=pltpu.CompilerParams(vmem_limit_bytes=VMEM),
        cost_estimate=pl.CostEstimate(
            flops=2_000_000_000, bytes_accessed=5_000_000, transcendentals=0
        ),
        name="qkv_grads",
    )(rows, grad_qkv)


def store_by_owner(ref, at, value):
    value = value.astype(BF16)
    for x in range(4):
        for zl in range(2):
            for c in range(2):
                row = (x * 4 + zl * 2 + c) * 64
                ref[x * 2 + c, zl, at] = value[row : row + 64, :]


def mlp_kernel(*refs):
    row_refs, back_refs = refs[:M], refs[M : 2 * M]
    w0_ref, w1_ref, act_ref, gh_ref = refs[2 * M : 2 * M + 4]
    dn_refs = refs[2 * M + 4 : 3 * M + 4]
    rows, back, dn, weights = refs[3 * M + 4 :]
    step = pl.program_id(0)

    @pl.when(step == 0)
    def _():
        for r in range(M):
            rows[r * ROWS : (r + 1) * ROWS, :] = row_refs[r][...]
            back[r * ROWS : (r + 1) * ROWS, :] = back_refs[r][...]
        dn[...] = jnp.zeros_like(dn)
        weights[...] = w0_ref[...]

    @pl.when(step == 1)
    def _():
        weights[...] = w1_ref[...]

    w_act = weights[:, 0].reshape(WIDTH, PAD)
    w_gate = weights[:, 1].reshape(WIDTH, PAD)
    w_down = weights[:, 2].reshape(WIDTH, PAD)
    a_in = dot(rows[...], w_act, 1, 0)
    gate = dot(rows[...], w_gate, 1, 0)
    grad_act = dot(back[...], w_down, 1, 0)
    cdf = 0.5 * (1.0 + lax.erf(a_in * (0.5**0.5)))
    gelu = a_in * cdf
    slope = cdf + a_in * (jnp.exp(-0.5 * a_in * a_in) * 0.3989422804014327)
    act_ref[0] = (gelu * gate).astype(BF16)
    g_act = (grad_act * gate * slope).astype(BF16)
    g_gate = (grad_act * gelu).astype(BF16)
    gh_ref[0, 0] = g_act
    gh_ref[0, 1] = g_gate
    dn[...] += dot(g_act, w_act, 1, 1) + dot(g_gate, w_gate, 1, 1)

    @pl.when(step == PRE - 1)
    def _():
        for r in range(M):
            dn_refs[r][...] = dn[r * ROWS : (r + 1) * ROWS, :].astype(BF16)


MLP_SPEC = pl.BlockSpec((16, 3, 64, PAD), lambda p: (0, 0, 0, 0))
DOWN_SPEC = pl.BlockSpec((16, 1, 64, PAD), lambda p: (0, 2, 0, 0))
ACT_SPEC = pl.BlockSpec((1, M * ROWS, PAD), lambda p: (p, 0, 0))
HIDDEN_SPEC = pl.BlockSpec((1, 2, M * ROWS, PAD), lambda p: (p, 0, 0, 0))


def mlp(row_blocks, back_blocks, weights, weights_more):
    group = M * ROWS
    return pl.pallas_call(
        mlp_kernel,
        grid=(PRE,),
        in_specs=[whole(ROWS, WIDTH)] * (2 * M) + [MLP_SPEC, MLP_SPEC],
        out_specs=[ACT_SPEC, HIDDEN_SPEC] + [whole(ROWS, WIDTH)] * M,
        out_shape=[
            jax.ShapeDtypeStruct((PRE, group, PAD), BF16),
            jax.ShapeDtypeStruct((PRE, 2, group, PAD), BF16),
        ]
        + [jax.ShapeDtypeStruct((ROWS, WIDTH), BF16)] * M,
        scratch_shapes=[
            pltpu.VMEM((group, WIDTH), BF16),
            pltpu.VMEM((group, WIDTH), BF16),
            pltpu.VMEM((group, WIDTH), F32),
            pltpu.VMEM((16, 3, 64, PAD), BF16),
        ],
        compiler_params=pltpu.CompilerParams(vmem_limit_bytes=VMEM),
        cost_estimate=pl.CostEstimate(
            flops=10_000_000_000, bytes_accessed=10_000_000, transcendentals=1_000_000
        ),
        name="mlp",
    )(*row_blocks, *back_blocks, weights, weights_more)


def mlp_grads_kernel(*refs):
    row_refs, back_refs = refs[:M], refs[M : 2 * M]
    w0_ref, w1_ref, act_ref, gh_ref, grad_ref = refs[2 * M : 2 * M + 5]
    sum_refs = refs[2 * M + 5 : 3 * M + 5]
    rows, back, sums = refs[3 * M + 5 :]
    step = pl.program_id(0)

    @pl.when(step == 0)
    def _():
        for r in range(M):
            rows[:, r * ROWS : (r + 1) * ROWS] = row_refs[r][...].T
            back[:, r * ROWS : (r + 1) * ROWS] = back_refs[r][...].T
        sums[...] = dot(act_ref[0], w0_ref[...].reshape(WIDTH, PAD), 1, 1)

    store_by_owner(grad_ref, 0, dot(rows[...], gh_ref[0, 0], 1, 0))
    store_by_owner(grad_ref, 1, dot(rows[...], gh_ref[0, 1], 1, 0))
    store_by_owner(grad_ref, 2, dot(back[...], act_ref[0], 1, 0))

    @pl.when(step == 1)
    def _():
        sums[...] += dot(act_ref[0], w1_ref[...].reshape(WIDTH, PAD), 1, 1)
        for r in range(M):
            sum_refs[r][...] = sums[r * ROWS : (r + 1) * ROWS, :].astype(BF16)


def mlp_grads(row_blocks, back_blocks, weights, weights_more, act, grad_hidden):
    group = M * ROWS
    return pl.pallas_call(
        mlp_grads_kernel,
        grid=(PRE,),
        in_specs=[whole(ROWS, WIDTH)] * (2 * M)
        + [DOWN_SPEC, DOWN_SPEC, ACT_SPEC, HIDDEN_SPEC],
        out_specs=[pl.BlockSpec((8, 2, 3, 64, PAD), lambda p: (0, 0, p, 0, 0))]
        + [whole(ROWS, WIDTH)] * M,
        out_shape=[jax.ShapeDtypeStruct((8, 2, 3 * PRE + 3, 64, PAD), BF16)]
        + [jax.ShapeDtypeStruct((ROWS, WIDTH), BF16)] * M,
        scratch_shapes=[
            pltpu.VMEM((WIDTH, group), BF16),
            pltpu.VMEM((WIDTH, group), BF16),
            pltpu.VMEM((group, WIDTH), F32),
        ],
        compiler_params=pltpu.CompilerParams(vmem_limit_bytes=VMEM),
        cost_estimate=pl.CostEstimate(
            flops=8_000_000_000, bytes_accessed=12_000_000, transcendentals=0
        ),
        name="mlp_grads",
    )(*row_blocks, *back_blocks, weights, weights_more, act, grad_hidden)


def out_grads_kernel(g_ref, mixed_ref, held_ref, grad_ref):
    del held_ref
    turned = g_ref[...].T
    for b in range(3):
        columns = mixed_ref[:, b * PAD : (b + 1) * PAD]
        store_by_owner(grad_ref, b, dot(turned, columns, 1, 0))


def out_grads(grad_attn, mixed_own, grads):
    return pl.pallas_call(
        out_grads_kernel,
        grid=(1,),
        in_specs=[whole(ROWS, WIDTH), whole(ROWS, 3 * PAD), pl.BlockSpec(memory_space=pl.ANY)],
        out_specs=pl.BlockSpec((8, 2, 3, 64, PAD), lambda p: (0, 0, PRE, 0, 0)),
        out_shape=jax.ShapeDtypeStruct(grads.shape, BF16),
        input_output_aliases={2: 0},
        compiler_params=pltpu.CompilerParams(vmem_limit_bytes=VMEM),
        cost_estimate=pl.CostEstimate(
            flops=400_000_000, bytes_accessed=4_000_000, transcendentals=0
        ),
        name="out_grads",
    )(grad_attn, mixed_own, grads)


def two_parts(value):
    high = value.astype(BF16)
    return high, (value - high.astype(F32)).astype(BF16)


def on_device(tokens, gain_attn, w_qkv, w_out, gain_mlp, w_in, w_down, cotangent):
    own_mlp = jnp.concatenate([w_in, w_down[:, None, :]], axis=1).transpose(1, 0, 2)
    own_mlp = jnp.pad(own_mlp, ((0, 0), (0, 0), (0, PAD - FFB)))
    own_qkv = w_qkv.reshape(64, PAD)
    weights = lax.all_gather(jnp.concatenate([own_mlp, own_qkv[None]], axis=0), FS, axis=0)
    partner_mlp = exchange(own_mlp, PRE_AX, PRE, 1)
    cosine, sine = rope_tables()

    resid = tokens.astype(F32)
    hat_attn, scale_attn = normalize(resid)
    normed_attn = (hat_attn * gain_attn).astype(BF16)
    sent = jnp.concatenate(
        [normed_attn, w_out.reshape(8, WIDTH), jnp.zeros((SENT - ROWS - 8, WIDTH), BF16)], axis=0
    )
    sent = jnp.broadcast_to(sent[None], (8, SENT, WIDTH))
    rows = lax.all_to_all(sent, TP, 0, 0)
    out_wide = rows[:, ROWS : ROWS + 8].reshape(8, 64, 2 * HD).transpose(1, 0, 2)
    out_wide = jnp.pad(out_wide.reshape(64, WIDTH), ((0, 0), (0, 3 * PAD - WIDTH)))
    out_wide = out_wide.reshape(64, 3, PAD).transpose(1, 0, 2)
    weights_more = lax.all_gather(jnp.concatenate([partner_mlp, out_wide], axis=0), FS, axis=0)

    cotangent_later, rows = lax.optimization_barrier((cotangent, rows))
    back_blocks = gather_by_mask(cotangent_later, MLP_AX, M)
    q, k, v, mixed, lse = attend(rows, weights, cosine, sine)
    mixed_own = lax.all_to_all(mixed.reshape(8, ROWS, 2 * HD), TP, 0, 0)
    mixed_own = mixed_own.transpose(1, 0, 2).reshape(ROWS, WIDTH)
    mixed_own = jnp.pad(mixed_own, ((0, 0), (0, 3 * PAD - WIDTH)))
    full_out = [weights_more[:, 3 + b].reshape(WIDTH, PAD) for b in range(3)]
    attn_sum = sum(
        dot(mixed_own[:, b * PAD : (b + 1) * PAD], full_out[b], 1, 1) for b in range(3)
    )
    resid_mid = resid + attn_sum
    hat_mlp, scale_mlp = normalize(resid_mid)
    normed_mlp = (hat_mlp * gain_mlp).astype(BF16)

    row_blocks = gather_by_mask(normed_mlp, MLP_AX, M)
    act, grad_hidden, *dn_parts = mlp(row_blocks, back_blocks, weights, weights_more)
    grad_normed_mlp = total(scatter_by_mask(dn_parts, MLP_AX, M))
    grads, *sum_parts = mlp_grads(
        row_blocks, back_blocks, weights, weights_more, act, grad_hidden
    )

    grad_mid_norm, gain_mlp_part = norm_back(grad_normed_mlp, hat_mlp, scale_mlp, gain_mlp)
    grad_mid = cotangent.astype(F32) + grad_mid_norm
    grad_attn = grad_mid.astype(BF16)
    grad_mixed = jnp.concatenate([dot(grad_attn, full_out[b], 1, 0) for b in range(3)], axis=1)
    grad_mixed = grad_mixed[:, :WIDTH].astype(BF16)
    gm_parts = grad_mixed.reshape(ROWS, 8, 2 * HD).transpose(1, 0, 2)
    grads = out_grads(grad_attn, mixed_own, grads)
    gm_parts, grads = lax.optimization_barrier((gm_parts, grads))
    grads = lax.psum_scatter(grads, ("x", "c"), scatter_dimension=0)
    gm_own = lax.all_to_all(gm_parts, TP, 0, 0).reshape(LEN, 2 * HD)

    *sum_parts, gm_own = lax.optimization_barrier((*sum_parts, gm_own))
    mlp_sum = total(scatter_by_mask(sum_parts, MLP_AX, M))
    layer_out = (resid_mid + mlp_sum).astype(BF16)
    me = lax.axis_index(TP).astype(jnp.int32)[None]
    grad_qkv, *dn_attn_parts = attend_back(
        me, q, k, v, lse, gm_own, cosine, sine, weights
    )
    grad_normed_attn = total(scatter_by_mask(dn_attn_parts, TP, 8))

    qkv_part = qkv_grads(rows, grad_qkv)
    high, low = two_parts(gain_mlp_part.reshape(16, 1, 64))
    extra = jnp.pad(jnp.concatenate([high, low], axis=1), ((0, 0), (0, 14), (0, PAD - 64)))
    got = lax.all_to_all(jnp.concatenate([qkv_part, extra], axis=1), FS, 0, 0)
    got = jnp.sum(got.astype(F32), axis=0)
    grad_qkv_w = got[:64]
    gain_mlp_own = got[64, :64] + got[65, :64]
    gain_own = lax.dynamic_slice_in_dim(gain_attn, lax.axis_index(FS) * 64, 64)
    gain_attn_own = jnp.sum(grad_qkv_w * own_qkv.astype(F32), axis=1) / gain_own
    gains = jnp.concatenate([gain_attn_own, gain_mlp_own])
    gains = jnp.broadcast_to(gains[None, None], (128, 1, 128))
    gains = lax.all_to_all(gains, AXES, 0, 0).reshape(16, 8, 128).sum(axis=1)

    bit = lax.axis_index("zl")
    keep = lax.dynamic_index_in_dim(grads, bit, 0, keepdims=False)
    send = lax.dynamic_index_in_dim(grads, 1 - bit, 0, keepdims=False)
    halves = keep.astype(F32) + exchange(send, ("zl",), 2, 1).astype(F32)
    from_partner = exchange(halves[3:6].astype(BF16), PRE_AX, PRE, 1)
    grad_mlp = halves[:3] + from_partner.astype(F32)
    grad_in = grad_mlp[:2, :, :FFB].transpose(1, 0, 2)
    grad_down = grad_mlp[2, :, :FFB]
    out_parts = halves[6:].astype(BF16).transpose(1, 0, 2).reshape(64, 3 * PAD)[:, :WIDTH]
    out_parts = out_parts.reshape(64, 8, 2 * HD).transpose(1, 0, 2)
    grad_out = jnp.sum(lax.all_to_all(out_parts, TP, 0, 0).astype(F32), axis=0)

    grad_first, _ = norm_back(grad_normed_attn, hat_attn, scale_attn, gain_attn)
    grad_tokens = (grad_mid + grad_first).astype(BF16)
    return (
        layer_out,
        grad_tokens,
        gains[:, :64].reshape(WIDTH),
        grad_qkv_w.reshape(64, 3, 2 * HD),
        grad_out,
        gains[:, 64:].reshape(WIDTH),
        grad_in,
        grad_down,
    )


def solution(mesh):
    fine = Mesh(mesh.devices.reshape(4, 2, 2, 2, 2, 2), AXES)
    in_specs = (
        P(AXES, None),
        P(),
        P(FS, None, TP),
        P(FS, TP),
        P(),
        P(FS, None, TP),
        P(FS, TP),
        P(AXES, None),
    )
    out_specs = (
        P(AXES, None),
        P(AXES, None),
        P(),
        P(FS, None, TP),
        P(FS, TP),
        P(),
        P(FS, None, TP),
        P(FS, TP),
    )
    return jax.shard_map(
        on_device, mesh=fine, in_specs=in_specs, out_specs=out_specs, check_vma=False
    )
```

time: 404 us -> 330 us (0.82)
  starting transfers between devices: 122 us -> 80.9 us
  blocking collectives: 36.9 us -> 0 us
  local copies, waits for them, and re-layouts: 32.3 us -> 19.2 us
  waiting for transfers between devices: 111 us -> 123 us
  Pallas kernels: 50.7 us -> 62 us
  matrix products: 10.8 us -> 3.28 us
  other arithmetic: 17.9 us -> 22.5 us
    ppermute x62 -> x22, starting transfers between devices: 109 us -> 38.6 us  [exchange(): return lax.ppermute(value, axes, [(i, i ^ mask) for i in range(count)])]
    all_to_all x0 -> x6, waiting for transfers between devices: none -> 67.3 us  [the longest x1 40.1 us: on_device(): rows = lax.all_to_all(sent, TP, 0, 0)]
    ppermute x62 -> x22, waiting for transfers between devices: 84.9 us -> 40.6 us  [exchange(): return lax.ppermute(value, axes, [(i, i ^ mask) for i in range(count)])]
    all_to_all x0 -> x6, starting transfers between devices: none -> 42.2 us  [the longest x1 15.1 us: on_device(): gm_own = lax.all_to_all(gm_parts, TP, 0, 0).reshape(LEN, 2 * HD)]
    all_gather x1 -> x0, blocking collectives: 36.9 us -> none  [on_device(): full_qkv = lax.all_gather(w_qkv.transpose(1, 0, 2), FS, axis=1, tiled=True)]
    ppermute x11 -> x0, waiting for transfers between devices: 25.6 us -> none  [the longest x5 11.7 us: on_device(): gains = gains + lax.ppermute(gains, axis, [(0, 1), (1, 0)])]
    all_gather x1 -> x2, waiting for transfers between devices: 0.02 us -> 14.7 us  [the longest x1 14.7 us: on_device(): lax.all_gather(jnp.concatenate([partner_mlp, out_wide], axis=0), FS, axis=0)]
    unnamed x98 -> x51, local copies, waits for them, and re-layouts: 15.9 us -> 3.3 us
  transfers between devices with their start and end apart: 75 -> 31, of which waited for: 30 -> 17; matrix products, arithmetic and copies ran while one was open for 12% -> 9% of each run, Pallas kernels for 10% -> 14%
where the time goes in v2:
time: 330 us; the launch traced here: 325 us
  waiting for transfers between devices  123 us (37%)
  starting transfers between devices  80.9 us (25%)
  Pallas kernels  62 us (19%)
  other arithmetic  22.5 us (7%)
  local copies, waits for them, and re-layouts  19.2 us (6%)
  between operations  14.5 us (4%)
    ppermute x22, waiting for transfers between devices, exchange(): return lax.ppermute(value, axes, [(i, i ^ mask) for i in range(count)])  40.6 us
    all_to_all x1, waiting for transfers between devices, on_device(): rows = lax.all_to_all(sent, TP, 0, 0)  40.1 us
    ppermute x22, starting transfers between devices, exchange(): return lax.ppermute(value, axes, [(i, i ^ mask) for i in range(count)])  38.6 us
    pallas_call x1, Pallas kernels, attend_back(): pl.pallas_call(attend_back_kernel, grid=(1,), in_specs=[pl.BlockSpec(memo...  16 us
    all_to_all x1, starting transfers between devices, on_device(): gm_own = lax.all_to_all(gm_parts, TP, 0, 0).reshape(LEN, 2 * HD)  15.1 us
    all_gather x1, waiting for transfers between devices, on_device(): lax.all_gather(jnp.concatenate([partner_mlp, out_wide], axis=0), FS, axis=0)  14.7 us
    pallas_call x1, Pallas kernels, mlp(): pl.pallas_call(mlp_kernel, grid=(PRE,), in_specs=[whole(ROWS, WIDTH)] * (...  12.9 us
    pallas_call x1, Pallas kernels, mlp_grads(): pl.pallas_call(mlp_grads_kernel, grid=(PRE,), in_specs=[whole(ROWS, WIDTH...  12.3 us
  transfers between devices with their start and end apart: 31, of which 17 were waited for; matrix products, arithmetic and copies ran while one was open for 9% of the time, Pallas kernels for 14%

profile of v2, /device:TPU:0, one launch (start us, length us, event | category | flops | bytes accessed | tf_op | source)
XLA Modules:
  0.0 325.0 jit_solution(8527170078294394250)
XLA Ops:
  15.8 7.9 %all-to-all-start = ((bf16[8,176,1024]{2,1,0:T(8,128)(2,1)}), bf16[8,176,1024]{2,1,0:T(8,128)(2,1)S(1)}, u32[]{:S(2)}, u32[]{:S(2)}) async-start(bf16[8,176,1024]{2,1,0:T(8,128)(2,1)} %broadcast_in_dim.11), calls=%async_computation | async-start | bytes 5767168 | tf_op jit(solution)/shard_map/all_to_all | solution.py:412
  23.7 3.5 %collective-permute-start = (bf16[3,64,384]{2,0,1:T(4,128)(2,1)S(1)}, bf16[3,64,384]{2,0,1:T(4,128)(2,1)}, u32[]{:S(2)}, u32[]{:S(2)}) collective-permute-start(bf16[3,64,384]{2,0,1:T(4,128)(2,1)S(1)} %pad.16), channel_id=1, source_target_pairs={{0,1},{1,0},{2,3},{3,2},{4,5},{5,4},{6,7},{7,6},{8,9},{9,8},{10,11... | collective-permute-start | bytes 442376 | tf_op jit(solution)/shard_map/ppermute | solution.py:33
  27.1 40.1 %all-to-all-done.rows_ref = bf16[8,176,1024]{2,1,0:T(8,128)(2,1)S(1)} async-done(((bf16[8,176,1024]{2,1,0:T(8,128)(2,1)}), bf16[8,176,1024]{2,1,0:T(8,128)(2,1)S(1)}, u32[]{:S(2)}, u32[]{:S(2)}) %all-to-all-start) | async-done | bytes 2883616 | tf_op jit(solution)/shard_map/all_to_all | solution.py:412
  70.0 5.1 %collective-permute-done = bf16[3,64,384]{2,0,1:T(4,128)(2,1)} collective-permute-done((bf16[3,64,384]{2,0,1:T(4,128)(2,1)S(1)}, bf16[3,64,384]{2,0,1:T(4,128)(2,1)}, u32[]{:S(2)}, u32[]{:S(2)}) %collective-permute-start) | collective-permute-done | bytes 147488 | tf_op jit(solution)/shard_map/ppermute | solution.py:33
  77.2 2.4 fusion.21
  81.8 12.0 %attend.1 = (bf16[1280,128]{1,0:T(8,128)(2,1)}, bf16[1280,128]{1,0:T(8,128)(2,1)}, bf16[1280,128]{1,0:T(8,128)(2,1)}, bf16[1280,128]{1,0:T(8,128)(2,1)}, f32[1280,128]{1,0:T(8,128)}) custom-call(bf16[8,176,1024]{2,1,0:T(8,128)(2,1)} %copy-done.4, bf16[16,4,64,384]{3,2,1,0:T(8,128)(2,1)} %bitcast.95, f32[1280,128]{1,0:T(8,128)} %get-tuple-element.151.cos_ref.refs_5_, ...), custom_call_target="tpu_custom_call" | custom-call | flops 6000000000 | bytes 8000000 | tf_op jit(solution)/shard_map/attend/pallas_call | solution.py:136
  93.8 4.0 %all-to-all-start.1 = ((bf16[8,160,128]{2,1,0:T(8,128)(2,1)}), bf16[8,160,128]{2,1,0:T(8,128)(2,1)S(1)}, u32[]{:S(2)}, u32[]{:S(2)}) async-start(bf16[8,160,128]{2,1,0:T(8,128)(2,1)} %bitcast.91), calls=%async_computation.1 | async-start | bytes 655360 | tf_op jit(solution)/shard_map/all_to_all | solution.py:421
  99.8 2.7 collective-permute-start.5
  102.6 4.5 %all-to-all-done.1 = bf16[8,160,128]{2,1,0:T(8,128)(2,1)S(1)} async-done(((bf16[8,160,128]{2,1,0:T(8,128)(2,1)}), bf16[8,160,128]{2,1,0:T(8,128)(2,1)S(1)}, u32[]{:S(2)}, u32[]{:S(2)}) %all-to-all-start.1) | async-done | bytes 327712 | tf_op jit(solution)/shard_map/all_to_all | solution.py:421
  107.1 14.7 %all-gather.7.cloned.1.call-done = bf16[96,64,384]{2,1,0:T(8,128)(2,1)} async-done(((bf16[6,64,384]{2,1,0:T(8,128)(2,1)}), bf16[96,64,384]{2,1,0:T(8,128)(2,1)}) %all-gather.7.cloned.1.call-update) | async-done | bytes 4718608 | tf_op jit(solution)/shard_map/all_gather | solution.py:416
  127.7 3.0 collective-permute-start.2
  132.2 4.8 %collective-permute-done.1.refs_1_ = bf16[160,1024]{1,0:T(8,128)(2,1)S(1)} collective-permute-done((bf16[160,1024]{1,0:T(8,128)(2,1)S(1)}, bf16[160,1024]{1,0:T(8,128)(2,1)S(1)}, u32[]{:S(2)}, u32[]{:S(2)}) %collective-permute-start.1) | collective-permute-done | bytes 327712 | tf_op jit(solution)/shard_map/ppermute | solution.py:33
  137.0 8.3 %collective-permute-done.2.refs_2_ = bf16[160,1024]{1,0:T(8,128)(2,1)S(1)} collective-permute-done((bf16[160,1024]{1,0:T(8,128)(2,1)S(1)}, bf16[160,1024]{1,0:T(8,128)(2,1)S(1)}, u32[]{:S(2)}, u32[]{:S(2)}) %collective-permute-start.2) | collective-permute-done | bytes 327712 | tf_op jit(solution)/shard_map/ppermute | solution.py:33
  148.3 12.9 %mlp.1 = (bf16[2,640,384]{2,1,0:T(8,128)(2,1)}, bf16[2,2,640,384]{3,2,1,0:T(8,128)(2,1)}, bf16[160,1024]{1,0:T(8,128)(2,1)}, bf16[160,1024]{1,0:T(8,128)(2,1)}, ...) custom-call(bf16[160,1024]{1,0:T(8,128)(2,1)} %copy-done.13, bf16[160,1024]{1,0:T(8,128)(2,1)} %copy-done.22, ...), custom_call_target="tpu_custom_call" | custom-call | flops 10000000000 | bytes 10000000 | tf_op jit(solution)/shard_map/mlp/pallas_call | solution.py:295
  165.9 12.3 %mlp_grads.1 = (bf16[8,2,9,64,384]{4,3,2,1,0:T(8,128)(2,1)}, bf16[160,1024]{1,0:T(8,128)(2,1)}, bf16[160,1024]{1,0:T(8,128)(2,1)}, bf16[160,1024]{1,0:T(8,128)(2,1)}, bf16[160,1024]{1,0:T(8,128)(2,1)}) custom-call(bf16[160,1024]{1,0:T(8,128)(2,1)} %copy-done.13, bf16[160,1024]{1,0:T(8,128)(2,1)} %copy-done.22, bf16[160,1024]{1,0:T(8,128)(2,1)} %copy-done.23, ...), custom_call_target="tpu_custom_call" | custom-call | flops 8000000000 | bytes 12000000 | tf_op jit(solution)/shard_map/mlp_grads/pallas_call | solution.py:346
  184.6 3.5 %out_grads.1 = bf16[8,2,9,64,384]{4,3,2,1,0:T(8,128)(2,1)} custom-call(bf16[160,1024]{1,0:T(8,128)(2,1)} %copy-done.1, bf16[160,1152]{1,0:T(8,128)(2,1)} %pad.18.mixed_ref, bf16[8,2,9,64,384]{4,3,2,1,0:T(8,128)(2,1)} %get-tuple-element.55.held_ref), custom_call_target="tpu_custom_call", output_to_operand_aliasing={{}: (2, {})} | custom-call | flops 400000000 | bytes 4000000 | tf_op jit(solution)/shard_map/out_grads/pallas_call | solution.py:377
  189.0 15.1 %all-to-all-start.2 = ((bf16[8,160,128]{2,1,0:T(8,128)(2,1)}), bf16[8,160,128]{2,1,0:T(8,128)(2,1)S(1)}, u32[]{:S(2)}, u32[]{:S(2)}) async-start(bf16[8,160,128]{2,1,0:T(8,128)(2,1)} %bitcast_bitcast_fusion), calls=%async_computation.2 | async-start | bytes 655360 | tf_op jit(solution)/shard_map/all_to_all | solution.py:448
  204.1 8.7 %all-to-all-done.2 = bf16[8,160,128]{2,1,0:T(8,128)(2,1)S(1)} async-done(((bf16[8,160,128]{2,1,0:T(8,128)(2,1)}), bf16[8,160,128]{2,1,0:T(8,128)(2,1)S(1)}, u32[]{:S(2)}, u32[]{:S(2)}) %all-to-all-start.2) | async-done | bytes 327712 | tf_op jit(solution)/shard_map/all_to_all | solution.py:448
  213.5 16.0 %attend_back.1 = (bf16[1280,384]{1,0:T(8,128)(2,1)}, bf16[160,1024]{1,0:T(8,128)(2,1)}, bf16[160,1024]{1,0:T(8,128)(2,1)}, bf16[160,1024]{1,0:T(8,128)(2,1)}, bf...) custom-call(s32[1]{0:T(128)} %bitcast.13.me_ref, ...), custom_call_target="tpu_custom_call" | custom-call | flops 12000000000 | bytes 8000000 | tf_op jit(solution)/shard_map/attend_back/pallas_call | solution.py:193
  231.5 3.2 collective-permute-start.15
  236.1 2.8 collective-permute-start.17
  238.9 2.8 collective-permute-done.13
  242.8 2.9 collective-permute-start.19
  245.7 5.3 %qkv_grads.1 = bf16[16,64,384]{2,1,0:T(8,128)(2,1)} custom-call(bf16[8,176,1024]{2,1,0:T(8,128)(2,1)} %copy-done.4, bf16[1280,384]{1,0:T(8,128)(2,1)} %get-tuple-element.74.g_ref), custom_call_target="tpu_custom_call" | custom-call | flops 2000000000 | bytes 5000000 | tf_op jit(solution)/shard_map/qkv_grads/pallas_call | solution.py:222
  253.4 3.6 %all-to-all-start.3 = ((bf16[16,80,384]{2,1,0:T(8,128)(2,1)}), bf16[16,80,384]{2,1,0:T(8,128)(2,1)S(1)}, u32[]{:S(2)}, u32[]{:S(2)}) async-start(bf16[16,80,384]{2,1,0:T(8,128)(2,1)} %pad_maximum_fusion), calls=%async_computation.3 | async-start | bytes 1966080 | tf_op jit(solution)/shard_map/all_to_all | solution.py:462
  257.2 2.6 collective-permute-start.11
  262.4 9.7 %collective-permute-done.19 = bf16[160,1024]{1,0:T(8,128)(2,1)} collective-permute-done((bf16[160,1024]{1,0:T(8,128)(2,1)}, bf16[160,1024]{1,0:T(8,128)(2,1)}, u32[]{:S(2)}, u32[]{:S(2)}) %collective-permute-start.19) | collective-permute-done | bytes 327712 | tf_op jit(solution)/shard_map/ppermute | solution.py:33
  275.0 4.9 %collective-permute-done.12 = bf16[160,1024]{1,0:T(8,128)(2,1)S(1)} collective-permute-done((bf16[160,1024]{1,0:T(8,128)(2,1)}, bf16[160,1024]{1,0:T(8,128)(2,1)S(1)}, u32[]{:S(2)}, u32[]{:S(2)}) %collective-permute-start.12) | collective-permute-done | bytes 327712 | tf_op jit(solution)/shard_map/ppermute | solution.py:33
  283.9 7.5 %all-to-all-start.4 = ((f32[128,1,128]{2,1,0:T(1,128)}), f32[128,1,128]{2,1,0:T(1,128)S(1)}, u32[]{:S(2)}, u32[]{:S(2)}) async-start(f32[128,1,128]{2,1,0:T(1,128)} %broadcast_in_dim.14), calls=%async_computation.4 | async-start | bytes 131072 | tf_op jit(solution)/shard_map/all_to_all | solution.py:470
  293.0 7.5 %all-to-all-done.4 = f32[128,1,128]{2,1,0:T(1,128)S(1)} async-done(((f32[128,1,128]{2,1,0:T(1,128)}), f32[128,1,128]{2,1,0:T(1,128)S(1)}, u32[]{:S(2)}, u32[]{:S(2)}) %all-to-all-start.4) | async-done | bytes 65568 | tf_op jit(solution)/shard_map/all_to_all | solution.py:470
  304.1 4.1 %all-to-all-start.5 = ((bf16[8,64,128]{2,1,0:T(8,128)(2,1)}), bf16[8,64,128]{2,1,0:T(8,128)(2,1)S(1)}, u32[]{:S(2)}, u32[]{:S(2)}) async-start(bf16[8,64,128]{2,1,0:T(8,128)(2,1)} %bitcast_bitcast_fusion.1), calls=%async_computation.6 | async-start | bytes 262144 | tf_op jit(solution)/shard_map/all_to_all | solution.py:482
  309.6 6.5 %all-to-all-done.5 = bf16[8,64,128]{2,1,0:T(8,128)(2,1)S(1)} async-done(((bf16[8,64,128]{2,1,0:T(8,128)(2,1)}), bf16[8,64,128]{2,1,0:T(8,128)(2,1)S(1)}, u32[]{:S(2)}, u32[]{:S(2)}) %all-to-all-start.5) | async-done | bytes 131104 | tf_op jit(solution)/shard_map/all_to_all | solution.py:482
  (163 shorter events, 65.5 us)
Async XLA Ops:
  7.2 74.6 %all-gather.5.cloned.1.call-start = ((), (), s32[]{:S(2)}) async-start(), calls=%async_computation.8 | async-start | bytes 3342336 | tf_op jit(solution)/shard_map/all_gather | solution.py:401
  15.8 51.5 %all-to-all-start = ((bf16[8,176,1024]{2,1,0:T(8,128)(2,1)}), bf16[8,176,1024]{2,1,0:T(8,128)(2,1)S(1)}, u32[]{:S(2)}, u32[]{:S(2)}) async-start(bf16[8,176,1024]{2,1,0:T(8,128)(2,1)} %broadcast_in_dim.11), calls=%async_computation | async-start | bytes 5767168 | tf_op jit(solution)/shard_map/all_to_all | solution.py:412
  23.6 98.2 %all-gather.7.cloned.1.call-start = ((), (), s32[]{:S(2)}) async-start(), calls=%async_computation.9 | async-start | bytes 5013504 | tf_op jit(solution)/shard_map/all_gather | solution.py:416
  23.7 51.5 %collective-permute-start = (bf16[3,64,384]{2,0,1:T(4,128)(2,1)S(1)}, bf16[3,64,384]{2,0,1:T(4,128)(2,1)}, u32[]{:S(2)}, u32[]{:S(2)}) collective-permute-start(bf16[3,64,384]{2,0,1:T(4,128)(2,1)S(1)} %pad.16), channel_id=1, source_target_pairs={{0,1},{1,0},{2,3},{3,2},{4,5},{5,4},{6,7},{7,6},{8,9},{9,8},{10,11... | collective-permute-start | bytes 442376 | tf_op jit(solution)/shard_map/ppermute | solution.py:33
  93.8 13.3 %all-to-all-start.1 = ((bf16[8,160,128]{2,1,0:T(8,128)(2,1)}), bf16[8,160,128]{2,1,0:T(8,128)(2,1)S(1)}, u32[]{:S(2)}, u32[]{:S(2)}) async-start(bf16[8,160,128]{2,1,0:T(8,128)(2,1)} %bitcast.91), calls=%async_computation.1 | async-start | bytes 655360 | tf_op jit(solution)/shard_map/all_to_all | solution.py:421
  97.8 183.5 %reduce-scatter.2.cloned.1.call-start = ((), (), s32[]{:S(2)}) async-start(), calls=%async_computation.7 | async-start | bytes 7962624 | tf_op jit(solution)/shard_map/reduce_scatter | solution.py:447
  97.8 32.8 %collective-permute-start.4 = (bf16[160,1024]{1,0:T(8,128)(2,1)}, bf16[160,1024]{1,0:T(8,128)(2,1)}, u32[]{:S(2)}, u32[]{:S(2)}) collective-permute-start(bf16[160,1024]{1,0:T(8,128)(2,1)} %refs_4_.1), channel_id=1, source_target_pairs={{0,2},{2,0},{4,6},{6,4},{1,3},{3,1},{5,7},{7,5},{8,10},{10,8},{12,... | collective-permute-start | bytes 983048 | tf_op jit(solution)/shard_map/ppermute | solution.py:33
  99.8 32.4 %collective-permute-start.5 = (bf16[160,1024]{1,0:T(8,128)(2,1)}, bf16[160,1024]{1,0:T(8,128)(2,1)}, u32[]{:S(2)}, u32[]{:S(2)}) collective-permute-start(bf16[160,1024]{1,0:T(8,128)(2,1)} %refs_4_.1), channel_id=1, source_target_pairs={{0,4},{2,6},{4,0},{6,2},{1,5},{3,7},{5,1},{7,3},{8,12},{10,14},{12... | collective-permute-start | bytes 983048 | tf_op jit(solution)/shard_map/ppermute | solution.py:33
  102.5 29.8 %collective-permute-start.6 = (bf16[160,1024]{1,0:T(8,128)(2,1)}, bf16[160,1024]{1,0:T(8,128)(2,1)}, u32[]{:S(2)}, u32[]{:S(2)}) collective-permute-start(bf16[160,1024]{1,0:T(8,128)(2,1)} %refs_4_.1), channel_id=1, source_target_pairs={{0,6},{2,4},{4,2},{6,0},{1,7},{3,5},{5,3},{7,1},{8,14},{10,12},{12... | collective-permute-start | bytes 983048 | tf_op jit(solution)/shard_map/ppermute | solution.py:33
  126.4 10.6 %collective-permute-start.1 = (bf16[160,1024]{1,0:T(8,128)(2,1)S(1)}, bf16[160,1024]{1,0:T(8,128)(2,1)S(1)}, u32[]{:S(2)}, u32[]{:S(2)}) collective-permute-start(bf16[160,1024]{1,0:T(8,128)(2,1)S(1)} %multiply_convert_fusion.refs_0_), channel_id=1, source_target_pairs={{0,2},{2,0},{4,6},{6,4},{1,3},{3,1},{5,7},{7,5},{8,10},{10,8},{12,... | collective-permute-start | bytes 983048 | tf_op jit(solution)/shard_map/ppermute | solution.py:33
  127.7 17.7 %collective-permute-start.2 = (bf16[160,1024]{1,0:T(8,128)(2,1)S(1)}, bf16[160,1024]{1,0:T(8,128)(2,1)S(1)}, u32[]{:S(2)}, u32[]{:S(2)}) collective-permute-start(bf16[160,1024]{1,0:T(8,128)(2,1)S(1)} %multiply_convert_fusion.refs_0_), channel_id=1, source_target_pairs={{0,4},{2,6},{4,0},{6,2},{1,5},{3,7},{5,1},{7,3},{8,12},{10,14},{12... | collective-permute-start | bytes 983048 | tf_op jit(solution)/shard_map/ppermute | solution.py:33
  130.6 17.6 %collective-permute-start.3 = (bf16[160,1024]{1,0:T(8,128)(2,1)S(1)}, bf16[160,1024]{1,0:T(8,128)(2,1)}, u32[]{:S(2)}, u32[]{:S(2)}) collective-permute-start(bf16[160,1024]{1,0:T(8,128)(2,1)S(1)} %multiply_convert_fusion.refs_0_), channel_id=1, source_target_pairs={{0,6},{2,4},{4,2},{6,0},{1,7},{3,5},{5,3},{7,1},{8,14},{10,12},{12... | collective-permute-start | bytes 983048 | tf_op jit(solution)/shard_map/ppermute | solution.py:33
  161.1 17.1 %collective-permute-start.7 = (bf16[160,1024]{1,0:T(8,128)(2,1)}, bf16[160,1024]{1,0:T(8,128)(2,1)}, u32[]{:S(2)}, u32[]{:S(2)}) collective-permute-start(bf16[160,1024]{1,0:T(8,128)(2,1)} %get-tuple-element.52), channel_id=1, source_target_pairs={{0,2},{2,0},{4,6},{6,4},{1,3},{3,1},{5,7},{7,5},{8,10},{10,8},{12,... | collective-permute-start | bytes 983048 | tf_op jit(solution)/shard_map/ppermute | solution.py:33
  161.2 17.0 %collective-permute-start.8 = (bf16[160,1024]{1,0:T(8,128)(2,1)}, bf16[160,1024]{1,0:T(8,128)(2,1)}, u32[]{:S(2)}, u32[]{:S(2)}) collective-permute-start(bf16[160,1024]{1,0:T(8,128)(2,1)} %get-tuple-element.53), channel_id=1, source_target_pairs={{0,4},{2,6},{4,0},{6,2},{1,5},{3,7},{5,1},{7,3},{8,12},{10,14},{12... | collective-permute-start | bytes 983048 | tf_op jit(solution)/shard_map/ppermute | solution.py:33
  163.5 16.4 %collective-permute-start.9 = (bf16[160,1024]{1,0:T(8,128)(2,1)}, bf16[160,1024]{1,0:T(8,128)(2,1)}, u32[]{:S(2)}, u32[]{:S(2)}) collective-permute-start(bf16[160,1024]{1,0:T(8,128)(2,1)} %get-tuple-element.54), channel_id=1, source_target_pairs={{0,6},{2,4},{4,2},{6,0},{1,7},{3,5},{5,3},{7,1},{8,14},{10,12},{12... | collective-permute-start | bytes 983048 | tf_op jit(solution)/shard_map/ppermute | solution.py:33
  189.0 23.8 %all-to-all-start.2 = ((bf16[8,160,128]{2,1,0:T(8,128)(2,1)}), bf16[8,160,128]{2,1,0:T(8,128)(2,1)S(1)}, u32[]{:S(2)}, u32[]{:S(2)}) async-start(bf16[8,160,128]{2,1,0:T(8,128)(2,1)} %bitcast_bitcast_fusion), calls=%async_computation.2 | async-start | bytes 655360 | tf_op jit(solution)/shard_map/all_to_all | solution.py:448
  229.5 12.2 %collective-permute-start.13 = (bf16[160,1024]{1,0:T(8,128)(2,1)}, bf16[160,1024]{1,0:T(8,128)(2,1)S(1)}, u32[]{:S(2)}, u32[]{:S(2)}) collective-permute-start(bf16[160,1024]{1,0:T(8,128)(2,1)} %get-tuple-element.67), channel_id=1, source_target_pairs={{0,1},{1,0},{2,3},{3,2},{4,5},{5,4},{6,7},{7,6},{8,9},{9,8},{10,11... | collective-permute-start | bytes 983048 | tf_op jit(solution)/shard_map/ppermute | solution.py:33
  230.8 12.0 %collective-permute-start.14 = (bf16[160,1024]{1,0:T(8,128)(2,1)}, bf16[160,1024]{1,0:T(8,128)(2,1)S(1)}, u32[]{:S(2)}, u32[]{:S(2)}) collective-permute-start(bf16[160,1024]{1,0:T(8,128)(2,1)} %get-tuple-element.68), channel_id=1, source_target_pairs={{0,2},{1,3},{2,0},{3,1},{4,6},{5,7},{6,4},{7,5},{8,10},{9,11},{10,... | collective-permute-start | bytes 983048 | tf_op jit(solution)/shard_map/ppermute | solution.py:33
  231.5 25.6 %collective-permute-start.15 = (bf16[160,1024]{1,0:T(8,128)(2,1)}, bf16[160,1024]{1,0:T(8,128)(2,1)S(1)}, u32[]{:S(2)}, u32[]{:S(2)}) collective-permute-start(bf16[160,1024]{1,0:T(8,128)(2,1)} %get-tuple-element.69), channel_id=1, source_target_pairs={{0,3},{1,2},{2,1},{3,0},{4,7},{5,6},{6,5},{7,4},{8,11},{9,10},{10,... | collective-permute-start | bytes 983048 | tf_op jit(solution)/shard_map/ppermute | solution.py:33
  234.7 22.5 %collective-permute-start.16 = (bf16[160,1024]{1,0:T(8,128)(2,1)}, bf16[160,1024]{1,0:T(8,128)(2,1)}, u32[]{:S(2)}, u32[]{:S(2)}) collective-permute-start(bf16[160,1024]{1,0:T(8,128)(2,1)} %get-tuple-element.70), channel_id=1, source_target_pairs={{0,4},{1,5},{2,6},{3,7},{4,0},{5,1},{6,2},{7,3},{8,12},{9,13},{10,... | collective-permute-start | bytes 983048 | tf_op jit(solution)/shard_map/ppermute | solution.py:33
  236.1 23.8 %collective-permute-start.17 = (bf16[160,1024]{1,0:T(8,128)(2,1)}, bf16[160,1024]{1,0:T(8,128)(2,1)}, u32[]{:S(2)}, u32[]{:S(2)}) collective-permute-start(bf16[160,1024]{1,0:T(8,128)(2,1)} %get-tuple-element.71), channel_id=1, source_target_pairs={{0,5},{1,4},{2,7},{3,6},{4,1},{5,0},{6,3},{7,2},{8,13},{9,12},{10,... | collective-permute-start | bytes 983048 | tf_op jit(solution)/shard_map/ppermute | solution.py:33
  241.7 20.7 %collective-permute-start.18 = (bf16[160,1024]{1,0:T(8,128)(2,1)}, bf16[160,1024]{1,0:T(8,128)(2,1)}, u32[]{:S(2)}, u32[]{:S(2)}) collective-permute-start(bf16[160,1024]{1,0:T(8,128)(2,1)} %get-tuple-element.72), channel_id=1, source_target_pairs={{0,6},{1,7},{2,4},{3,5},{4,2},{5,3},{6,0},{7,1},{8,14},{9,15},{10,... | collective-permute-start | bytes 983048 | tf_op jit(solution)/shard_map/ppermute | solution.py:33
  242.8 29.4 %collective-permute-start.19 = (bf16[160,1024]{1,0:T(8,128)(2,1)}, bf16[160,1024]{1,0:T(8,128)(2,1)}, u32[]{:S(2)}, u32[]{:S(2)}) collective-permute-start(bf16[160,1024]{1,0:T(8,128)(2,1)} %get-tuple-element.73), channel_id=1, source_target_pairs={{0,7},{1,6},{2,5},{3,4},{4,3},{5,2},{6,1},{7,0},{8,15},{9,14},{10,... | collective-permute-start | bytes 983048 | tf_op jit(solution)/shard_map/ppermute | solution.py:33
  253.4 27.5 %all-to-all-start.3 = ((bf16[16,80,384]{2,1,0:T(8,128)(2,1)}), bf16[16,80,384]{2,1,0:T(8,128)(2,1)S(1)}, u32[]{:S(2)}, u32[]{:S(2)}) async-start(bf16[16,80,384]{2,1,0:T(8,128)(2,1)} %pad_maximum_fusion), calls=%async_computation.3 | async-start | bytes 1966080 | tf_op jit(solution)/shard_map/all_to_all | solution.py:462
  257.0 22.8 %copy-start.7 = (bf16[160,1024]{1,0:T(8,128)(2,1)S(1)}, bf16[160,1024]{1,0:T(8,128)(2,1)}, u32[]{:S(2)}) copy-start(bf16[160,1024]{1,0:T(8,128)(2,1)} %get-tuple-element.57) | copy-start | bytes 983044
  257.1 17.2 %collective-permute-start.10 = (bf16[160,1024]{1,0:T(8,128)(2,1)}, bf16[160,1024]{1,0:T(8,128)(2,1)S(1)}, u32[]{:S(2)}, u32[]{:S(2)}) collective-permute-start(bf16[160,1024]{1,0:T(8,128)(2,1)} %get-tuple-element.58), channel_id=1, source_target_pairs={{0,2},{2,0},{4,6},{6,4},{1,3},{3,1},{5,7},{7,5},{8,10},{10,8},{12,... | collective-permute-start | bytes 983048 | tf_op jit(solution)/shard_map/ppermute | solution.py:33
  257.2 17.8 %collective-permute-start.11 = (bf16[160,1024]{1,0:T(8,128)(2,1)}, bf16[160,1024]{1,0:T(8,128)(2,1)S(1)}, u32[]{:S(2)}, u32[]{:S(2)}) collective-permute-start(bf16[160,1024]{1,0:T(8,128)(2,1)} %get-tuple-element.59), channel_id=1, source_target_pairs={{0,4},{2,6},{4,0},{6,2},{1,5},{3,7},{5,1},{7,3},{8,12},{10,14},{12... | collective-permute-start | bytes 983048 | tf_op jit(solution)/shard_map/ppermute | solution.py:33
  260.0 19.9 %collective-permute-start.12 = (bf16[160,1024]{1,0:T(8,128)(2,1)}, bf16[160,1024]{1,0:T(8,128)(2,1)S(1)}, u32[]{:S(2)}, u32[]{:S(2)}) collective-permute-start(bf16[160,1024]{1,0:T(8,128)(2,1)} %get-tuple-element.60), channel_id=1, source_target_pairs={{0,6},{2,4},{4,2},{6,0},{1,7},{3,5},{5,3},{7,1},{8,14},{10,12},{12... | collective-permute-start | bytes 983048 | tf_op jit(solution)/shard_map/ppermute | solution.py:33
  282.4 18.2 %collective-permute-start.20 = (bf16[9,64,384]{2,1,0:T(8,128)(2,1)S(1)}, bf16[9,64,384]{2,1,0:T(8,128)(2,1)}, u32[]{:S(2)}, u32[]{:S(2)}) collective-permute-start(bf16[9,64,384]{2,1,0:T(8,128)(2,1)S(1)} %dynamic-slice_bitcast_fusion), channel_id=1, source_target_pairs={{0,16},{16,0},{1,17},{17,1},{2,18},{18,2},{3,19},{19,3},{4,20},{20... | collective-permute-start | bytes 1327112 | tf_op jit(solution)/shard_map/ppermute | solution.py:33
  283.9 16.6 %all-to-all-start.4 = ((f32[128,1,128]{2,1,0:T(1,128)}), f32[128,1,128]{2,1,0:T(1,128)S(1)}, u32[]{:S(2)}, u32[]{:S(2)}) async-start(f32[128,1,128]{2,1,0:T(1,128)} %broadcast_in_dim.14), calls=%async_computation.4 | async-start | bytes 131072 | tf_op jit(solution)/shard_map/all_to_all | solution.py:470
  301.8 15.0 %collective-permute-start.21 = (bf16[3,64,384]{2,1,0:T(8,128)(2,1)S(1)}, bf16[3,64,384]{2,1,0:T(8,128)(2,1)S(1)}, u32[]{:S(2)}, u32[]{:S(2)}) collective-permute-start(bf16[3,64,384]{2,1,0:T(8,128)(2,1)S(1)} %get-tuple-element.138), channel_id=1, source_target_pairs={{0,1},{1,0},{2,3},{3,2},{4,5},{5,4},{6,7},{7,6},{8,9},{9,8},{10,11... | collective-permute-start | bytes 442376 | tf_op jit(solution)/shard_map/ppermute | solution.py:33
  304.1 12.0 %all-to-all-start.5 = ((bf16[8,64,128]{2,1,0:T(8,128)(2,1)}), bf16[8,64,128]{2,1,0:T(8,128)(2,1)S(1)}, u32[]{:S(2)}, u32[]{:S(2)}) async-start(bf16[8,64,128]{2,1,0:T(8,128)(2,1)} %bitcast_bitcast_fusion.1), calls=%async_computation.6 | async-start | bytes 262144 | tf_op jit(solution)/shard_map/all_to_all | solution.py:482
  (23 other events, 257.4 us)
Sparse Core Ops, SparseCore 0:
  11.3 65.7 all-gather.4
  78.9 42.8 all-gather.6
  189.1 46.0 reduce-scatter.1

commit v3 on v2

--- a/solution.py
+++ b/solution.py
@@ -1,5 +1,8 @@
+import functools
+
 import jax
 import jax.numpy as jnp
+import numpy as np
 from jax import lax
 from jax.experimental import pallas as pl
 from jax.experimental.pallas import tpu as pltpu
@@ -15,7 +18,6 @@
 FFB = 328
 PAD = 384
 QB = 256
-SENT = 176
 VMEM = 60 * 1024 * 1024
 
 AXES = ("x", "zl", "c", "yh", "yl", "zh")
@@ -66,12 +68,12 @@
 
 def rope_tables():
     half = HD // 2
-    freqs = THETA ** (-jnp.arange(half, dtype=F32) * 2.0 / HD)
-    angles = jnp.arange(LEN, dtype=F32)[:, None] * freqs[None, :]
-    cosine, sine = jnp.cos(angles), jnp.sin(angles)
+    freqs = THETA ** (-np.arange(half) * 2.0 / HD)
+    angles = np.arange(LEN)[:, None] * freqs[None, :]
+    cosine, sine = np.cos(angles), np.sin(angles)
     return (
-        jnp.concatenate([cosine] * 4, axis=1),
-        jnp.concatenate([-sine, sine, -sine, sine], axis=1),
+        jnp.asarray(np.concatenate([cosine] * 4, axis=1), F32),
+        jnp.asarray(np.concatenate([-sine, sine, -sine, sine], axis=1), F32),
     )
 
 
@@ -243,111 +245,120 @@
                 ref[x * 2 + c, zl, at] = value[row : row + 64, :]
 
 
-def mlp_kernel(*refs):
-    row_refs, back_refs = refs[:M], refs[M : 2 * M]
-    w0_ref, w1_ref, act_ref, gh_ref = refs[2 * M : 2 * M + 4]
-    dn_refs = refs[2 * M + 4 : 3 * M + 4]
-    rows, back, dn, weights = refs[3 * M + 4 :]
-    step = pl.program_id(0)
-
-    @pl.when(step == 0)
-    def _():
-        for r in range(M):
-            rows[r * ROWS : (r + 1) * ROWS, :] = row_refs[r][...]
-            back[r * ROWS : (r + 1) * ROWS, :] = back_refs[r][...]
-        dn[...] = jnp.zeros_like(dn)
-        weights[...] = w0_ref[...]
-
-    @pl.when(step == 1)
-    def _():
-        weights[...] = w1_ref[...]
-
-    w_act = weights[:, 0].reshape(WIDTH, PAD)
-    w_gate = weights[:, 1].reshape(WIDTH, PAD)
-    w_down = weights[:, 2].reshape(WIDTH, PAD)
-    a_in = dot(rows[...], w_act, 1, 0)
-    gate = dot(rows[...], w_gate, 1, 0)
-    grad_act = dot(back[...], w_down, 1, 0)
-    cdf = 0.5 * (1.0 + lax.erf(a_in * (0.5**0.5)))
-    gelu = a_in * cdf
-    slope = cdf + a_in * (jnp.exp(-0.5 * a_in * a_in) * 0.3989422804014327)
-    act_ref[0] = (gelu * gate).astype(BF16)
-    g_act = (grad_act * gate * slope).astype(BF16)
-    g_gate = (grad_act * gelu).astype(BF16)
-    gh_ref[0, 0] = g_act
-    gh_ref[0, 1] = g_gate
-    dn[...] += dot(g_act, w_act, 1, 1) + dot(g_gate, w_gate, 1, 1)
-
-    @pl.when(step == PRE - 1)
-    def _():
-        for r in range(M):
-            dn_refs[r][...] = dn[r * ROWS : (r + 1) * ROWS, :].astype(BF16)
+def mlp_kernel(count, *refs):
+    row_refs, back_refs = refs[:count], refs[count : 2 * count]
+    w0_ref, w1_ref, act_ref, gh_ref = refs[2 * count : 2 * count + 4]
+    dn_refs = refs[2 * count + 4 : 3 * count + 4]
+    rows, back, dn = refs[3 * count + 4 :]
+    for r in range(count):
+        rows[r * ROWS : (r + 1) * ROWS, :] = row_refs[r][...]
+        back[r * ROWS : (r + 1) * ROWS, :] = back_refs[r][...]
+    for step, w_ref in enumerate((w0_ref, w1_ref)):
+        w_act = w_ref[:, 0].reshape(WIDTH, PAD)
+        w_gate = w_ref[:, 1].reshape(WIDTH, PAD)
+        w_down = w_ref[:, 2].reshape(WIDTH, PAD)
+        a_in = dot(rows[...], w_act, 1, 0)
+        gate = dot(rows[...], w_gate, 1, 0)
+        grad_act = dot(back[...], w_down, 1, 0)
+        cdf = 0.5 * (1.0 + lax.erf(a_in * (0.5**0.5)))
+        gelu = a_in * cdf
+        slope = cdf + a_in * (jnp.exp(-0.5 * a_in * a_in) * 0.3989422804014327)
+        act_ref[step] = (gelu * gate).astype(BF16)
+        g_act = (grad_act * gate * slope).astype(BF16)
+        g_gate = (grad_act * gelu).astype(BF16)
+        gh_ref[step, 0] = g_act
+        gh_ref[step, 1] = g_gate
+        part = dot(g_act, w_act, 1, 1) + dot(g_gate, w_gate, 1, 1)
+        if step == 0:
+            dn[...] = part
+        else:
+            dn[...] += part
+    for r in range(count):
+        dn_refs[r][...] = dn[r * ROWS : (r + 1) * ROWS, :].astype(BF16)
 
 
 MLP_SPEC = pl.BlockSpec((16, 3, 64, PAD), lambda p: (0, 0, 0, 0))
+MORE_SPEC = pl.BlockSpec((16, 3, 64, PAD), lambda p: (0, 1, 0, 0))
 DOWN_SPEC = pl.BlockSpec((16, 1, 64, PAD), lambda p: (0, 2, 0, 0))
-ACT_SPEC = pl.BlockSpec((1, M * ROWS, PAD), lambda p: (p, 0, 0))
-HIDDEN_SPEC = pl.BlockSpec((1, 2, M * ROWS, PAD), lambda p: (p, 0, 0, 0))
-
-
-def mlp(row_blocks, back_blocks, weights, weights_more):
-    group = M * ROWS
+DOWN_MORE_SPEC = pl.BlockSpec((16, 1, 64, PAD), lambda p: (0, 5, 0, 0))
+
+
+def act_spec(count):
+    return pl.BlockSpec((1, count * ROWS, PAD), lambda p: (p, 0, 0))
+
+
+def hidden_spec(count):
+    return pl.BlockSpec((1, 2, count * ROWS, PAD), lambda p: (p, 0, 0, 0))
+
+
+def mlp(row_blocks, back_blocks, weights):
+    count = len(row_blocks)
+    group = count * ROWS
     return pl.pallas_call(
-        mlp_kernel,
-        grid=(PRE,),
-        in_specs=[whole(ROWS, WIDTH)] * (2 * M) + [MLP_SPEC, MLP_SPEC],
-        out_specs=[ACT_SPEC, HIDDEN_SPEC] + [whole(ROWS, WIDTH)] * M,
+        functools.partial(mlp_kernel, count),
+        grid=(1,),
+        in_specs=[whole(ROWS, WIDTH)] * (2 * count) + [MLP_SPEC, MORE_SPEC],
+        out_specs=[whole(PRE, group, PAD), whole(PRE, 2, group, PAD)]
+        + [whole(ROWS, WIDTH)] * count,
         out_shape=[
             jax.ShapeDtypeStruct((PRE, group, PAD), BF16),
             jax.ShapeDtypeStruct((PRE, 2, group, PAD), BF16),
         ]
-        + [jax.ShapeDtypeStruct((ROWS, WIDTH), BF16)] * M,
+        + [jax.ShapeDtypeStruct((ROWS, WIDTH), BF16)] * count,
         scratch_shapes=[
             pltpu.VMEM((group, WIDTH), BF16),
             pltpu.VMEM((group, WIDTH), BF16),
             pltpu.VMEM((group, WIDTH), F32),
-            pltpu.VMEM((16, 3, 64, PAD), BF16),
         ],
         compiler_params=pltpu.CompilerParams(vmem_limit_bytes=VMEM),
         cost_estimate=pl.CostEstimate(
-            flops=10_000_000_000, bytes_accessed=10_000_000, transcendentals=1_000_000
+            flops=5_000_000_000, bytes_accessed=8_000_000, transcendentals=500_000
         ),
         name="mlp",
-    )(*row_blocks, *back_blocks, weights, weights_more)
+    )(*row_blocks, *back_blocks, weights, weights)
 
 
 def mlp_grads_kernel(*refs):
     row_refs, back_refs = refs[:M], refs[M : 2 * M]
-    w0_ref, w1_ref, act_ref, gh_ref, grad_ref = refs[2 * M : 2 * M + 5]
-    sum_refs = refs[2 * M + 5 : 3 * M + 5]
-    rows, back, sums = refs[3 * M + 5 :]
+    w0_ref, w1_ref, act0_ref, act1_ref, gh0_ref, gh1_ref, grad_ref = refs[2 * M : 2 * M + 7]
+    sum_refs = refs[2 * M + 7 : 3 * M + 7]
+    rows, back, sums = refs[3 * M + 7 :]
     step = pl.program_id(0)
+    half = M // 2 * ROWS
 
     @pl.when(step == 0)
     def _():
         for r in range(M):
             rows[:, r * ROWS : (r + 1) * ROWS] = row_refs[r][...].T
             back[:, r * ROWS : (r + 1) * ROWS] = back_refs[r][...].T
-        sums[...] = dot(act_ref[0], w0_ref[...].reshape(WIDTH, PAD), 1, 1)
-
-    store_by_owner(grad_ref, 0, dot(rows[...], gh_ref[0, 0], 1, 0))
-    store_by_owner(grad_ref, 1, dot(rows[...], gh_ref[0, 1], 1, 0))
-    store_by_owner(grad_ref, 2, dot(back[...], act_ref[0], 1, 0))
+        w_down = w0_ref[...].reshape(WIDTH, PAD)
+        sums[:half] = dot(act0_ref[0], w_down, 1, 1)
+        sums[half:] = dot(act1_ref[0], w_down, 1, 1)
+
+    act = jnp.concatenate([act0_ref[0], act1_ref[0]], axis=0)
+    for c in range(2):
+        grad_hidden = jnp.concatenate([gh0_ref[0, c], gh1_ref[0, c]], axis=0)
+        store_by_owner(grad_ref, c, dot(rows[...], grad_hidden, 1, 0))
+    store_by_owner(grad_ref, 2, dot(back[...], act, 1, 0))
 
     @pl.when(step == 1)
     def _():
-        sums[...] += dot(act_ref[0], w1_ref[...].reshape(WIDTH, PAD), 1, 1)
+        w_down = w1_ref[...].reshape(WIDTH, PAD)
+        sums[:half] += dot(act0_ref[0], w_down, 1, 1)
+        sums[half:] += dot(act1_ref[0], w_down, 1, 1)
         for r in range(M):
             sum_refs[r][...] = sums[r * ROWS : (r + 1) * ROWS, :].astype(BF16)
 
 
-def mlp_grads(row_blocks, back_blocks, weights, weights_more, act, grad_hidden):
+def mlp_grads(row_blocks, back_blocks, weights, acts, grads_hidden):
     group = M * ROWS
     return pl.pallas_call(
         mlp_grads_kernel,
         grid=(PRE,),
         in_specs=[whole(ROWS, WIDTH)] * (2 * M)
-        + [DOWN_SPEC, DOWN_SPEC, ACT_SPEC, HIDDEN_SPEC],
+        + [DOWN_SPEC, DOWN_MORE_SPEC]
+        + [act_spec(M // 2)] * 2
+        + [hidden_spec(M // 2)] * 2,
         out_specs=[pl.BlockSpec((8, 2, 3, 64, PAD), lambda p: (0, 0, p, 0, 0))]
         + [whole(ROWS, WIDTH)] * M,
         out_shape=[jax.ShapeDtypeStruct((8, 2, 3 * PRE + 3, 64, PAD), BF16)]
@@ -362,7 +373,7 @@
             flops=8_000_000_000, bytes_accessed=12_000_000, transcendentals=0
         ),
         name="mlp_grads",
-    )(*row_blocks, *back_blocks, weights, weights_more, act, grad_hidden)
+    )(*row_blocks, *back_blocks, weights, weights, *acts, *grads_hidden)
 
 
 def out_grads_kernel(g_ref, mixed_ref, held_ref, grad_ref):
@@ -398,30 +409,37 @@
     own_mlp = jnp.concatenate([w_in, w_down[:, None, :]], axis=1).transpose(1, 0, 2)
     own_mlp = jnp.pad(own_mlp, ((0, 0), (0, 0), (0, PAD - FFB)))
     own_qkv = w_qkv.reshape(64, PAD)
-    weights = lax.all_gather(jnp.concatenate([own_mlp, own_qkv[None]], axis=0), FS, axis=0)
+    out_wide = lax.all_to_all(jnp.broadcast_to(w_out[None], (8, 64, 2 * HD)), TP, 0, 0)
+    out_wide = out_wide.transpose(1, 0, 2).reshape(64, WIDTH)
+    out_wide = jnp.concatenate([out_wide, jnp.zeros((64, 2 * HD), BF16), own_qkv], axis=1)
+    out_wide = out_wide.reshape(64, 4, PAD).transpose(1, 0, 2)
+    weights = lax.all_gather(out_wide, FS, axis=0)
     partner_mlp = exchange(own_mlp, PRE_AX, PRE, 1)
+    weights_mlp = lax.all_gather(jnp.concatenate([own_mlp, partner_mlp], axis=0), FS, axis=0)
     cosine, sine = rope_tables()
 
     resid = tokens.astype(F32)
     hat_attn, scale_attn = normalize(resid)
     normed_attn = (hat_attn * gain_attn).astype(BF16)
-    sent = jnp.concatenate(
-        [normed_attn, w_out.reshape(8, WIDTH), jnp.zeros((SENT - ROWS - 8, WIDTH), BF16)], axis=0
-    )
-    sent = jnp.broadcast_to(sent[None], (8, SENT, WIDTH))
-    rows = lax.all_to_all(sent, TP, 0, 0)
-    out_wide = rows[:, ROWS : ROWS + 8].reshape(8, 64, 2 * HD).transpose(1, 0, 2)
-    out_wide = jnp.pad(out_wide.reshape(64, WIDTH), ((0, 0), (0, 3 * PAD - WIDTH)))
-    out_wide = out_wide.reshape(64, 3, PAD).transpose(1, 0, 2)
-    weights_more = lax.all_gather(jnp.concatenate([partner_mlp, out_wide], axis=0), FS, axis=0)
+    partner_rows = exchange(normed_attn, PRE_AX, PRE, 1)
+    first = lax.axis_index("zh") == 0
+    pair = jnp.stack(
+        [
+            jnp.where(first, normed_attn, partner_rows),
+            jnp.where(first, partner_rows, normed_attn),
+        ]
+    )
+    rows = lax.all_to_all(jnp.broadcast_to(pair[None], (M, PRE, ROWS, WIDTH)), MLP_AX, 0, 0)
+    rows = rows.reshape(8, ROWS, WIDTH)
 
     cotangent_later, rows = lax.optimization_barrier((cotangent, rows))
     back_blocks = gather_by_mask(cotangent_later, MLP_AX, M)
     q, k, v, mixed, lse = attend(rows, weights, cosine, sine)
+    mixed, *back_blocks = lax.optimization_barrier((mixed, *back_blocks))
     mixed_own = lax.all_to_all(mixed.reshape(8, ROWS, 2 * HD), TP, 0, 0)
     mixed_own = mixed_own.transpose(1, 0, 2).reshape(ROWS, WIDTH)
     mixed_own = jnp.pad(mixed_own, ((0, 0), (0, 3 * PAD - WIDTH)))
-    full_out = [weights_more[:, 3 + b].reshape(WIDTH, PAD) for b in range(3)]
+    full_out = [weights[:, b].reshape(WIDTH, PAD) for b in range(3)]
     attn_sum = sum(
         dot(mixed_own[:, b * PAD : (b + 1) * PAD], full_out[b], 1, 1) for b in range(3)
     )
@@ -430,10 +448,13 @@
     normed_mlp = (hat_mlp * gain_mlp).astype(BF16)
 
     row_blocks = gather_by_mask(normed_mlp, MLP_AX, M)
-    act, grad_hidden, *dn_parts = mlp(row_blocks, back_blocks, weights, weights_more)
-    grad_normed_mlp = total(scatter_by_mask(dn_parts, MLP_AX, M))
+    act0, hidden0, *dn0 = mlp(row_blocks[:2], back_blocks[:2], weights_mlp)
+    *later, dn0[1] = lax.optimization_barrier((*row_blocks[2:], dn0[1]))
+    row_blocks = row_blocks[:2] + later
+    act1, hidden1, *dn1 = mlp(row_blocks[2:], back_blocks[2:], weights_mlp)
+    grad_normed_mlp = total(scatter_by_mask(dn0 + dn1, MLP_AX, M))
     grads, *sum_parts = mlp_grads(
-        row_blocks, back_blocks, weights, weights_more, act, grad_hidden
+        row_blocks, back_blocks, weights_mlp, (act0, act1), (hidden0, hidden1)
     )
 
     grad_mid_norm, gain_mlp_part = norm_back(grad_normed_mlp, hat_mlp, scale_mlp, gain_mlp)
@@ -443,18 +464,19 @@
     grad_mixed = grad_mixed[:, :WIDTH].astype(BF16)
     gm_parts = grad_mixed.reshape(ROWS, 8, 2 * HD).transpose(1, 0, 2)
     grads = out_grads(grad_attn, mixed_own, grads)
-    gm_parts, grads = lax.optimization_barrier((gm_parts, grads))
     grads = lax.psum_scatter(grads, ("x", "c"), scatter_dimension=0)
     gm_own = lax.all_to_all(gm_parts, TP, 0, 0).reshape(LEN, 2 * HD)
 
     *sum_parts, gm_own = lax.optimization_barrier((*sum_parts, gm_own))
-    mlp_sum = total(scatter_by_mask(sum_parts, MLP_AX, M))
-    layer_out = (resid_mid + mlp_sum).astype(BF16)
+    sum_parts = scatter_by_mask(sum_parts, MLP_AX, M)
     me = lax.axis_index(TP).astype(jnp.int32)[None]
     grad_qkv, *dn_attn_parts = attend_back(
         me, q, k, v, lse, gm_own, cosine, sine, weights
     )
-    grad_normed_attn = total(scatter_by_mask(dn_attn_parts, TP, 8))
+    held = lax.optimization_barrier((*sum_parts, *dn_attn_parts))
+    sum_parts, dn_attn_parts = held[:M], held[M:]
+    layer_out = (resid_mid + total(sum_parts)).astype(BF16)
+    received = scatter_by_mask(dn_attn_parts, TP, 8)
 
     qkv_part = qkv_grads(rows, grad_qkv)
     high, low = two_parts(gain_mlp_part.reshape(16, 1, 64))
@@ -466,9 +488,6 @@
     gain_own = lax.dynamic_slice_in_dim(gain_attn, lax.axis_index(FS) * 64, 64)
     gain_attn_own = jnp.sum(grad_qkv_w * own_qkv.astype(F32), axis=1) / gain_own
     gains = jnp.concatenate([gain_attn_own, gain_mlp_own])
-    gains = jnp.broadcast_to(gains[None, None], (128, 1, 128))
-    gains = lax.all_to_all(gains, AXES, 0, 0).reshape(16, 8, 128).sum(axis=1)
-
     bit = lax.axis_index("zl")
     keep = lax.dynamic_index_in_dim(grads, bit, 0, keepdims=False)
     send = lax.dynamic_index_in_dim(grads, 1 - bit, 0, keepdims=False)
@@ -479,8 +498,11 @@
     grad_down = grad_mlp[2, :, :FFB]
     out_parts = halves[6:].astype(BF16).transpose(1, 0, 2).reshape(64, 3 * PAD)[:, :WIDTH]
     out_parts = out_parts.reshape(64, 8, 2 * HD).transpose(1, 0, 2)
+    gains = jnp.broadcast_to(gains[None, None], (128, 1, 128))
+    gains = lax.all_to_all(gains, AXES, 0, 0).reshape(16, 8, 128).sum(axis=1)
     grad_out = jnp.sum(lax.all_to_all(out_parts, TP, 0, 0).astype(F32), axis=0)
 
+    grad_normed_attn = total(received)
     grad_first, _ = norm_back(grad_normed_attn, hat_attn, scale_attn, gain_attn)
     grad_tokens = (grad_mid + grad_first).astype(BF16)
     return (

time: 330 us -> 294 us (0.89); the launches traced: 325 us -> 293 us
  waiting for transfers between devices: 123 us -> 73.4 us
  blocking collectives: 0 us -> 33.3 us
  starting transfers between devices: 80.9 us -> 70.8 us
  local copies, waits for them, and re-layouts: 19.2 us -> 14.1 us
    all_to_all x0 -> x1, blocking collectives: none -> 33.3 us  [on_device(): lax.all_to_all(jnp.broadcast_to(pair[None], (M, PRE, ROWS, WIDTH)), MLP_A...]
    all_to_all x1, waiting for transfers between devices: 40.1 us -> 7.82 us  [on_device(): lax.all_to_all(jnp.broadcast_to(w_out[None], (8, 64, 2 * HD)), TP, 0, 0)]
    all_gather x2, waiting for transfers between devices: 14.7 us -> 0.01 us  [the longest x1 0.01 us: on_device(): lax.all_gather(jnp.concatenate([own_mlp, partner_mlp], axis=0), FS, axis=0)]
    ppermute x22 -> x23, waiting for transfers between devices: 40.6 us -> 26.9 us  [exchange(): return lax.ppermute(value, axes, [(i, i ^ mask) for i in range(count)])]
    all_to_all x1, starting transfers between devices: 15.1 us -> 4.77 us  [on_device(): gm_own = lax.all_to_all(gm_parts, TP, 0, 0).reshape(LEN, 2 * HD)]
    all_to_all x1, waiting for transfers between devices: 0.01 us -> 6.76 us  [on_device(): got = lax.all_to_all(jnp.concatenate([qkv_part, extra], axis=1), FS, 0, 0)]
    pallas_call x1 -> x2, Pallas kernels: 12.9 us -> 14.8 us  [mlp(): pl.pallas_call(functools.partial(mlp_kernel, count), grid=(1,), in_specs=...]
    ppermute x22 -> x23, starting transfers between devices: 38.6 us -> 37.6 us  [exchange(): return lax.ppermute(value, axes, [(i, i ^ mask) for i in range(count)])]
  transfers between devices with their start and end apart: 31 -> 32, of which waited for: 17 -> 11; matrix products, arithmetic and copies ran while one was open for 9% -> 9% of each run, Pallas kernels for 14% -> 18%
where the time goes in v3:
time: 294 us; the launch traced here: 293 us
  waiting for transfers between devices  73.4 us (25%)
  starting transfers between devices  70.8 us (24%)
  Pallas kernels  64.2 us (22%)
  blocking collectives  33.3 us (11%)
  other arithmetic  19.5 us (7%)
  between operations  14.3 us (5%)
  local copies, waits for them, and re-layouts  14.1 us (5%)
  matrix products  3.5 us (1%)
    ppermute x23, starting transfers between devices, exchange(): return lax.ppermute(value, axes, [(i, i ^ mask) for i in range(count)])  37.6 us
    all_to_all x1, blocking collectives, on_device(): lax.all_to_all(jnp.broadcast_to(pair[None], (M, PRE, ROWS, WIDTH)), MLP_A...  33.3 us
    ppermute x23, waiting for transfers between devices, exchange(): return lax.ppermute(value, axes, [(i, i ^ mask) for i in range(count)])  26.9 us
    pallas_call x1, Pallas kernels, attend_back(): pl.pallas_call(attend_back_kernel, grid=(1,), in_specs=[pl.BlockSpec(memo...  16 us
    pallas_call x2, Pallas kernels, mlp(): pl.pallas_call(functools.partial(mlp_kernel, count), grid=(1,), in_specs=...  14.8 us
    pallas_call x1, Pallas kernels, mlp_grads(): pl.pallas_call(mlp_grads_kernel, grid=(PRE,), in_specs=[whole(ROWS, WIDTH...  12.5 us
    pallas_call x1, Pallas kernels, attend(): pl.pallas_call(attend_kernel, grid=(1,), in_specs=[ROWS_SPEC, QKV_SPEC, w...  12 us
    all_to_all x1, waiting for transfers between devices, on_device(): gm_own = lax.all_to_all(gm_parts, TP, 0, 0).reshape(LEN, 2 * HD)  11.7 us
  transfers between devices with their start and end apart: 32, of which 11 were waited for; matrix products, arithmetic and copies ran while one was open for 9% of the time, Pallas kernels for 18%

profile of v3, /device:TPU:0, one launch (start us, length us, event | category | flops | bytes accessed | tf_op | source)
XLA Modules:
  0.0 293.3 jit_solution(10605424993281788763)
XLA Ops:
  8.6 7.9 %all-to-all-start.1 = ((bf16[8,64,128]{2,1,0:T(8,128)(2,1)}), bf16[8,64,128]{2,1,0:T(8,128)(2,1)S(1)}, u32[]{:S(2)}, u32[]{:S(2)}) async-start(bf16[8,64,128]{2,1,0:T(8,128)(2,1)} %broadcast_in_dim.13), calls=%async_computation.1 | async-start | bytes 262144 | tf_op jit(solution)/shard_map/all_to_all | solution.py:412
  16.6 7.8 %all-to-all-done.1 = bf16[8,64,128]{2,1,0:T(8,128)(2,1)S(1)} async-done(((bf16[8,64,128]{2,1,0:T(8,128)(2,1)}), bf16[8,64,128]{2,1,0:T(8,128)(2,1)S(1)}, u32[]{:S(2)}, u32[]{:S(2)}) %all-to-all-start.1) | async-done | bytes 131104 | tf_op jit(solution)/shard_map/all_to_all | solution.py:412
  28.2 5.6 %collective-permute-done.7 = bf16[3,64,384]{2,1,0:T(8,128)(2,1)S(1)} collective-permute-done((bf16[3,64,384]{2,1,0:T(8,128)(2,1)S(1)}, bf16[3,64,384]{2,1,0:T(8,128)(2,1)S(1)}, u32[]{:S(2)}, u32[]{:S(2)}) %collective-permute-start.7) | collective-permute-done | bytes 147488 | tf_op jit(solution)/shard_map/ppermute | solution.py:35
  36.4 15.1 %collective-permute-done = bf16[160,1024]{1,0:T(8,128)(2,1)S(1)} collective-permute-done((bf16[160,1024]{1,0:T(8,128)(2,1)S(1)}, bf16[160,1024]{1,0:T(8,128)(2,1)S(1)}, u32[]{:S(2)}, u32[]{:S(2)}) %collective-permute-start) | collective-permute-done | bytes 327712 | tf_op jit(solution)/shard_map/ppermute | solution.py:35
  52.2 33.3 %all_to_all.35 = bf16[4,2,160,1024]{3,2,1,0:T(8,128)(2,1)} all-to-all(bf16[4,2,160,1024]{3,2,1,0:T(8,128)(2,1)S(1)} %broadcast_in_dim.12), channel_id=1, replica_groups=mesh['x'=4,'zl'=2,'c'=2,'yh'=2,'yl'=2,'zh'=2] {'yh','yl'}, dimensions={0} | all-to-all | bytes 5242880 | tf_op jit(solution)/shard_map/all_to_all | solution.py:432
  87.3 3.0 %collective-permute-start.3 = (bf16[160,1024]{1,0:T(8,128)(2,1)S(1)}, bf16[160,1024]{1,0:T(8,128)(2,1)S(1)}, u32[]{:S(2)}, u32[]{:S(2)}) collective-permute-start(bf16[160,1024]{1,0:T(8,128)(2,1)S(1)} %copy-done.6), channel_id=1, source_target_pairs={{0,6},{2,4},{4,2},{6,0},{1,7},{3,5},{5,3},{7,1},{8,14},{10,12},{12... | collective-permute-start | bytes 983048 | tf_op jit(solution)/shard_map/ppermute | solution.py:35
  90.3 12.0 %attend.1 = (bf16[1280,128]{1,0:T(8,128)(2,1)}, bf16[1280,128]{1,0:T(8,128)(2,1)}, bf16[1280,128]{1,0:T(8,128)(2,1)}, bf16[1280,128]{1,0:T(8,128)(2,1)}, f32[1280,128]{1,0:T(8,128)}) custom-call(bf16[8,160,1024]{2,1,0:T(8,128)(2,1)} %bitcast.91, bf16[16,4,64,384]{3,2,1,0:T(8,128)(2,1)} %bitcast.93, f32[1280,128]{1,0:T(8,128)} %constant.65.clone.cos_ref.refs_5_, ...), custom_call_target="tpu_custom_call" | custom-call | flops 6000000000 | bytes 8000000 | tf_op jit(solution)/shard_map/attend/pallas_call | solution.py:138
  102.3 3.4 %all-to-all-start.2 = ((bf16[8,160,128]{2,1,0:T(8,128)(2,1)}), bf16[8,160,128]{2,1,0:T(8,128)(2,1)S(1)}, u32[]{:S(2)}, u32[]{:S(2)}) async-start(bf16[8,160,128]{2,1,0:T(8,128)(2,1)} %bitcast.99), calls=%async_computation.2 | async-start | bytes 655360 | tf_op jit(solution)/shard_map/all_to_all | solution.py:439
  107.8 6.9 %all-to-all-done.2 = bf16[8,160,128]{2,1,0:T(8,128)(2,1)S(1)} async-done(((bf16[8,160,128]{2,1,0:T(8,128)(2,1)}), bf16[8,160,128]{2,1,0:T(8,128)(2,1)S(1)}, u32[]{:S(2)}, u32[]{:S(2)}) %all-to-all-start.2) | async-done | bytes 327712 | tf_op jit(solution)/shard_map/all_to_all | solution.py:439
  117.0 2.9 collective-permute-start.5
  124.4 7.4 %mlp.2 = (bf16[2,320,384]{2,1,0:T(8,128)(2,1)}, bf16[2,2,320,384]{3,2,1,0:T(8,128)(2,1)}, bf16[160,1024]{1,0:T(8,128)(2,1)}, bf16[160,1024]{1,0:T(8,128)(2,1)}) custom-call(bf16[160,1024]{1,0:T(8,128)(2,1)} %copy-done.15, bf16[160,1024]{1,0:T(8,128)(2,1)} %copy-done.24, bf16[160,1024]{1,0:T(8,128)(2,1)} %refs_4_, bf16[160,1024]{1,0:T(8,128)(2,1)} %copy-done.21, ...), custom_call_target="tpu_custom_call" | custom-call | flops 5000000000 | bytes 8000000 | tf_op jit(solution)/shard_map/mlp/pallas_call | solution.py:297
  131.8 7.4 %mlp.3 = (bf16[2,320,384]{2,1,0:T(8,128)(2,1)}, bf16[2,2,320,384]{3,2,1,0:T(8,128)(2,1)}, bf16[160,1024]{1,0:T(8,128)(2,1)}, bf16[160,1024]{1,0:T(8,128)(2,1)}) custom-call(bf16[160,1024]{1,0:T(8,128)(2,1)} %collective-permute-done.5.refs_0_.refs_2_, bf16[160,1024]{1,0:T(8,128)(2,1)} %collective-permute-done.6.refs_1_.refs_3_, bf16[160,1024]{1,0:T(8,128)(2,1)} %copy-done.22, ...), custom_call_target="tpu_custom_call" | custom-call | flops 5000000000 | bytes 8000000 | tf_op jit(solution)/shard_map/mlp/pallas_call | solution.py:297
  143.3 12.5 %mlp_grads.1 = (bf16[8,2,9,64,384]{4,3,2,1,0:T(8,128)(2,1)}, bf16[160,1024]{1,0:T(8,128)(2,1)}, bf16[160,1024]{1,0:T(8,128)(2,1)}, bf16[160,1024]{1,0:T(8,128)(2,1)}, bf16[160,1024]{1,0:T(8,128)(2,1)}) custom-call(bf16[160,1024]{1,0:T(8,128)(2,1)} %copy-done.15, bf16[160,1024]{1,0:T(8,128)(2,1)} %copy-done.24, ...), custom_call_target="tpu_custom_call" | custom-call | flops 8000000000 | bytes 12000000 | tf_op jit(solution)/shard_map/mlp_grads/pallas_call | solution.py:355
  158.6 3.5 %out_grads.1 = bf16[8,2,9,64,384]{4,3,2,1,0:T(8,128)(2,1)} custom-call(bf16[160,1024]{1,0:T(8,128)(2,1)} %get-tuple-element.164.g_ref, bf16[160,1152]{1,0:T(8,128)(2,1)} %pad.12.mixed_ref, bf16[8,2,9,64,384]{4,3,2,1,0:T(8,128)(2,1)} %get-tuple-element.115.held_ref), custom_call_target="tpu_custom_call", output_to_operand_aliasing={{}: (2, {})} | custom-call | flops 400000000 | bytes 4000000 | tf_op jit(solution)/shard_map/out_grads/pallas_call | solution.py:388
  166.0 4.8 %all-to-all-start.3 = ((bf16[8,160,128]{2,1,0:T(8,128)(2,1)}), bf16[8,160,128]{2,1,0:T(8,128)(2,1)S(1)}, u32[]{:S(2)}, u32[]{:S(2)}) async-start(bf16[8,160,128]{2,1,0:T(8,128)(2,1)} %bitcast_bitcast_fusion), calls=%async_computation.3 | async-start | bytes 655360 | tf_op jit(solution)/shard_map/all_to_all | solution.py:468
  170.9 11.7 %all-to-all-done.3 = bf16[8,160,128]{2,1,0:T(8,128)(2,1)S(1)} async-done(((bf16[8,160,128]{2,1,0:T(8,128)(2,1)}), bf16[8,160,128]{2,1,0:T(8,128)(2,1)S(1)}, u32[]{:S(2)}, u32[]{:S(2)}) %all-to-all-start.3) | async-done | bytes 327712 | tf_op jit(solution)/shard_map/all_to_all | solution.py:468
  182.6 3.5 %collective-permute-start.12 = (bf16[160,1024]{1,0:T(8,128)(2,1)}, bf16[160,1024]{1,0:T(8,128)(2,1)S(1)}, u32[]{:S(2)}, u32[]{:S(2)}) collective-permute-start(bf16[160,1024]{1,0:T(8,128)(2,1)} %get-tuple-element.87), channel_id=1, source_target_pairs={{0,4},{2,6},{4,0},{6,2},{1,5},{3,7},{5,1},{7,3},{8,12},{10,14},{12... | collective-permute-start | bytes 983048 | tf_op jit(solution)/shard_map/ppermute | solution.py:35
  187.3 16.0 %attend_back.1 = (bf16[1280,384]{1,0:T(8,128)(2,1)}, bf16[160,1024]{1,0:T(8,128)(2,1)}, bf16[160,1024]{1,0:T(8,128)(2,1)}, bf16[160,1024]{1,0:T(8,128)(2,1)}, bf...) custom-call(s32[1]{0:T(128)} %bitcast.16.me_ref, ...), custom_call_target="tpu_custom_call" | custom-call | flops 12000000000 | bytes 8000000 | tf_op jit(solution)/shard_map/attend_back/pallas_call | solution.py:195
  204.8 5.4 %qkv_grads.1 = bf16[16,64,384]{2,1,0:T(8,128)(2,1)} custom-call(bf16[8,160,1024]{2,1,0:T(8,128)(2,1)} %bitcast.92, bf16[1280,384]{1,0:T(8,128)(2,1)} %get-tuple-element.114.g_ref), custom_call_target="tpu_custom_call" | custom-call | flops 2000000000 | bytes 5000000 | tf_op jit(solution)/shard_map/qkv_grads/pallas_call | solution.py:224
  210.2 3.8 %collective-permute-start.16 = (bf16[160,1024]{1,0:T(8,128)(2,1)}, bf16[160,1024]{1,0:T(8,128)(2,1)}, u32[]{:S(2)}, u32[]{:S(2)}) collective-permute-start(bf16[160,1024]{1,0:T(8,128)(2,1)} %get-tuple-element.109), channel_id=1, source_target_pairs={{0,3},{1,2},{2,1},{3,0},{4,7},{5,6},{6,5},{7,4},{8,11},{9,10},{10,... | collective-permute-start | bytes 983048 | tf_op jit(solution)/shard_map/ppermute | solution.py:35
  215.5 2.6 collective-permute-start.18
  219.3 3.8 %collective-permute-start.20 = (bf16[160,1024]{1,0:T(8,128)(2,1)}, bf16[160,1024]{1,0:T(8,128)(2,1)}, u32[]{:S(2)}, u32[]{:S(2)}) collective-permute-start(bf16[160,1024]{1,0:T(8,128)(2,1)} %get-tuple-element.113), channel_id=1, source_target_pairs={{0,7},{1,6},{2,5},{3,4},{4,3},{5,2},{6,1},{7,0},{8,15},{9,14},{10,... | collective-permute-start | bytes 983048 | tf_op jit(solution)/shard_map/ppermute | solution.py:35
  223.1 2.3 pad_maximum_fusion
  225.4 6.0 %all-to-all-start.4 = ((bf16[16,80,384]{2,1,0:T(8,128)(2,1)}), bf16[16,80,384]{2,1,0:T(8,128)(2,1)S(1)}, u32[]{:S(2)}, u32[]{:S(2)}) async-start(bf16[16,80,384]{2,1,0:T(8,128)(2,1)} %pad_maximum_fusion), calls=%async_computation.4 | async-start | bytes 1966080 | tf_op jit(solution)/shard_map/all_to_all | solution.py:484
  231.4 1.9 add_convert_fusion
  233.7 4.2 %collective-permute-done.20 = bf16[160,1024]{1,0:T(8,128)(2,1)} collective-permute-done((bf16[160,1024]{1,0:T(8,128)(2,1)}, bf16[160,1024]{1,0:T(8,128)(2,1)}, u32[]{:S(2)}, u32[]{:S(2)}) %collective-permute-start.20) | collective-permute-done | bytes 327712 | tf_op jit(solution)/shard_map/ppermute | solution.py:35
  237.9 2.1 fusion.26
  241.2 6.8 %all-to-all-done.4 = bf16[16,80,384]{2,1,0:T(8,128)(2,1)S(1)} async-done(((bf16[16,80,384]{2,1,0:T(8,128)(2,1)}), bf16[16,80,384]{2,1,0:T(8,128)(2,1)S(1)}, u32[]{:S(2)}, u32[]{:S(2)}) %all-to-all-start.4) | async-done | bytes 983072 | tf_op jit(solution)/shard_map/all_to_all | solution.py:484
  253.0 7.2 %all-to-all-start.5 = ((f32[128,1,128]{2,1,0:T(1,128)}), f32[128,1,128]{2,1,0:T(1,128)}, u32[]{:S(2)}, u32[]{:S(2)}) async-start(f32[128,1,128]{2,1,0:T(1,128)} %broadcast_in_dim.17), calls=%async_computation.5 | async-start | bytes 131072 | tf_op jit(solution)/shard_map/all_to_all | solution.py:502
  262.6 6.7 %all-to-all-done.5 = f32[128,1,128]{2,1,0:T(1,128)} async-done(((f32[128,1,128]{2,1,0:T(1,128)}), f32[128,1,128]{2,1,0:T(1,128)}, u32[]{:S(2)}, u32[]{:S(2)}) %all-to-all-start.5) | async-done | bytes 65568 | tf_op jit(solution)/shard_map/all_to_all | solution.py:502
  272.7 4.0 %all-to-all-start.6 = ((bf16[8,64,128]{2,1,0:T(8,128)(2,1)}), bf16[8,64,128]{2,1,0:T(8,128)(2,1)S(1)}, u32[]{:S(2)}, u32[]{:S(2)}) async-start(bf16[8,64,128]{2,1,0:T(8,128)(2,1)} %bitcast_bitcast_fusion.1), calls=%async_computation.7 | async-start | bytes 262144 | tf_op jit(solution)/shard_map/all_to_all | solution.py:503
  278.1 6.5 %all-to-all-done.6 = bf16[8,64,128]{2,1,0:T(8,128)(2,1)S(1)} async-done(((bf16[8,64,128]{2,1,0:T(8,128)(2,1)}), bf16[8,64,128]{2,1,0:T(8,128)(2,1)S(1)}, u32[]{:S(2)}, u32[]{:S(2)}) %all-to-all-start.6) | async-done | bytes 131104 | tf_op jit(solution)/shard_map/all_to_all | solution.py:503
  (160 shorter events, 50.9 us)
Async XLA Ops:
  8.6 15.8 %all-to-all-start.1 = ((bf16[8,64,128]{2,1,0:T(8,128)(2,1)}), bf16[8,64,128]{2,1,0:T(8,128)(2,1)S(1)}, u32[]{:S(2)}, u32[]{:S(2)}) async-start(bf16[8,64,128]{2,1,0:T(8,128)(2,1)} %broadcast_in_dim.13), calls=%async_computation.1 | async-start | bytes 262144 | tf_op jit(solution)/shard_map/all_to_all | solution.py:412
  16.5 73.8 %all-gather.5.cloned.1.call-start = ((), (), s32[]{:S(2)}) async-start(), calls=%async_computation.9 | async-start | bytes 3342336 | tf_op jit(solution)/shard_map/all_gather | solution.py:416
  25.3 98.4 %all-gather.7.cloned.1.call-start = ((), (), s32[]{:S(2)}) async-start(), calls=%async_computation.10 | async-start | bytes 5013504 | tf_op jit(solution)/shard_map/all_gather | solution.py:418
  27.1 6.7 %collective-permute-start.7 = (bf16[3,64,384]{2,1,0:T(8,128)(2,1)S(1)}, bf16[3,64,384]{2,1,0:T(8,128)(2,1)S(1)}, u32[]{:S(2)}, u32[]{:S(2)}) collective-permute-start(bf16[3,64,384]{2,1,0:T(8,128)(2,1)S(1)} %pad.13), channel_id=1, source_target_pairs={{0,1},{1,0},{2,3},{3,2},{4,5},{5,4},{6,7},{7,6},{8,9},{9,8},{10,11... | collective-permute-start | bytes 442376 | tf_op jit(solution)/shard_map/ppermute | solution.py:35
  35.3 16.2 %collective-permute-start = (bf16[160,1024]{1,0:T(8,128)(2,1)S(1)}, bf16[160,1024]{1,0:T(8,128)(2,1)S(1)}, u32[]{:S(2)}, u32[]{:S(2)}) collective-permute-start(bf16[160,1024]{1,0:T(8,128)(2,1)S(1)} %fusion.6), channel_id=1, source_target_pairs={{0,1},{1,0},{2,3},{3,2},{4,5},{5,4},{6,7},{7,6},{8,9},{9,8},{10,11... | collective-permute-start | bytes 983048 | tf_op jit(solution)/shard_map/ppermute | solution.py:35
  85.6 16.7 %collective-permute-start.1 = (bf16[160,1024]{1,0:T(8,128)(2,1)S(1)}, bf16[160,1024]{1,0:T(8,128)(2,1)S(1)}, u32[]{:S(2)}, u32[]{:S(2)}) collective-permute-start(bf16[160,1024]{1,0:T(8,128)(2,1)S(1)} %copy-done.6), channel_id=1, source_target_pairs={{0,2},{2,0},{4,6},{6,4},{1,3},{3,1},{5,7},{7,5},{8,10},{10,8},{12,... | collective-permute-start | bytes 983048 | tf_op jit(solution)/shard_map/ppermute | solution.py:35
  87.0 15.3 %collective-permute-start.2 = (bf16[160,1024]{1,0:T(8,128)(2,1)S(1)}, bf16[160,1024]{1,0:T(8,128)(2,1)S(1)}, u32[]{:S(2)}, u32[]{:S(2)}) collective-permute-start(bf16[160,1024]{1,0:T(8,128)(2,1)S(1)} %copy-done.6), channel_id=1, source_target_pairs={{0,4},{2,6},{4,0},{6,2},{1,5},{3,7},{5,1},{7,3},{8,12},{10,14},{12... | collective-permute-start | bytes 983048 | tf_op jit(solution)/shard_map/ppermute | solution.py:35
  87.3 15.0 %collective-permute-start.3 = (bf16[160,1024]{1,0:T(8,128)(2,1)S(1)}, bf16[160,1024]{1,0:T(8,128)(2,1)S(1)}, u32[]{:S(2)}, u32[]{:S(2)}) collective-permute-start(bf16[160,1024]{1,0:T(8,128)(2,1)S(1)} %copy-done.6), channel_id=1, source_target_pairs={{0,6},{2,4},{4,2},{6,0},{1,7},{3,5},{5,3},{7,1},{8,14},{10,12},{12... | collective-permute-start | bytes 983048 | tf_op jit(solution)/shard_map/ppermute | solution.py:35
  102.3 12.3 %all-to-all-start.2 = ((bf16[8,160,128]{2,1,0:T(8,128)(2,1)}), bf16[8,160,128]{2,1,0:T(8,128)(2,1)S(1)}, u32[]{:S(2)}, u32[]{:S(2)}) async-start(bf16[8,160,128]{2,1,0:T(8,128)(2,1)} %bitcast.99), calls=%async_computation.2 | async-start | bytes 655360 | tf_op jit(solution)/shard_map/all_to_all | solution.py:439
  105.8 143.5 %reduce-scatter.2.cloned.1.call-start = ((), (), s32[]{:S(2)}) async-start(), calls=%async_computation.8 | async-start | bytes 7962624 | tf_op jit(solution)/shard_map/reduce_scatter | solution.py:467
  116.5 7.2 %collective-permute-start.4 = (bf16[160,1024]{1,0:T(8,128)(2,1)S(1)}, bf16[160,1024]{1,0:T(8,128)(2,1)S(1)}, u32[]{:S(2)}, u32[]{:S(2)}) collective-permute-start(bf16[160,1024]{1,0:T(8,128)(2,1)S(1)} %multiply_convert_fusion.refs_0_), channel_id=1, source_target_pairs={{0,2},{2,0},{4,6},{6,4},{1,3},{3,1},{5,7},{7,5},{8,10},{10,8},{12,... | collective-permute-start | bytes 983048 | tf_op jit(solution)/shard_map/ppermute | solution.py:35
  117.0 14.8 %collective-permute-start.5 = (bf16[160,1024]{1,0:T(8,128)(2,1)S(1)}, bf16[160,1024]{1,0:T(8,128)(2,1)}, u32[]{:S(2)}, u32[]{:S(2)}) collective-permute-start(bf16[160,1024]{1,0:T(8,128)(2,1)S(1)} %multiply_convert_fusion.refs_0_), channel_id=1, source_target_pairs={{0,4},{2,6},{4,0},{6,2},{1,5},{3,7},{5,1},{7,3},{8,12},{10,14},{12... | collective-permute-start | bytes 983048 | tf_op jit(solution)/shard_map/ppermute | solution.py:35
  119.9 11.9 %collective-permute-start.6 = (bf16[160,1024]{1,0:T(8,128)(2,1)S(1)}, bf16[160,1024]{1,0:T(8,128)(2,1)}, u32[]{:S(2)}, u32[]{:S(2)}) collective-permute-start(bf16[160,1024]{1,0:T(8,128)(2,1)S(1)} %multiply_convert_fusion.refs_0_), channel_id=1, source_target_pairs={{0,6},{2,4},{4,2},{6,0},{1,7},{3,5},{5,3},{7,1},{8,14},{10,12},{12... | collective-permute-start | bytes 983048 | tf_op jit(solution)/shard_map/ppermute | solution.py:35
  139.2 16.6 %collective-permute-start.10 = (bf16[160,1024]{1,0:T(8,128)(2,1)}, bf16[160,1024]{1,0:T(8,128)(2,1)S(1)}, u32[]{:S(2)}, u32[]{:S(2)}) collective-permute-start(bf16[160,1024]{1,0:T(8,128)(2,1)} %get-tuple-element.84), channel_id=1, source_target_pairs={{0,6},{2,4},{4,2},{6,0},{1,7},{3,5},{5,3},{7,1},{8,14},{10,12},{12... | collective-permute-start | bytes 983048 | tf_op jit(solution)/shard_map/ppermute | solution.py:35
  141.0 14.8 %collective-permute-start.9 = (bf16[160,1024]{1,0:T(8,128)(2,1)}, bf16[160,1024]{1,0:T(8,128)(2,1)S(1)}, u32[]{:S(2)}, u32[]{:S(2)}) collective-permute-start(bf16[160,1024]{1,0:T(8,128)(2,1)} %get-tuple-element.83), channel_id=1, source_target_pairs={{0,4},{2,6},{4,0},{6,2},{1,5},{3,7},{5,1},{7,3},{8,12},{10,14},{12... | collective-permute-start | bytes 983048 | tf_op jit(solution)/shard_map/ppermute | solution.py:35
  141.8 14.0 %collective-permute-start.8 = (bf16[160,1024]{1,0:T(8,128)(2,1)}, bf16[160,1024]{1,0:T(8,128)(2,1)}, u32[]{:S(2)}, u32[]{:S(2)}) collective-permute-start(bf16[160,1024]{1,0:T(8,128)(2,1)} %get-tuple-element.82), channel_id=1, source_target_pairs={{0,2},{2,0},{4,6},{6,4},{1,3},{3,1},{5,7},{7,5},{8,10},{10,8},{12,... | collective-permute-start | bytes 983048 | tf_op jit(solution)/shard_map/ppermute | solution.py:35
  166.0 16.6 %all-to-all-start.3 = ((bf16[8,160,128]{2,1,0:T(8,128)(2,1)}), bf16[8,160,128]{2,1,0:T(8,128)(2,1)S(1)}, u32[]{:S(2)}, u32[]{:S(2)}) async-start(bf16[8,160,128]{2,1,0:T(8,128)(2,1)} %bitcast_bitcast_fusion), calls=%async_computation.3 | async-start | bytes 655360 | tf_op jit(solution)/shard_map/all_to_all | solution.py:468
  182.6 20.8 %collective-permute-start.11 = (bf16[160,1024]{1,0:T(8,128)(2,1)}, bf16[160,1024]{1,0:T(8,128)(2,1)S(1)}, u32[]{:S(2)}, u32[]{:S(2)}) collective-permute-start(bf16[160,1024]{1,0:T(8,128)(2,1)} %get-tuple-element.86), channel_id=1, source_target_pairs={{0,2},{2,0},{4,6},{6,4},{1,3},{3,1},{5,7},{7,5},{8,10},{10,8},{12,... | collective-permute-start | bytes 983048 | tf_op jit(solution)/shard_map/ppermute | solution.py:35
  182.6 20.8 %collective-permute-start.12 = (bf16[160,1024]{1,0:T(8,128)(2,1)}, bf16[160,1024]{1,0:T(8,128)(2,1)S(1)}, u32[]{:S(2)}, u32[]{:S(2)}) collective-permute-start(bf16[160,1024]{1,0:T(8,128)(2,1)} %get-tuple-element.87), channel_id=1, source_target_pairs={{0,4},{2,6},{4,0},{6,2},{1,5},{3,7},{5,1},{7,3},{8,12},{10,14},{12... | collective-permute-start | bytes 983048 | tf_op jit(solution)/shard_map/ppermute | solution.py:35
  186.1 17.2 %collective-permute-start.13 = (bf16[160,1024]{1,0:T(8,128)(2,1)S(1)}, bf16[160,1024]{1,0:T(8,128)(2,1)S(1)}, u32[]{:S(2)}, u32[]{:S(2)}) collective-permute-start(bf16[160,1024]{1,0:T(8,128)(2,1)S(1)} %copy-done.20), channel_id=1, source_target_pairs={{0,6},{2,4},{4,2},{6,0},{1,7},{3,5},{5,3},{7,1},{8,14},{10,12},{12... | collective-permute-start | bytes 983048 | tf_op jit(solution)/shard_map/ppermute | solution.py:35
  203.4 14.7 %collective-permute-start.14 = (bf16[160,1024]{1,0:T(8,128)(2,1)}, bf16[160,1024]{1,0:T(8,128)(2,1)S(1)}, u32[]{:S(2)}, u32[]{:S(2)}) collective-permute-start(bf16[160,1024]{1,0:T(8,128)(2,1)} %get-tuple-element.107), channel_id=1, source_target_pairs={{0,1},{1,0},{2,3},{3,2},{4,5},{5,4},{6,7},{7,6},{8,9},{9,8},{10,11... | collective-permute-start | bytes 983048 | tf_op jit(solution)/shard_map/ppermute | solution.py:35
  204.7 14.7 %collective-permute-start.15 = (bf16[160,1024]{1,0:T(8,128)(2,1)}, bf16[160,1024]{1,0:T(8,128)(2,1)S(1)}, u32[]{:S(2)}, u32[]{:S(2)}) collective-permute-start(bf16[160,1024]{1,0:T(8,128)(2,1)} %get-tuple-element.108), channel_id=1, source_target_pairs={{0,2},{1,3},{2,0},{3,1},{4,6},{5,7},{6,4},{7,5},{8,10},{9,11},{10,... | collective-permute-start | bytes 983048 | tf_op jit(solution)/shard_map/ppermute | solution.py:35
  210.2 23.2 %collective-permute-start.16 = (bf16[160,1024]{1,0:T(8,128)(2,1)}, bf16[160,1024]{1,0:T(8,128)(2,1)}, u32[]{:S(2)}, u32[]{:S(2)}) collective-permute-start(bf16[160,1024]{1,0:T(8,128)(2,1)} %get-tuple-element.109), channel_id=1, source_target_pairs={{0,3},{1,2},{2,1},{3,0},{4,7},{5,6},{6,5},{7,4},{8,11},{9,10},{10,... | collective-permute-start | bytes 983048 | tf_op jit(solution)/shard_map/ppermute | solution.py:35
  214.0 19.4 %collective-permute-start.17 = (bf16[160,1024]{1,0:T(8,128)(2,1)}, bf16[160,1024]{1,0:T(8,128)(2,1)}, u32[]{:S(2)}, u32[]{:S(2)}) collective-permute-start(bf16[160,1024]{1,0:T(8,128)(2,1)} %get-tuple-element.110), channel_id=1, source_target_pairs={{0,4},{1,5},{2,6},{3,7},{4,0},{5,1},{6,2},{7,3},{8,12},{9,13},{10,... | collective-permute-start | bytes 983048 | tf_op jit(solution)/shard_map/ppermute | solution.py:35
  215.5 17.9 %collective-permute-start.18 = (bf16[160,1024]{1,0:T(8,128)(2,1)}, bf16[160,1024]{1,0:T(8,128)(2,1)}, u32[]{:S(2)}, u32[]{:S(2)}) collective-permute-start(bf16[160,1024]{1,0:T(8,128)(2,1)} %get-tuple-element.111), channel_id=1, source_target_pairs={{0,5},{1,4},{2,7},{3,6},{4,1},{5,0},{6,3},{7,2},{8,13},{9,12},{10,... | collective-permute-start | bytes 983048 | tf_op jit(solution)/shard_map/ppermute | solution.py:35
  218.1 15.6 %collective-permute-start.19 = (bf16[160,1024]{1,0:T(8,128)(2,1)}, bf16[160,1024]{1,0:T(8,128)(2,1)}, u32[]{:S(2)}, u32[]{:S(2)}) collective-permute-start(bf16[160,1024]{1,0:T(8,128)(2,1)} %get-tuple-element.112), channel_id=1, source_target_pairs={{0,6},{1,7},{2,4},{3,5},{4,2},{5,3},{6,0},{7,1},{8,14},{9,15},{10,... | collective-permute-start | bytes 983048 | tf_op jit(solution)/shard_map/ppermute | solution.py:35
  219.3 18.6 %collective-permute-start.20 = (bf16[160,1024]{1,0:T(8,128)(2,1)}, bf16[160,1024]{1,0:T(8,128)(2,1)}, u32[]{:S(2)}, u32[]{:S(2)}) collective-permute-start(bf16[160,1024]{1,0:T(8,128)(2,1)} %get-tuple-element.113), channel_id=1, source_target_pairs={{0,7},{1,6},{2,5},{3,4},{4,3},{5,2},{6,1},{7,0},{8,15},{9,14},{10,... | collective-permute-start | bytes 983048 | tf_op jit(solution)/shard_map/ppermute | solution.py:35
  225.4 22.5 %all-to-all-start.4 = ((bf16[16,80,384]{2,1,0:T(8,128)(2,1)}), bf16[16,80,384]{2,1,0:T(8,128)(2,1)S(1)}, u32[]{:S(2)}, u32[]{:S(2)}) async-start(bf16[16,80,384]{2,1,0:T(8,128)(2,1)} %pad_maximum_fusion), calls=%async_computation.4 | async-start | bytes 1966080 | tf_op jit(solution)/shard_map/all_to_all | solution.py:484
  250.4 19.7 %collective-permute-start.21 = (bf16[9,64,384]{2,1,0:T(8,128)(2,1)S(1)}, bf16[9,64,384]{2,1,0:T(8,128)(2,1)S(1)}, u32[]{:S(2)}, u32[]{:S(2)}) collective-permute-start(bf16[9,64,384]{2,1,0:T(8,128)(2,1)S(1)} %dynamic-slice_bitcast_fusion), channel_id=1, source_target_pairs={{0,16},{16,0},{1,17},{17,1},{2,18},{18,2},{3,19},{19,3},{4,20},{20... | collective-permute-start | bytes 1327112 | tf_op jit(solution)/shard_map/ppermute | solution.py:35
  253.0 16.3 %all-to-all-start.5 = ((f32[128,1,128]{2,1,0:T(1,128)}), f32[128,1,128]{2,1,0:T(1,128)}, u32[]{:S(2)}, u32[]{:S(2)}) async-start(f32[128,1,128]{2,1,0:T(1,128)} %broadcast_in_dim.17), calls=%async_computation.5 | async-start | bytes 131072 | tf_op jit(solution)/shard_map/all_to_all | solution.py:502
  270.4 14.9 %collective-permute-start.22 = (bf16[3,64,384]{2,1,0:T(8,128)(2,1)S(1)}, bf16[3,64,384]{2,1,0:T(8,128)(2,1)S(1)}, u32[]{:S(2)}, u32[]{:S(2)}) collective-permute-start(bf16[3,64,384]{2,1,0:T(8,128)(2,1)S(1)} %get-tuple-element.172), channel_id=1, source_target_pairs={{0,1},{1,0},{2,3},{3,2},{4,5},{5,4},{6,7},{7,6},{8,9},{9,8},{10,11... | collective-permute-start | bytes 442376 | tf_op jit(solution)/shard_map/ppermute | solution.py:35
  272.7 11.9 %all-to-all-start.6 = ((bf16[8,64,128]{2,1,0:T(8,128)(2,1)}), bf16[8,64,128]{2,1,0:T(8,128)(2,1)S(1)}, u32[]{:S(2)}, u32[]{:S(2)}) async-start(bf16[8,64,128]{2,1,0:T(8,128)(2,1)} %bitcast_bitcast_fusion.1), calls=%async_computation.7 | async-start | bytes 262144 | tf_op jit(solution)/shard_map/all_to_all | solution.py:503
  (25 other events, 688.1 us)
Sparse Core Ops, SparseCore 0:
  25.4 36.3 all-gather.4
  63.5 37.9 all-gather.6
  162.2 49.2 reduce-scatter.1

commit v4 on v3

--- a/solution.py
+++ b/solution.py
@@ -18,6 +18,7 @@
 FFB = 328
 PAD = 384
 QB = 256
+BACK_QB = 320
 VMEM = 60 * 1024 * 1024
 
 AXES = ("x", "zl", "c", "yh", "yl", "zh")
@@ -74,6 +75,14 @@
     return (
         jnp.asarray(np.concatenate([cosine] * 4, axis=1), F32),
         jnp.asarray(np.concatenate([-sine, sine, -sine, sine], axis=1), F32),
+    )
+
+
+def by_head(values):
+    lane = lax.broadcasted_iota(jnp.int32, values.shape, 1)
+    zeros = jnp.zeros_like(values)
+    return jnp.concatenate(
+        [jnp.where(lane < HD, values, zeros), jnp.where(lane < HD, zeros, values)], axis=0
     )
 
 
@@ -158,28 +167,26 @@
     val_sum[...] = jnp.zeros_like(val_sum)
 
     def block(i, carry):
-        at = pl.ds(pl.multiple_of(i * QB, QB), QB)
-        query = q_ref[at, :]
-        grad = g_ref[at, :]
-        grad_query = jnp.zeros((QB, 2 * HD), F32)
-        for head in range(2):
-            query_h = head_mask(query, head)
-            grad_h = head_mask(grad, head)
-            scores = dot(query_h, k_ref[...], 1, 1)
-            probs = jnp.exp(scores - lse_ref[at, head * HD : head * HD + 1])
-            grad_probs = dot(grad_h, v_ref[...], 1, 1)
-            inner = jnp.sum(grad_probs * probs, axis=1, keepdims=True)
-            grad_scores = (probs * (grad_probs - inner)).astype(BF16)
-            grad_query = grad_query + dot(grad_scores, head_mask(k_ref[...], head), 1, 0)
-            key_sum[...] += dot(query_h, grad_scores, 0, 0)
-            val_sum[...] += dot(grad_h, probs.astype(BF16), 0, 0)
+        at = pl.ds(pl.multiple_of(i * BACK_QB, BACK_QB), BACK_QB)
+        query = by_head(q_ref[at, :])
+        grad = by_head(g_ref[at, :])
+        logs = jnp.concatenate([lse_ref[at, :1], lse_ref[at, HD : HD + 1]], axis=0)
+        probs = jnp.exp(dot(query, k_ref[...], 1, 1) - logs)
+        grad_probs = dot(grad, v_ref[...], 1, 1)
+        inner = jnp.sum(grad_probs * probs, axis=1, keepdims=True)
+        grad_scores = (probs * (grad_probs - inner)).astype(BF16)
+        both = dot(grad_scores, k_ref[...], 1, 0)
+        lane = lax.broadcasted_iota(jnp.int32, (BACK_QB, 2 * HD), 1)
+        grad_query = jnp.where(lane < HD, both[:BACK_QB], both[BACK_QB:])
+        key_sum[...] += dot(query, grad_scores, 0, 0)
+        val_sum[...] += dot(grad, probs.astype(BF16), 0, 0)
         grad_query = grad_query * 0.125
         cosine, sine = cos_ref[at, :], sin_ref[at, :]
         grad_query = grad_query * cosine - swap_halves(grad_query) * sine
         out_ref[at, : 2 * HD] = grad_query.astype(BF16)
         return carry
 
-    lax.fori_loop(0, LEN // QB, block, 0)
+    lax.fori_loop(0, LEN // BACK_QB, block, 0)
     grad_key = key_sum[...].T
     grad_key = grad_key * cos_ref[...] - swap_halves(grad_key) * sin_ref[...]
     out_ref[:, 2 * HD : 4 * HD] = grad_key.astype(BF16)
@@ -406,22 +413,25 @@
 
 
 def on_device(tokens, gain_attn, w_qkv, w_out, gain_mlp, w_in, w_down, cotangent):
+    partner_tokens = exchange(tokens, PRE_AX, PRE, 1)
+    w_out_later, partner_tokens = lax.optimization_barrier((w_out, partner_tokens))
     own_mlp = jnp.concatenate([w_in, w_down[:, None, :]], axis=1).transpose(1, 0, 2)
     own_mlp = jnp.pad(own_mlp, ((0, 0), (0, 0), (0, PAD - FFB)))
     own_qkv = w_qkv.reshape(64, PAD)
-    out_wide = lax.all_to_all(jnp.broadcast_to(w_out[None], (8, 64, 2 * HD)), TP, 0, 0)
+    out_wide = lax.all_to_all(jnp.broadcast_to(w_out_later[None], (8, 64, 2 * HD)), TP, 0, 0)
     out_wide = out_wide.transpose(1, 0, 2).reshape(64, WIDTH)
     out_wide = jnp.concatenate([out_wide, jnp.zeros((64, 2 * HD), BF16), own_qkv], axis=1)
     out_wide = out_wide.reshape(64, 4, PAD).transpose(1, 0, 2)
     weights = lax.all_gather(out_wide, FS, axis=0)
+    own_mlp, out_wide = lax.optimization_barrier((own_mlp, out_wide))
     partner_mlp = exchange(own_mlp, PRE_AX, PRE, 1)
-    weights_mlp = lax.all_gather(jnp.concatenate([own_mlp, partner_mlp], axis=0), FS, axis=0)
     cosine, sine = rope_tables()
 
     resid = tokens.astype(F32)
     hat_attn, scale_attn = normalize(resid)
     normed_attn = (hat_attn * gain_attn).astype(BF16)
-    partner_rows = exchange(normed_attn, PRE_AX, PRE, 1)
+    partner_rows = normalize(partner_tokens.astype(F32))[0] * gain_attn
+    partner_rows = partner_rows.astype(BF16)
     first = lax.axis_index("zh") == 0
     pair = jnp.stack(
         [
@@ -431,6 +441,8 @@
     )
     rows = lax.all_to_all(jnp.broadcast_to(pair[None], (M, PRE, ROWS, WIDTH)), MLP_AX, 0, 0)
     rows = rows.reshape(8, ROWS, WIDTH)
+    partner_mlp, rows = lax.optimization_barrier((partner_mlp, rows))
+    weights_mlp = lax.all_gather(jnp.concatenate([own_mlp, partner_mlp], axis=0), FS, axis=0)
 
     cotangent_later, rows = lax.optimization_barrier((cotangent, rows))
     back_blocks = gather_by_mask(cotangent_later, MLP_AX, M)

time: 294 us -> 292 us (level)
  blocking collectives: 33.3 us -> 0 us
  waiting for transfers between devices: 73.4 us -> 97.6 us
  starting transfers between devices: 70.8 us -> 76.7 us
    all_to_all x1 -> x0, blocking collectives: 33.3 us -> none  [on_device(): lax.all_to_all(jnp.broadcast_to(pair[None], (M, PRE, ROWS, WIDTH)), MLP_A...]
    all_to_all x1 -> x2, waiting for transfers between devices: 7.82 us -> 28.9 us  [the longest x1 21 us: on_device(): lax.all_to_all(jnp.broadcast_to(pair[None], (M, PRE, ROWS, WIDTH)), MLP_A...]
    ppermute x23, waiting for transfers between devices: 26.9 us -> 40 us  [exchange(): return lax.ppermute(value, axes, [(i, i ^ mask) for i in range(count)])]
    all_to_all x1, waiting for transfers between devices: 6.76 us -> 0.01 us  [on_device(): got = lax.all_to_all(jnp.concatenate([qkv_part, extra], axis=1), FS, 0, 0)]
    all_to_all x1, waiting for transfers between devices: 11.7 us -> 8.62 us  [on_device(): gm_own = lax.all_to_all(gm_parts, TP, 0, 0).reshape(LEN, 2 * HD)]
    all_to_all x1 -> x2, starting transfers between devices: 7.87 us -> 11 us  [the longest x1 7.15 us: on_device(): lax.all_to_all(jnp.broadcast_to(w_out_later[None], (8, 64, 2 * HD)), TP,...]
  transfers between devices with their start and end apart: 32 -> 33, of which waited for: 11 -> 13; matrix products, arithmetic and copies ran while one was open for 9% -> 10% of each run, Pallas kernels for 18% -> 18%
where the time goes in v4:
time: 292 us; the launch traced here: 291 us
  waiting for transfers between devices  97.6 us (33%)
  starting transfers between devices  76.7 us (26%)
  Pallas kernels  63 us (22%)
  other arithmetic  21.6 us (7%)
  local copies, waits for them, and re-layouts  14.7 us (5%)
  between operations  14.3 us (5%)
  matrix products  3.46 us (1%)
    ppermute x23, starting transfers between devices, exchange(): return lax.ppermute(value, axes, [(i, i ^ mask) for i in range(count)])  40.2 us
    ppermute x23, waiting for transfers between devices, exchange(): return lax.ppermute(value, axes, [(i, i ^ mask) for i in range(count)])  40 us
    all_to_all x1, waiting for transfers between devices, on_device(): lax.all_to_all(jnp.broadcast_to(pair[None], (M, PRE, ROWS, WIDTH)), MLP_A...  21 us
    pallas_call x1, Pallas kernels, attend_back(): pl.pallas_call(attend_back_kernel, grid=(1,), in_specs=[pl.BlockSpec(memo...  14.9 us
    pallas_call x2, Pallas kernels, mlp(): pl.pallas_call(functools.partial(mlp_kernel, count), grid=(1,), in_specs=...  14.8 us
    pallas_call x1, Pallas kernels, mlp_grads(): pl.pallas_call(mlp_grads_kernel, grid=(PRE,), in_specs=[whole(ROWS, WIDTH...  12.4 us
    pallas_call x1, Pallas kernels, attend(): pl.pallas_call(attend_kernel, grid=(1,), in_specs=[ROWS_SPEC, QKV_SPEC, w...  12 us
    all_to_all x1, waiting for transfers between devices, on_device(): gm_own = lax.all_to_all(gm_parts, TP, 0, 0).reshape(LEN, 2 * HD)  8.62 us
  transfers between devices with their start and end apart: 33, of which 13 were waited for; matrix products, arithmetic and copies ran while one was open for 10% of the time, Pallas kernels for 18%

profile of v4, /device:TPU:0, one launch (start us, length us, event | category | flops | bytes accessed | tf_op | source)
XLA Modules:
  0.0 291.2 jit_solution(9599819840162621818)
XLA Ops:
  7.2 4.0 %collective-permute-start = (bf16[160,1024]{1,0:T(8,128)(2,1)}, bf16[160,1024]{1,0:T(8,128)(2,1)S(1)}, u32[]{:S(2)}, u32[]{:S(2)}) collective-permute-start(bf16[160,1024]{1,0:T(8,128)(2,1)} %param.10), channel_id=1, source_target_pairs={{0,1},{1,0},{2,3},{3,2},{4,5},{5,4},{6,7},{7,6},{8,9},{9,8},{10,11... | collective-permute-start | bytes 983048 | tf_op jit(solution)/shard_map/ppermute | solution.py:36
  11.3 7.9 %collective-permute-done = bf16[160,1024]{1,0:T(8,128)(2,1)S(1)} collective-permute-done((bf16[160,1024]{1,0:T(8,128)(2,1)}, bf16[160,1024]{1,0:T(8,128)(2,1)S(1)}, u32[]{:S(2)}, u32[]{:S(2)}) %collective-permute-start) | collective-permute-done | bytes 327712 | tf_op jit(solution)/shard_map/ppermute | solution.py:36
  20.6 7.1 %all-to-all-start = ((bf16[8,64,128]{2,1,0:T(8,128)(2,1)}), bf16[8,64,128]{2,1,0:T(8,128)(2,1)S(1)}, u32[]{:S(2)}, u32[]{:S(2)}) async-start(bf16[8,64,128]{2,1,0:T(8,128)(2,1)} %broadcast_in_dim.13), calls=%async_computation | async-start | bytes 262144 | tf_op jit(solution)/shard_map/all_to_all | solution.py:421
  27.8 7.8 %all-to-all-done = bf16[8,64,128]{2,1,0:T(8,128)(2,1)S(1)} async-done(((bf16[8,64,128]{2,1,0:T(8,128)(2,1)}), bf16[8,64,128]{2,1,0:T(8,128)(2,1)S(1)}, u32[]{:S(2)}, u32[]{:S(2)}) %all-to-all-start) | async-done | bytes 131104 | tf_op jit(solution)/shard_map/all_to_all | solution.py:421
  40.5 3.8 %all-to-all-start.1 = ((bf16[4,2,160,1024]{3,2,1,0:T(8,128)(2,1)}), bf16[4,2,160,1024]{3,2,1,0:T(8,128)(2,1)S(1)}, u32[]{:S(2)}, u32[]{:S(2)}) async-start(bf16[4,2,160,1024]{3,2,1,0:T(8,128)(2,1)} %broadcast_in_dim.15), calls=%async_computation.1 | async-start | bytes 5242880 | tf_op jit(solution)/shard_map/all_to_all | solution.py:442
  45.5 7.7 %collective-permute-done.1 = bf16[3,64,384]{2,1,0:T(8,128)(2,1)} collective-permute-done((bf16[3,64,384]{2,1,0:T(8,128)(2,1)S(1)}, bf16[3,64,384]{2,1,0:T(8,128)(2,1)}, u32[]{:S(2)}, u32[]{:S(2)}) %collective-permute-start.1) | collective-permute-done | bytes 147488 | tf_op jit(solution)/shard_map/ppermute | solution.py:36
  53.2 21.0 %all-to-all-done.1 = bf16[4,2,160,1024]{3,2,1,0:T(8,128)(2,1)S(1)} async-done(((bf16[4,2,160,1024]{3,2,1,0:T(8,128)(2,1)}), bf16[4,2,160,1024]{3,2,1,0:T(8,128)(2,1)S(1)}, u32[]{:S(2)}, u32[]{:S(2)}) %all-to-all-start.1) | async-done | bytes 2621472 | tf_op jit(solution)/shard_map/all_to_all | solution.py:442
  80.9 12.0 %attend.1 = (bf16[1280,128]{1,0:T(8,128)(2,1)}, bf16[1280,128]{1,0:T(8,128)(2,1)}, bf16[1280,128]{1,0:T(8,128)(2,1)}, bf16[1280,128]{1,0:T(8,128)(2,1)}, f32[1280,128]{1,0:T(8,128)}) custom-call(bf16[8,160,1024]{2,1,0:T(8,128)(2,1)} %bitcast.91, bf16[16,4,64,384]{3,2,1,0:T(8,128)(2,1)} %bitcast.93, f32[1280,128]{1,0:T(8,128)} %constant.67.clone.cos_ref.refs_5_, ...), custom_call_target="tpu_custom_call" | custom-call | flops 6000000000 | bytes 8000000 | tf_op jit(solution)/shard_map/attend/pallas_call | solution.py:147
  92.9 3.6 %all-to-all-start.2 = ((bf16[8,160,128]{2,1,0:T(8,128)(2,1)}), bf16[8,160,128]{2,1,0:T(8,128)(2,1)S(1)}, u32[]{:S(2)}, u32[]{:S(2)}) async-start(bf16[8,160,128]{2,1,0:T(8,128)(2,1)} %bitcast.99), calls=%async_computation.2 | async-start | bytes 655360 | tf_op jit(solution)/shard_map/all_to_all | solution.py:451
  98.5 6.8 %all-to-all-done.2 = bf16[8,160,128]{2,1,0:T(8,128)(2,1)S(1)} async-done(((bf16[8,160,128]{2,1,0:T(8,128)(2,1)}), bf16[8,160,128]{2,1,0:T(8,128)(2,1)S(1)}, u32[]{:S(2)}, u32[]{:S(2)}) %all-to-all-start.2) | async-done | bytes 327712 | tf_op jit(solution)/shard_map/all_to_all | solution.py:451
  107.8 2.7 collective-permute-start.6
  112.7 3.9 %collective-permute-done.5.refs_1_ = bf16[160,1024]{1,0:T(8,128)(2,1)S(1)} collective-permute-done((bf16[160,1024]{1,0:T(8,128)(2,1)S(1)}, bf16[160,1024]{1,0:T(8,128)(2,1)S(1)}, u32[]{:S(2)}, u32[]{:S(2)}) %collective-permute-start.5) | collective-permute-done | bytes 327712 | tf_op jit(solution)/shard_map/ppermute | solution.py:36
  117.4 7.4 %mlp.2 = (bf16[2,320,384]{2,1,0:T(8,128)(2,1)}, bf16[2,2,320,384]{3,2,1,0:T(8,128)(2,1)}, bf16[160,1024]{1,0:T(8,128)(2,1)}, bf16[160,1024]{1,0:T(8,128)(2,1)}) custom-call(bf16[160,1024]{1,0:T(8,128)(2,1)} %copy-done.14, bf16[160,1024]{1,0:T(8,128)(2,1)} %copy-done.21, bf16[160,1024]{1,0:T(8,128)(2,1)} %refs_4_, ...), custom_call_target="tpu_custom_call" | custom-call | flops 5000000000 | bytes 8000000 | tf_op jit(solution)/shard_map/mlp/pallas_call | solution.py:304
  124.8 7.4 %mlp.3 = (bf16[2,320,384]{2,1,0:T(8,128)(2,1)}, bf16[2,2,320,384]{3,2,1,0:T(8,128)(2,1)}, bf16[160,1024]{1,0:T(8,128)(2,1)}, bf16[160,1024]{1,0:T(8,128)(2,1)}) custom-call(bf16[160,1024]{1,0:T(8,128)(2,1)} %collective-permute-done.6.refs_0_.refs_2_, bf16[160,1024]{1,0:T(8,128)(2,1)} %collective-permute-done.7.refs_1_.refs_3_, ...), custom_call_target="tpu_custom_call" | custom-call | flops 5000000000 | bytes 8000000 | tf_op jit(solution)/shard_map/mlp/pallas_call | solution.py:304
  136.3 12.4 %mlp_grads.1 = (bf16[8,2,9,64,384]{4,3,2,1,0:T(8,128)(2,1)}, bf16[160,1024]{1,0:T(8,128)(2,1)}, bf16[160,1024]{1,0:T(8,128)(2,1)}, bf16[160,1024]{1,0:T(8,128)(2,1)}, bf16[160,1024]{1,0:T(8,128)(2,1)}) custom-call(bf16[160,1024]{1,0:T(8,128)(2,1)} %copy-done.14, bf16[160,1024]{1,0:T(8,128)(2,1)} %copy-done.21, ...), custom_call_target="tpu_custom_call" | custom-call | flops 8000000000 | bytes 12000000 | tf_op jit(solution)/shard_map/mlp_grads/pallas_call | solution.py:362
  151.5 3.6 %out_grads.1 = bf16[8,2,9,64,384]{4,3,2,1,0:T(8,128)(2,1)} custom-call(bf16[160,1024]{1,0:T(8,128)(2,1)} %get-tuple-element.174.g_ref, bf16[160,1152]{1,0:T(8,128)(2,1)} %pad.13.mixed_ref, bf16[8,2,9,64,384]{4,3,2,1,0:T(8,128)(2,1)} %get-tuple-element.125.held_ref), custom_call_target="tpu_custom_call", output_to_operand_aliasing={{}: (2, {})} | custom-call | flops 400000000 | bytes 4000000 | tf_op jit(solution)/shard_map/out_grads/pallas_call | solution.py:395
  159.0 6.9 %all-to-all-start.3 = ((bf16[8,160,128]{2,1,0:T(8,128)(2,1)}), bf16[8,160,128]{2,1,0:T(8,128)(2,1)S(1)}, u32[]{:S(2)}, u32[]{:S(2)}) async-start(bf16[8,160,128]{2,1,0:T(8,128)(2,1)} %bitcast_bitcast_fusion), calls=%async_computation.3 | async-start | bytes 655360 | tf_op jit(solution)/shard_map/all_to_all | solution.py:480
  166.0 8.6 %all-to-all-done.3 = bf16[8,160,128]{2,1,0:T(8,128)(2,1)S(1)} async-done(((bf16[8,160,128]{2,1,0:T(8,128)(2,1)}), bf16[8,160,128]{2,1,0:T(8,128)(2,1)S(1)}, u32[]{:S(2)}, u32[]{:S(2)}) %all-to-all-start.3) | async-done | bytes 327712 | tf_op jit(solution)/shard_map/all_to_all | solution.py:480
  175.1 2.4 collective-permute-start.12
  179.3 14.9 %attend_back.1 = (bf16[1280,384]{1,0:T(8,128)(2,1)}, bf16[160,1024]{1,0:T(8,128)(2,1)}, bf16[160,1024]{1,0:T(8,128)(2,1)}, bf16[160,1024]{1,0:T(8,128)(2,1)}, bf...) custom-call(s32[1]{0:T(128)} %bitcast.16.me_ref, ...), custom_call_target="tpu_custom_call" | custom-call | flops 12000000000 | bytes 8000000 | tf_op jit(solution)/shard_map/attend_back/pallas_call | solution.py:202
  195.9 5.3 %qkv_grads.1 = bf16[16,64,384]{2,1,0:T(8,128)(2,1)} custom-call(bf16[8,160,1024]{2,1,0:T(8,128)(2,1)} %bitcast.92, bf16[1280,384]{1,0:T(8,128)(2,1)} %get-tuple-element.124.g_ref), custom_call_target="tpu_custom_call" | custom-call | flops 2000000000 | bytes 5000000 | tf_op jit(solution)/shard_map/qkv_grads/pallas_call | solution.py:231
  201.2 3.7 %collective-permute-start.16 = (bf16[160,1024]{1,0:T(8,128)(2,1)}, bf16[160,1024]{1,0:T(8,128)(2,1)}, u32[]{:S(2)}, u32[]{:S(2)}) collective-permute-start(bf16[160,1024]{1,0:T(8,128)(2,1)} %get-tuple-element.119), channel_id=1, source_target_pairs={{0,3},{1,2},{2,1},{3,0},{4,7},{5,6},{6,5},{7,4},{8,11},{9,10},{10,... | collective-permute-start | bytes 983048 | tf_op jit(solution)/shard_map/ppermute | solution.py:36
  205.9 3.3 %collective-permute-start.18 = (bf16[160,1024]{1,0:T(8,128)(2,1)}, bf16[160,1024]{1,0:T(8,128)(2,1)}, u32[]{:S(2)}, u32[]{:S(2)}) collective-permute-start(bf16[160,1024]{1,0:T(8,128)(2,1)} %get-tuple-element.121), channel_id=1, source_target_pairs={{0,5},{1,4},{2,7},{3,6},{4,1},{5,0},{6,3},{7,2},{8,13},{9,12},{10,... | collective-permute-start | bytes 983048 | tf_op jit(solution)/shard_map/ppermute | solution.py:36
  210.4 3.7 %collective-permute-start.20 = (bf16[160,1024]{1,0:T(8,128)(2,1)}, bf16[160,1024]{1,0:T(8,128)(2,1)}, u32[]{:S(2)}, u32[]{:S(2)}) collective-permute-start(bf16[160,1024]{1,0:T(8,128)(2,1)} %get-tuple-element.123), channel_id=1, source_target_pairs={{0,7},{1,6},{2,5},{3,4},{4,3},{5,2},{6,1},{7,0},{8,15},{9,14},{10,... | collective-permute-start | bytes 983048 | tf_op jit(solution)/shard_map/ppermute | solution.py:36
  216.4 3.8 %all-to-all-start.4 = ((bf16[16,80,384]{2,1,0:T(8,128)(2,1)}), bf16[16,80,384]{2,1,0:T(8,128)(2,1)S(1)}, u32[]{:S(2)}, u32[]{:S(2)}) async-start(bf16[16,80,384]{2,1,0:T(8,128)(2,1)} %pad_maximum_fusion), calls=%async_computation.4 | async-start | bytes 1966080 | tf_op jit(solution)/shard_map/all_to_all | solution.py:496
  222.1 5.0 %collective-permute-done.18 = bf16[160,1024]{1,0:T(8,128)(2,1)} collective-permute-done((bf16[160,1024]{1,0:T(8,128)(2,1)}, bf16[160,1024]{1,0:T(8,128)(2,1)}, u32[]{:S(2)}, u32[]{:S(2)}) %collective-permute-start.18) | collective-permute-done | bytes 327712 | tf_op jit(solution)/shard_map/ppermute | solution.py:36
  227.1 4.6 %collective-permute-done.19 = bf16[160,1024]{1,0:T(8,128)(2,1)} collective-permute-done((bf16[160,1024]{1,0:T(8,128)(2,1)}, bf16[160,1024]{1,0:T(8,128)(2,1)}, u32[]{:S(2)}, u32[]{:S(2)}) %collective-permute-start.19) | collective-permute-done | bytes 327712 | tf_op jit(solution)/shard_map/ppermute | solution.py:36
  231.7 10.8 %collective-permute-done.20 = bf16[160,1024]{1,0:T(8,128)(2,1)} collective-permute-done((bf16[160,1024]{1,0:T(8,128)(2,1)}, bf16[160,1024]{1,0:T(8,128)(2,1)}, u32[]{:S(2)}, u32[]{:S(2)}) %collective-permute-start.20) | collective-permute-done | bytes 327712 | tf_op jit(solution)/shard_map/ppermute | solution.py:36
  250.8 7.1 %all-to-all-start.5 = ((f32[128,1,128]{2,1,0:T(1,128)}), f32[128,1,128]{2,1,0:T(1,128)}, u32[]{:S(2)}, u32[]{:S(2)}) async-start(f32[128,1,128]{2,1,0:T(1,128)} %broadcast_in_dim.17), calls=%async_computation.5 | async-start | bytes 131072 | tf_op jit(solution)/shard_map/all_to_all | solution.py:514
  260.3 6.7 %all-to-all-done.5 = f32[128,1,128]{2,1,0:T(1,128)} async-done(((f32[128,1,128]{2,1,0:T(1,128)}), f32[128,1,128]{2,1,0:T(1,128)}, u32[]{:S(2)}, u32[]{:S(2)}) %all-to-all-start.5) | async-done | bytes 65568 | tf_op jit(solution)/shard_map/all_to_all | solution.py:514
  270.5 4.1 %all-to-all-start.6 = ((bf16[8,64,128]{2,1,0:T(8,128)(2,1)}), bf16[8,64,128]{2,1,0:T(8,128)(2,1)S(1)}, u32[]{:S(2)}, u32[]{:S(2)}) async-start(bf16[8,64,128]{2,1,0:T(8,128)(2,1)} %bitcast_bitcast_fusion.1), calls=%async_computation.7 | async-start | bytes 262144 | tf_op jit(solution)/shard_map/all_to_all | solution.py:515
  276.0 6.5 %all-to-all-done.6 = bf16[8,64,128]{2,1,0:T(8,128)(2,1)S(1)} async-done(((bf16[8,64,128]{2,1,0:T(8,128)(2,1)}), bf16[8,64,128]{2,1,0:T(8,128)(2,1)S(1)}, u32[]{:S(2)}, u32[]{:S(2)}) %all-to-all-start.6) | async-done | bytes 131104 | tf_op jit(solution)/shard_map/all_to_all | solution.py:515
  (158 shorter events, 60.3 us)
Async XLA Ops:
  7.2 12.0 %collective-permute-start = (bf16[160,1024]{1,0:T(8,128)(2,1)}, bf16[160,1024]{1,0:T(8,128)(2,1)S(1)}, u32[]{:S(2)}, u32[]{:S(2)}) collective-permute-start(bf16[160,1024]{1,0:T(8,128)(2,1)} %param.10), channel_id=1, source_target_pairs={{0,1},{1,0},{2,3},{3,2},{4,5},{5,4},{6,7},{7,6},{8,9},{9,8},{10,11... | collective-permute-start | bytes 983048 | tf_op jit(solution)/shard_map/ppermute | solution.py:36
  20.6 15.1 %all-to-all-start = ((bf16[8,64,128]{2,1,0:T(8,128)(2,1)}), bf16[8,64,128]{2,1,0:T(8,128)(2,1)S(1)}, u32[]{:S(2)}, u32[]{:S(2)}) async-start(bf16[8,64,128]{2,1,0:T(8,128)(2,1)} %broadcast_in_dim.13), calls=%async_computation | async-start | bytes 262144 | tf_op jit(solution)/shard_map/all_to_all | solution.py:421
  27.7 53.2 %all-gather.5.cloned.1.call-start = ((), (), s32[]{:S(2)}) async-start(), calls=%async_computation.9 | async-start | bytes 3342336 | tf_op jit(solution)/shard_map/all_gather | solution.py:425
  40.5 33.8 %all-to-all-start.1 = ((bf16[4,2,160,1024]{3,2,1,0:T(8,128)(2,1)}), bf16[4,2,160,1024]{3,2,1,0:T(8,128)(2,1)S(1)}, u32[]{:S(2)}, u32[]{:S(2)}) async-start(bf16[4,2,160,1024]{3,2,1,0:T(8,128)(2,1)} %broadcast_in_dim.15), calls=%async_computation.1 | async-start | bytes 5242880 | tf_op jit(solution)/shard_map/all_to_all | solution.py:442
  44.3 72.3 %all-gather.7.cloned.1.call-start = ((), (), s32[]{:S(2)}) async-start(), calls=%async_computation.10 | async-start | bytes 5013504 | tf_op jit(solution)/shard_map/all_gather | solution.py:445
  76.1 16.8 %collective-permute-start.2 = (bf16[160,1024]{1,0:T(8,128)(2,1)S(1)}, bf16[160,1024]{1,0:T(8,128)(2,1)}, u32[]{:S(2)}, u32[]{:S(2)}) collective-permute-start(bf16[160,1024]{1,0:T(8,128)(2,1)S(1)} %copy-done.7), channel_id=1, source_target_pairs={{0,2},{2,0},{4,6},{6,4},{1,3},{3,1},{5,7},{7,5},{8,10},{10,8},{12,... | collective-permute-start | bytes 983048 | tf_op jit(solution)/shard_map/ppermute | solution.py:36
  76.8 16.2 %collective-permute-start.3 = (bf16[160,1024]{1,0:T(8,128)(2,1)S(1)}, bf16[160,1024]{1,0:T(8,128)(2,1)}, u32[]{:S(2)}, u32[]{:S(2)}) collective-permute-start(bf16[160,1024]{1,0:T(8,128)(2,1)S(1)} %copy-done.7), channel_id=1, source_target_pairs={{0,4},{2,6},{4,0},{6,2},{1,5},{3,7},{5,1},{7,3},{8,12},{10,14},{12... | collective-permute-start | bytes 983048 | tf_op jit(solution)/shard_map/ppermute | solution.py:36
  78.8 14.1 %collective-permute-start.4 = (bf16[160,1024]{1,0:T(8,128)(2,1)S(1)}, bf16[160,1024]{1,0:T(8,128)(2,1)}, u32[]{:S(2)}, u32[]{:S(2)}) collective-permute-start(bf16[160,1024]{1,0:T(8,128)(2,1)S(1)} %copy-done.7), channel_id=1, source_target_pairs={{0,6},{2,4},{4,2},{6,0},{1,7},{3,5},{5,3},{7,1},{8,14},{10,12},{12... | collective-permute-start | bytes 983048 | tf_op jit(solution)/shard_map/ppermute | solution.py:36
  92.9 12.4 %all-to-all-start.2 = ((bf16[8,160,128]{2,1,0:T(8,128)(2,1)}), bf16[8,160,128]{2,1,0:T(8,128)(2,1)S(1)}, u32[]{:S(2)}, u32[]{:S(2)}) async-start(bf16[8,160,128]{2,1,0:T(8,128)(2,1)} %bitcast.99), calls=%async_computation.2 | async-start | bytes 655360 | tf_op jit(solution)/shard_map/all_to_all | solution.py:451
  96.5 151.2 %reduce-scatter.2.cloned.1.call-start = ((), (), s32[]{:S(2)}) async-start(), calls=%async_computation.8 | async-start | bytes 7962624 | tf_op jit(solution)/shard_map/reduce_scatter | solution.py:479
  107.1 9.5 %collective-permute-start.5 = (bf16[160,1024]{1,0:T(8,128)(2,1)S(1)}, bf16[160,1024]{1,0:T(8,128)(2,1)S(1)}, u32[]{:S(2)}, u32[]{:S(2)}) collective-permute-start(bf16[160,1024]{1,0:T(8,128)(2,1)S(1)} %multiply_convert_fusion.refs_0_), channel_id=1, source_target_pairs={{0,2},{2,0},{4,6},{6,4},{1,3},{3,1},{5,7},{7,5},{8,10},{10,8},{12,... | collective-permute-start | bytes 983048 | tf_op jit(solution)/shard_map/ppermute | solution.py:36
  107.8 17.0 %collective-permute-start.6 = (bf16[160,1024]{1,0:T(8,128)(2,1)S(1)}, bf16[160,1024]{1,0:T(8,128)(2,1)}, u32[]{:S(2)}, u32[]{:S(2)}) collective-permute-start(bf16[160,1024]{1,0:T(8,128)(2,1)S(1)} %multiply_convert_fusion.refs_0_), channel_id=1, source_target_pairs={{0,4},{2,6},{4,0},{6,2},{1,5},{3,7},{5,1},{7,3},{8,12},{10,14},{12... | collective-permute-start | bytes 983048 | tf_op jit(solution)/shard_map/ppermute | solution.py:36
  110.5 14.4 %collective-permute-start.7 = (bf16[160,1024]{1,0:T(8,128)(2,1)S(1)}, bf16[160,1024]{1,0:T(8,128)(2,1)}, u32[]{:S(2)}, u32[]{:S(2)}) collective-permute-start(bf16[160,1024]{1,0:T(8,128)(2,1)S(1)} %multiply_convert_fusion.refs_0_), channel_id=1, source_target_pairs={{0,6},{2,4},{4,2},{6,0},{1,7},{3,5},{5,3},{7,1},{8,14},{10,12},{12... | collective-permute-start | bytes 983048 | tf_op jit(solution)/shard_map/ppermute | solution.py:36
  132.2 16.5 %collective-permute-start.10 = (bf16[160,1024]{1,0:T(8,128)(2,1)}, bf16[160,1024]{1,0:T(8,128)(2,1)S(1)}, u32[]{:S(2)}, u32[]{:S(2)}) collective-permute-start(bf16[160,1024]{1,0:T(8,128)(2,1)} %get-tuple-element.94), channel_id=1, source_target_pairs={{0,6},{2,4},{4,2},{6,0},{1,7},{3,5},{5,3},{7,1},{8,14},{10,12},{12... | collective-permute-start | bytes 983048 | tf_op jit(solution)/shard_map/ppermute | solution.py:36
  133.6 15.0 %collective-permute-start.9 = (bf16[160,1024]{1,0:T(8,128)(2,1)}, bf16[160,1024]{1,0:T(8,128)(2,1)S(1)}, u32[]{:S(2)}, u32[]{:S(2)}) collective-permute-start(bf16[160,1024]{1,0:T(8,128)(2,1)} %get-tuple-element.93), channel_id=1, source_target_pairs={{0,4},{2,6},{4,0},{6,2},{1,5},{3,7},{5,1},{7,3},{8,12},{10,14},{12... | collective-permute-start | bytes 983048 | tf_op jit(solution)/shard_map/ppermute | solution.py:36
  134.5 14.3 %collective-permute-start.8 = (bf16[160,1024]{1,0:T(8,128)(2,1)}, bf16[160,1024]{1,0:T(8,128)(2,1)}, u32[]{:S(2)}, u32[]{:S(2)}) collective-permute-start(bf16[160,1024]{1,0:T(8,128)(2,1)} %get-tuple-element.92), channel_id=1, source_target_pairs={{0,2},{2,0},{4,6},{6,4},{1,3},{3,1},{5,7},{7,5},{8,10},{10,8},{12,... | collective-permute-start | bytes 983048 | tf_op jit(solution)/shard_map/ppermute | solution.py:36
  159.0 15.6 %all-to-all-start.3 = ((bf16[8,160,128]{2,1,0:T(8,128)(2,1)}), bf16[8,160,128]{2,1,0:T(8,128)(2,1)S(1)}, u32[]{:S(2)}, u32[]{:S(2)}) async-start(bf16[8,160,128]{2,1,0:T(8,128)(2,1)} %bitcast_bitcast_fusion), calls=%async_computation.3 | async-start | bytes 655360 | tf_op jit(solution)/shard_map/all_to_all | solution.py:480
  174.6 19.6 %collective-permute-start.11 = (bf16[160,1024]{1,0:T(8,128)(2,1)}, bf16[160,1024]{1,0:T(8,128)(2,1)S(1)}, u32[]{:S(2)}, u32[]{:S(2)}) collective-permute-start(bf16[160,1024]{1,0:T(8,128)(2,1)} %get-tuple-element.96), channel_id=1, source_target_pairs={{0,2},{2,0},{4,6},{6,4},{1,3},{3,1},{5,7},{7,5},{8,10},{10,8},{12,... | collective-permute-start | bytes 983048 | tf_op jit(solution)/shard_map/ppermute | solution.py:36
  175.1 19.1 %collective-permute-start.12 = (bf16[160,1024]{1,0:T(8,128)(2,1)}, bf16[160,1024]{1,0:T(8,128)(2,1)S(1)}, u32[]{:S(2)}, u32[]{:S(2)}) collective-permute-start(bf16[160,1024]{1,0:T(8,128)(2,1)} %get-tuple-element.97), channel_id=1, source_target_pairs={{0,4},{2,6},{4,0},{6,2},{1,5},{3,7},{5,1},{7,3},{8,12},{10,14},{12... | collective-permute-start | bytes 983048 | tf_op jit(solution)/shard_map/ppermute | solution.py:36
  177.5 16.7 %collective-permute-start.13 = (bf16[160,1024]{1,0:T(8,128)(2,1)}, bf16[160,1024]{1,0:T(8,128)(2,1)S(1)}, u32[]{:S(2)}, u32[]{:S(2)}) collective-permute-start(bf16[160,1024]{1,0:T(8,128)(2,1)} %get-tuple-element.98), channel_id=1, source_target_pairs={{0,6},{2,4},{4,2},{6,0},{1,7},{3,5},{5,3},{7,1},{8,14},{10,12},{12... | collective-permute-start | bytes 983048 | tf_op jit(solution)/shard_map/ppermute | solution.py:36
  194.2 15.0 %collective-permute-start.14 = (bf16[160,1024]{1,0:T(8,128)(2,1)}, bf16[160,1024]{1,0:T(8,128)(2,1)}, u32[]{:S(2)}, u32[]{:S(2)}) collective-permute-start(bf16[160,1024]{1,0:T(8,128)(2,1)} %get-tuple-element.117), channel_id=1, source_target_pairs={{0,1},{1,0},{2,3},{3,2},{4,5},{5,4},{6,7},{7,6},{8,9},{9,8},{10,11... | collective-permute-start | bytes 983048 | tf_op jit(solution)/shard_map/ppermute | solution.py:36
  195.8 14.5 %collective-permute-start.15 = (bf16[160,1024]{1,0:T(8,128)(2,1)}, bf16[160,1024]{1,0:T(8,128)(2,1)}, u32[]{:S(2)}, u32[]{:S(2)}) collective-permute-start(bf16[160,1024]{1,0:T(8,128)(2,1)} %get-tuple-element.118), channel_id=1, source_target_pairs={{0,2},{1,3},{2,0},{3,1},{4,6},{5,7},{6,4},{7,5},{8,10},{9,11},{10,... | collective-permute-start | bytes 983048 | tf_op jit(solution)/shard_map/ppermute | solution.py:36
  201.2 20.9 %collective-permute-start.16 = (bf16[160,1024]{1,0:T(8,128)(2,1)}, bf16[160,1024]{1,0:T(8,128)(2,1)}, u32[]{:S(2)}, u32[]{:S(2)}) collective-permute-start(bf16[160,1024]{1,0:T(8,128)(2,1)} %get-tuple-element.119), channel_id=1, source_target_pairs={{0,3},{1,2},{2,1},{3,0},{4,7},{5,6},{6,5},{7,4},{8,11},{9,10},{10,... | collective-permute-start | bytes 983048 | tf_op jit(solution)/shard_map/ppermute | solution.py:36
  204.9 17.2 %collective-permute-start.17 = (bf16[160,1024]{1,0:T(8,128)(2,1)}, bf16[160,1024]{1,0:T(8,128)(2,1)}, u32[]{:S(2)}, u32[]{:S(2)}) collective-permute-start(bf16[160,1024]{1,0:T(8,128)(2,1)} %get-tuple-element.120), channel_id=1, source_target_pairs={{0,4},{1,5},{2,6},{3,7},{4,0},{5,1},{6,2},{7,3},{8,12},{9,13},{10,... | collective-permute-start | bytes 983048 | tf_op jit(solution)/shard_map/ppermute | solution.py:36
  205.9 21.2 %collective-permute-start.18 = (bf16[160,1024]{1,0:T(8,128)(2,1)}, bf16[160,1024]{1,0:T(8,128)(2,1)}, u32[]{:S(2)}, u32[]{:S(2)}) collective-permute-start(bf16[160,1024]{1,0:T(8,128)(2,1)} %get-tuple-element.121), channel_id=1, source_target_pairs={{0,5},{1,4},{2,7},{3,6},{4,1},{5,0},{6,3},{7,2},{8,13},{9,12},{10,... | collective-permute-start | bytes 983048 | tf_op jit(solution)/shard_map/ppermute | solution.py:36
  209.2 22.5 %collective-permute-start.19 = (bf16[160,1024]{1,0:T(8,128)(2,1)}, bf16[160,1024]{1,0:T(8,128)(2,1)}, u32[]{:S(2)}, u32[]{:S(2)}) collective-permute-start(bf16[160,1024]{1,0:T(8,128)(2,1)} %get-tuple-element.122), channel_id=1, source_target_pairs={{0,6},{1,7},{2,4},{3,5},{4,2},{5,3},{6,0},{7,1},{8,14},{9,15},{10,... | collective-permute-start | bytes 983048 | tf_op jit(solution)/shard_map/ppermute | solution.py:36
  210.4 32.1 %collective-permute-start.20 = (bf16[160,1024]{1,0:T(8,128)(2,1)}, bf16[160,1024]{1,0:T(8,128)(2,1)}, u32[]{:S(2)}, u32[]{:S(2)}) collective-permute-start(bf16[160,1024]{1,0:T(8,128)(2,1)} %get-tuple-element.123), channel_id=1, source_target_pairs={{0,7},{1,6},{2,5},{3,4},{4,3},{5,2},{6,1},{7,0},{8,15},{9,14},{10,... | collective-permute-start | bytes 983048 | tf_op jit(solution)/shard_map/ppermute | solution.py:36
  216.4 29.4 %all-to-all-start.4 = ((bf16[16,80,384]{2,1,0:T(8,128)(2,1)}), bf16[16,80,384]{2,1,0:T(8,128)(2,1)S(1)}, u32[]{:S(2)}, u32[]{:S(2)}) async-start(bf16[16,80,384]{2,1,0:T(8,128)(2,1)} %pad_maximum_fusion), calls=%async_computation.4 | async-start | bytes 1966080 | tf_op jit(solution)/shard_map/all_to_all | solution.py:496
  248.9 19.0 %collective-permute-start.21 = (bf16[9,64,384]{2,1,0:T(8,128)(2,1)S(1)}, bf16[9,64,384]{2,1,0:T(8,128)(2,1)S(1)}, u32[]{:S(2)}, u32[]{:S(2)}) collective-permute-start(bf16[9,64,384]{2,1,0:T(8,128)(2,1)S(1)} %dynamic-slice_bitcast_fusion), channel_id=1, source_target_pairs={{0,16},{16,0},{1,17},{17,1},{2,18},{18,2},{3,19},{19,3},{4,20},{20... | collective-permute-start | bytes 1327112 | tf_op jit(solution)/shard_map/ppermute | solution.py:36
  250.8 16.2 %all-to-all-start.5 = ((f32[128,1,128]{2,1,0:T(1,128)}), f32[128,1,128]{2,1,0:T(1,128)}, u32[]{:S(2)}, u32[]{:S(2)}) async-start(f32[128,1,128]{2,1,0:T(1,128)} %broadcast_in_dim.17), calls=%async_computation.5 | async-start | bytes 131072 | tf_op jit(solution)/shard_map/all_to_all | solution.py:514
  268.1 15.0 %collective-permute-start.22 = (bf16[3,64,384]{2,1,0:T(8,128)(2,1)S(1)}, bf16[3,64,384]{2,1,0:T(8,128)(2,1)S(1)}, u32[]{:S(2)}, u32[]{:S(2)}) collective-permute-start(bf16[3,64,384]{2,1,0:T(8,128)(2,1)S(1)} %get-tuple-element.182), channel_id=1, source_target_pairs={{0,1},{1,0},{2,3},{3,2},{4,5},{5,4},{6,7},{7,6},{8,9},{9,8},{10,11... | collective-permute-start | bytes 442376 | tf_op jit(solution)/shard_map/ppermute | solution.py:36
  270.5 12.0 %all-to-all-start.6 = ((bf16[8,64,128]{2,1,0:T(8,128)(2,1)}), bf16[8,64,128]{2,1,0:T(8,128)(2,1)S(1)}, u32[]{:S(2)}, u32[]{:S(2)}) async-start(bf16[8,64,128]{2,1,0:T(8,128)(2,1)} %bitcast_bitcast_fusion.1), calls=%async_computation.7 | async-start | bytes 262144 | tf_op jit(solution)/shard_map/all_to_all | solution.py:515
  (23 other events, 707.6 us)
Sparse Core Ops, SparseCore 0:
  36.6 34.3 all-gather.4
  76.2 38.6 all-gather.6
  155.3 46.5 reduce-scatter.1

commit v5 on v4

--- a/solution.py
+++ b/solution.py
@@ -475,7 +475,8 @@
     grad_mixed = jnp.concatenate([dot(grad_attn, full_out[b], 1, 0) for b in range(3)], axis=1)
     grad_mixed = grad_mixed[:, :WIDTH].astype(BF16)
     gm_parts = grad_mixed.reshape(ROWS, 8, 2 * HD).transpose(1, 0, 2)
-    grads = out_grads(grad_attn, mixed_own, grads)
+    grad_attn_later, gm_parts = lax.optimization_barrier((grad_attn, gm_parts))
+    grads = out_grads(grad_attn_later, mixed_own, grads)
     grads = lax.psum_scatter(grads, ("x", "c"), scatter_dimension=0)
     gm_own = lax.all_to_all(gm_parts, TP, 0, 0).reshape(LEN, 2 * HD)
 

time: 292 us -> 290 us (level)
  transfers between devices with their start and end apart: 33 -> 33, of which waited for: 13 -> 12; matrix products, arithmetic and copies ran while one was open for 10% -> 9% of each run, Pallas kernels for 18% -> 18%
where the time goes in v5:
time: 290 us; the launch traced here: 288 us
  waiting for transfers between devices  97.6 us (34%)
  starting transfers between devices  76.5 us (26%)
  Pallas kernels  63 us (22%)
  other arithmetic  21.7 us (7%)
  between operations  14.2 us (5%)
  local copies, waits for them, and re-layouts  13 us (4%)
    ppermute x23, waiting for transfers between devices, exchange(): return lax.ppermute(value, axes, [(i, i ^ mask) for i in range(count)])  40.2 us
    ppermute x23, starting transfers between devices, exchange(): return lax.ppermute(value, axes, [(i, i ^ mask) for i in range(count)])  40.1 us
    all_to_all x1, waiting for transfers between devices, on_device(): lax.all_to_all(jnp.broadcast_to(pair[None], (M, PRE, ROWS, WIDTH)), MLP_A...  21 us
    pallas_call x1, Pallas kernels, attend_back(): pl.pallas_call(attend_back_kernel, grid=(1,), in_specs=[pl.BlockSpec(memo...  14.9 us
    pallas_call x2, Pallas kernels, mlp(): pl.pallas_call(functools.partial(mlp_kernel, count), grid=(1,), in_specs=...  14.8 us
    pallas_call x1, Pallas kernels, mlp_grads(): pl.pallas_call(mlp_grads_kernel, grid=(PRE,), in_specs=[whole(ROWS, WIDTH...  12.4 us
    pallas_call x1, Pallas kernels, attend(): pl.pallas_call(attend_kernel, grid=(1,), in_specs=[ROWS_SPEC, QKV_SPEC, w...  12 us
    all_to_all x1, waiting for transfers between devices, on_device(): gm_own = lax.all_to_all(gm_parts, TP, 0, 0).reshape(LEN, 2 * HD)  8.62 us
  transfers between devices with their start and end apart: 33, of which 12 were waited for; matrix products, arithmetic and copies ran while one was open for 9% of the time, Pallas kernels for 18%

profile of v5, /device:TPU:0, one launch (start us, length us, event | category | flops | bytes accessed | tf_op | source)
XLA Modules:
  0.0 288.4 jit_solution(4706616415188233199)
XLA Ops:
  7.2 4.0 %collective-permute-start = (bf16[160,1024]{1,0:T(8,128)(2,1)}, bf16[160,1024]{1,0:T(8,128)(2,1)S(1)}, u32[]{:S(2)}, u32[]{:S(2)}) collective-permute-start(bf16[160,1024]{1,0:T(8,128)(2,1)} %param.10), channel_id=1, source_target_pairs={{0,1},{1,0},{2,3},{3,2},{4,5},{5,4},{6,7},{7,6},{8,9},{9,8},{10,11... | collective-permute-start | bytes 983048 | tf_op jit(solution)/shard_map/ppermute | solution.py:36
  11.3 7.9 %collective-permute-done = bf16[160,1024]{1,0:T(8,128)(2,1)S(1)} collective-permute-done((bf16[160,1024]{1,0:T(8,128)(2,1)}, bf16[160,1024]{1,0:T(8,128)(2,1)S(1)}, u32[]{:S(2)}, u32[]{:S(2)}) %collective-permute-start) | collective-permute-done | bytes 327712 | tf_op jit(solution)/shard_map/ppermute | solution.py:36
  20.6 7.1 %all-to-all-start = ((bf16[8,64,128]{2,1,0:T(8,128)(2,1)}), bf16[8,64,128]{2,1,0:T(8,128)(2,1)S(1)}, u32[]{:S(2)}, u32[]{:S(2)}) async-start(bf16[8,64,128]{2,1,0:T(8,128)(2,1)} %broadcast_in_dim.13), calls=%async_computation | async-start | bytes 262144 | tf_op jit(solution)/shard_map/all_to_all | solution.py:421
  27.8 7.8 %all-to-all-done = bf16[8,64,128]{2,1,0:T(8,128)(2,1)S(1)} async-done(((bf16[8,64,128]{2,1,0:T(8,128)(2,1)}), bf16[8,64,128]{2,1,0:T(8,128)(2,1)S(1)}, u32[]{:S(2)}, u32[]{:S(2)}) %all-to-all-start) | async-done | bytes 131104 | tf_op jit(solution)/shard_map/all_to_all | solution.py:421
  40.5 3.8 %all-to-all-start.1 = ((bf16[4,2,160,1024]{3,2,1,0:T(8,128)(2,1)}), bf16[4,2,160,1024]{3,2,1,0:T(8,128)(2,1)S(1)}, u32[]{:S(2)}, u32[]{:S(2)}) async-start(bf16[4,2,160,1024]{3,2,1,0:T(8,128)(2,1)} %broadcast_in_dim.15), calls=%async_computation.1 | async-start | bytes 5242880 | tf_op jit(solution)/shard_map/all_to_all | solution.py:442
  45.5 7.7 %collective-permute-done.1 = bf16[3,64,384]{2,1,0:T(8,128)(2,1)} collective-permute-done((bf16[3,64,384]{2,1,0:T(8,128)(2,1)S(1)}, bf16[3,64,384]{2,1,0:T(8,128)(2,1)}, u32[]{:S(2)}, u32[]{:S(2)}) %collective-permute-start.1) | collective-permute-done | bytes 147488 | tf_op jit(solution)/shard_map/ppermute | solution.py:36
  53.2 21.0 %all-to-all-done.1 = bf16[4,2,160,1024]{3,2,1,0:T(8,128)(2,1)S(1)} async-done(((bf16[4,2,160,1024]{3,2,1,0:T(8,128)(2,1)}), bf16[4,2,160,1024]{3,2,1,0:T(8,128)(2,1)S(1)}, u32[]{:S(2)}, u32[]{:S(2)}) %all-to-all-start.1) | async-done | bytes 2621472 | tf_op jit(solution)/shard_map/all_to_all | solution.py:442
  80.9 12.0 %attend.1 = (bf16[1280,128]{1,0:T(8,128)(2,1)}, bf16[1280,128]{1,0:T(8,128)(2,1)}, bf16[1280,128]{1,0:T(8,128)(2,1)}, bf16[1280,128]{1,0:T(8,128)(2,1)}, f32[1280,128]{1,0:T(8,128)}) custom-call(bf16[8,160,1024]{2,1,0:T(8,128)(2,1)} %bitcast.91, bf16[16,4,64,384]{3,2,1,0:T(8,128)(2,1)} %bitcast.93, f32[1280,128]{1,0:T(8,128)} %constant.67.clone.cos_ref.refs_5_, ...), custom_call_target="tpu_custom_call" | custom-call | flops 6000000000 | bytes 8000000 | tf_op jit(solution)/shard_map/attend/pallas_call | solution.py:147
  92.9 3.6 %all-to-all-start.2 = ((bf16[8,160,128]{2,1,0:T(8,128)(2,1)}), bf16[8,160,128]{2,1,0:T(8,128)(2,1)S(1)}, u32[]{:S(2)}, u32[]{:S(2)}) async-start(bf16[8,160,128]{2,1,0:T(8,128)(2,1)} %bitcast.99), calls=%async_computation.2 | async-start | bytes 655360 | tf_op jit(solution)/shard_map/all_to_all | solution.py:451
  98.5 6.8 %all-to-all-done.2 = bf16[8,160,128]{2,1,0:T(8,128)(2,1)S(1)} async-done(((bf16[8,160,128]{2,1,0:T(8,128)(2,1)}), bf16[8,160,128]{2,1,0:T(8,128)(2,1)S(1)}, u32[]{:S(2)}, u32[]{:S(2)}) %all-to-all-start.2) | async-done | bytes 327712 | tf_op jit(solution)/shard_map/all_to_all | solution.py:451
  108.4 2.7 collective-permute-start.6
  113.3 4.2 %collective-permute-done.5.refs_1_ = bf16[160,1024]{1,0:T(8,128)(2,1)} collective-permute-done((bf16[160,1024]{1,0:T(8,128)(2,1)}, bf16[160,1024]{1,0:T(8,128)(2,1)}, u32[]{:S(2)}, u32[]{:S(2)}) %collective-permute-start.5) | collective-permute-done | bytes 327712 | tf_op jit(solution)/shard_map/ppermute | solution.py:36
  117.6 7.4 %mlp.2 = (bf16[2,320,384]{2,1,0:T(8,128)(2,1)}, bf16[2,2,320,384]{3,2,1,0:T(8,128)(2,1)}, bf16[160,1024]{1,0:T(8,128)(2,1)}, bf16[160,1024]{1,0:T(8,128)(2,1)}) custom-call(bf16[160,1024]{1,0:T(8,128)(2,1)} %multiply_convert_fusion.refs_0_, bf16[160,1024]{1,0:T(8,128)(2,1)} %collective-permute-done.5.refs_1_, bf16[160,1024]{1,0:T(8,128)(2,1)} %refs_4_, ...), custom_call_target="tpu_custom_call" | custom-call | flops 5000000000 | bytes 8000000 | tf_op jit(solution)/shard_map/mlp/pallas_call | solution.py:304
  125.0 7.4 %mlp.3 = (bf16[2,320,384]{2,1,0:T(8,128)(2,1)}, bf16[2,2,320,384]{3,2,1,0:T(8,128)(2,1)}, bf16[160,1024]{1,0:T(8,128)(2,1)}, bf16[160,1024]{1,0:T(8,128)(2,1)}) custom-call(bf16[160,1024]{1,0:T(8,128)(2,1)} %collective-permute-done.6.refs_0_.refs_2_, bf16[160,1024]{1,0:T(8,128)(2,1)} %collective-permute-done.7.refs_1_.refs_3_, ...), custom_call_target="tpu_custom_call" | custom-call | flops 5000000000 | bytes 8000000 | tf_op jit(solution)/shard_map/mlp/pallas_call | solution.py:304
  136.5 12.4 %mlp_grads.1 = (bf16[8,2,9,64,384]{4,3,2,1,0:T(8,128)(2,1)}, bf16[160,1024]{1,0:T(8,128)(2,1)}, bf16[160,1024]{1,0:T(8,128)(2,1)}, bf16[160,1024]{1,0:T(8,128)(2,1)}, bf16[160,1024]{1,0:T(8,128)(2,1)}) custom-call(bf16[160,1024]{1,0:T(8,128)(2,1)} %multiply_convert_fusion.refs_0_, bf16[160,1024]{1,0:T(8,128)(2,1)} %collective-permute-done.5.refs_1_, ...), custom_call_target="tpu_custom_call" | custom-call | flops 8000000000 | bytes 12000000 | tf_op jit(solution)/shard_map/mlp_grads/pallas_call | solution.py:362
  153.5 3.5 %out_grads.1 = bf16[8,2,9,64,384]{4,3,2,1,0:T(8,128)(2,1)} custom-call(bf16[160,1024]{1,0:T(8,128)(2,1)} %copy-done.2, bf16[160,1152]{1,0:T(8,128)(2,1)} %pad.13.mixed_ref, bf16[8,2,9,64,384]{4,3,2,1,0:T(8,128)(2,1)} %get-tuple-element.129.held_ref), custom_call_target="tpu_custom_call", output_to_operand_aliasing={{}: (2, {})} | custom-call | flops 400000000 | bytes 4000000 | tf_op jit(solution)/shard_map/out_grads/pallas_call | solution.py:395
  157.1 6.8 %all-to-all-start.3 = ((bf16[8,160,128]{2,1,0:T(8,128)(2,1)}), bf16[8,160,128]{2,1,0:T(8,128)(2,1)S(1)}, u32[]{:S(2)}, u32[]{:S(2)}) async-start(bf16[8,160,128]{2,1,0:T(8,128)(2,1)} %bitcast_bitcast_fusion), calls=%async_computation.3 | async-start | bytes 655360 | tf_op jit(solution)/shard_map/all_to_all | solution.py:481
  164.0 8.6 %all-to-all-done.3 = bf16[8,160,128]{2,1,0:T(8,128)(2,1)S(1)} async-done(((bf16[8,160,128]{2,1,0:T(8,128)(2,1)}), bf16[8,160,128]{2,1,0:T(8,128)(2,1)S(1)}, u32[]{:S(2)}, u32[]{:S(2)}) %all-to-all-start.3) | async-done | bytes 327712 | tf_op jit(solution)/shard_map/all_to_all | solution.py:481
  173.2 2.4 collective-permute-start.12
  177.4 14.9 %attend_back.1 = (bf16[1280,384]{1,0:T(8,128)(2,1)}, bf16[160,1024]{1,0:T(8,128)(2,1)}, bf16[160,1024]{1,0:T(8,128)(2,1)}, bf16[160,1024]{1,0:T(8,128)(2,1)}, bf...) custom-call(s32[1]{0:T(128)} %bitcast.16.me_ref, ...), custom_call_target="tpu_custom_call" | custom-call | flops 12000000000 | bytes 8000000 | tf_op jit(solution)/shard_map/attend_back/pallas_call | solution.py:202
  194.0 5.4 %qkv_grads.1 = bf16[16,64,384]{2,1,0:T(8,128)(2,1)} custom-call(bf16[8,160,1024]{2,1,0:T(8,128)(2,1)} %bitcast.92, bf16[1280,384]{1,0:T(8,128)(2,1)} %get-tuple-element.127.g_ref), custom_call_target="tpu_custom_call" | custom-call | flops 2000000000 | bytes 5000000 | tf_op jit(solution)/shard_map/qkv_grads/pallas_call | solution.py:231
  199.4 3.7 %collective-permute-start.16 = (bf16[160,1024]{1,0:T(8,128)(2,1)}, bf16[160,1024]{1,0:T(8,128)(2,1)}, u32[]{:S(2)}, u32[]{:S(2)}) collective-permute-start(bf16[160,1024]{1,0:T(8,128)(2,1)} %get-tuple-element.122), channel_id=1, source_target_pairs={{0,3},{1,2},{2,1},{3,0},{4,7},{5,6},{6,5},{7,4},{8,11},{9,10},{10,... | collective-permute-start | bytes 983048 | tf_op jit(solution)/shard_map/ppermute | solution.py:36
  204.0 3.4 %collective-permute-start.18 = (bf16[160,1024]{1,0:T(8,128)(2,1)}, bf16[160,1024]{1,0:T(8,128)(2,1)}, u32[]{:S(2)}, u32[]{:S(2)}) collective-permute-start(bf16[160,1024]{1,0:T(8,128)(2,1)} %get-tuple-element.124), channel_id=1, source_target_pairs={{0,5},{1,4},{2,7},{3,6},{4,1},{5,0},{6,3},{7,2},{8,13},{9,12},{10,... | collective-permute-start | bytes 983048 | tf_op jit(solution)/shard_map/ppermute | solution.py:36
  208.5 3.7 %collective-permute-start.20 = (bf16[160,1024]{1,0:T(8,128)(2,1)}, bf16[160,1024]{1,0:T(8,128)(2,1)}, u32[]{:S(2)}, u32[]{:S(2)}) collective-permute-start(bf16[160,1024]{1,0:T(8,128)(2,1)} %get-tuple-element.126), channel_id=1, source_target_pairs={{0,7},{1,6},{2,5},{3,4},{4,3},{5,2},{6,1},{7,0},{8,15},{9,14},{10,... | collective-permute-start | bytes 983048 | tf_op jit(solution)/shard_map/ppermute | solution.py:36
  214.5 3.7 %all-to-all-start.4 = ((bf16[16,80,384]{2,1,0:T(8,128)(2,1)}), bf16[16,80,384]{2,1,0:T(8,128)(2,1)S(1)}, u32[]{:S(2)}, u32[]{:S(2)}) async-start(bf16[16,80,384]{2,1,0:T(8,128)(2,1)} %pad_maximum_fusion), calls=%async_computation.4 | async-start | bytes 1966080 | tf_op jit(solution)/shard_map/all_to_all | solution.py:497
  220.2 4.9 %collective-permute-done.18 = bf16[160,1024]{1,0:T(8,128)(2,1)} collective-permute-done((bf16[160,1024]{1,0:T(8,128)(2,1)}, bf16[160,1024]{1,0:T(8,128)(2,1)}, u32[]{:S(2)}, u32[]{:S(2)}) %collective-permute-start.18) | collective-permute-done | bytes 327712 | tf_op jit(solution)/shard_map/ppermute | solution.py:36
  225.2 4.7 %collective-permute-done.19 = bf16[160,1024]{1,0:T(8,128)(2,1)} collective-permute-done((bf16[160,1024]{1,0:T(8,128)(2,1)}, bf16[160,1024]{1,0:T(8,128)(2,1)}, u32[]{:S(2)}, u32[]{:S(2)}) %collective-permute-start.19) | collective-permute-done | bytes 327712 | tf_op jit(solution)/shard_map/ppermute | solution.py:36
  229.8 10.7 %collective-permute-done.20 = bf16[160,1024]{1,0:T(8,128)(2,1)} collective-permute-done((bf16[160,1024]{1,0:T(8,128)(2,1)}, bf16[160,1024]{1,0:T(8,128)(2,1)}, u32[]{:S(2)}, u32[]{:S(2)}) %collective-permute-start.20) | collective-permute-done | bytes 327712 | tf_op jit(solution)/shard_map/ppermute | solution.py:36
  248.2 7.1 %all-to-all-start.5 = ((f32[128,1,128]{2,1,0:T(1,128)}), f32[128,1,128]{2,1,0:T(1,128)}, u32[]{:S(2)}, u32[]{:S(2)}) async-start(f32[128,1,128]{2,1,0:T(1,128)} %broadcast_in_dim.17), calls=%async_computation.5 | async-start | bytes 131072 | tf_op jit(solution)/shard_map/all_to_all | solution.py:515
  257.7 6.6 %all-to-all-done.5 = f32[128,1,128]{2,1,0:T(1,128)} async-done(((f32[128,1,128]{2,1,0:T(1,128)}), f32[128,1,128]{2,1,0:T(1,128)}, u32[]{:S(2)}, u32[]{:S(2)}) %all-to-all-start.5) | async-done | bytes 65568 | tf_op jit(solution)/shard_map/all_to_all | solution.py:515
  267.7 4.1 %all-to-all-start.6 = ((bf16[8,64,128]{2,1,0:T(8,128)(2,1)}), bf16[8,64,128]{2,1,0:T(8,128)(2,1)S(1)}, u32[]{:S(2)}, u32[]{:S(2)}) async-start(bf16[8,64,128]{2,1,0:T(8,128)(2,1)} %bitcast_bitcast_fusion.1), calls=%async_computation.7 | async-start | bytes 262144 | tf_op jit(solution)/shard_map/all_to_all | solution.py:516
  273.2 6.5 %all-to-all-done.6 = bf16[8,64,128]{2,1,0:T(8,128)(2,1)S(1)} async-done(((bf16[8,64,128]{2,1,0:T(8,128)(2,1)}), bf16[8,64,128]{2,1,0:T(8,128)(2,1)S(1)}, u32[]{:S(2)}, u32[]{:S(2)}) %all-to-all-start.6) | async-done | bytes 131104 | tf_op jit(solution)/shard_map/all_to_all | solution.py:516
  (162 shorter events, 57.4 us)
Async XLA Ops:
  7.2 12.0 %collective-permute-start = (bf16[160,1024]{1,0:T(8,128)(2,1)}, bf16[160,1024]{1,0:T(8,128)(2,1)S(1)}, u32[]{:S(2)}, u32[]{:S(2)}) collective-permute-start(bf16[160,1024]{1,0:T(8,128)(2,1)} %param.10), channel_id=1, source_target_pairs={{0,1},{1,0},{2,3},{3,2},{4,5},{5,4},{6,7},{7,6},{8,9},{9,8},{10,11... | collective-permute-start | bytes 983048 | tf_op jit(solution)/shard_map/ppermute | solution.py:36
  20.6 15.1 %all-to-all-start = ((bf16[8,64,128]{2,1,0:T(8,128)(2,1)}), bf16[8,64,128]{2,1,0:T(8,128)(2,1)S(1)}, u32[]{:S(2)}, u32[]{:S(2)}) async-start(bf16[8,64,128]{2,1,0:T(8,128)(2,1)} %broadcast_in_dim.13), calls=%async_computation | async-start | bytes 262144 | tf_op jit(solution)/shard_map/all_to_all | solution.py:421
  27.7 53.2 %all-gather.5.cloned.1.call-start = ((), (), s32[]{:S(2)}) async-start(), calls=%async_computation.9 | async-start | bytes 3342336 | tf_op jit(solution)/shard_map/all_gather | solution.py:425
  40.5 33.8 %all-to-all-start.1 = ((bf16[4,2,160,1024]{3,2,1,0:T(8,128)(2,1)}), bf16[4,2,160,1024]{3,2,1,0:T(8,128)(2,1)S(1)}, u32[]{:S(2)}, u32[]{:S(2)}) async-start(bf16[4,2,160,1024]{3,2,1,0:T(8,128)(2,1)} %broadcast_in_dim.15), calls=%async_computation.1 | async-start | bytes 5242880 | tf_op jit(solution)/shard_map/all_to_all | solution.py:442
  44.3 73.3 %all-gather.7.cloned.1.call-start = ((), (), s32[]{:S(2)}) async-start(), calls=%async_computation.10 | async-start | bytes 5013504 | tf_op jit(solution)/shard_map/all_gather | solution.py:445
  76.1 16.8 %collective-permute-start.2 = (bf16[160,1024]{1,0:T(8,128)(2,1)S(1)}, bf16[160,1024]{1,0:T(8,128)(2,1)}, u32[]{:S(2)}, u32[]{:S(2)}) collective-permute-start(bf16[160,1024]{1,0:T(8,128)(2,1)S(1)} %copy-done.6), channel_id=1, source_target_pairs={{0,2},{2,0},{4,6},{6,4},{1,3},{3,1},{5,7},{7,5},{8,10},{10,8},{12,... | collective-permute-start | bytes 983048 | tf_op jit(solution)/shard_map/ppermute | solution.py:36
  76.8 16.1 %collective-permute-start.3 = (bf16[160,1024]{1,0:T(8,128)(2,1)S(1)}, bf16[160,1024]{1,0:T(8,128)(2,1)}, u32[]{:S(2)}, u32[]{:S(2)}) collective-permute-start(bf16[160,1024]{1,0:T(8,128)(2,1)S(1)} %copy-done.6), channel_id=1, source_target_pairs={{0,4},{2,6},{4,0},{6,2},{1,5},{3,7},{5,1},{7,3},{8,12},{10,14},{12... | collective-permute-start | bytes 983048 | tf_op jit(solution)/shard_map/ppermute | solution.py:36
  78.8 14.1 %collective-permute-start.4 = (bf16[160,1024]{1,0:T(8,128)(2,1)S(1)}, bf16[160,1024]{1,0:T(8,128)(2,1)}, u32[]{:S(2)}, u32[]{:S(2)}) collective-permute-start(bf16[160,1024]{1,0:T(8,128)(2,1)S(1)} %copy-done.6), channel_id=1, source_target_pairs={{0,6},{2,4},{4,2},{6,0},{1,7},{3,5},{5,3},{7,1},{8,14},{10,12},{12... | collective-permute-start | bytes 983048 | tf_op jit(solution)/shard_map/ppermute | solution.py:36
  92.9 12.4 %all-to-all-start.2 = ((bf16[8,160,128]{2,1,0:T(8,128)(2,1)}), bf16[8,160,128]{2,1,0:T(8,128)(2,1)S(1)}, u32[]{:S(2)}, u32[]{:S(2)}) async-start(bf16[8,160,128]{2,1,0:T(8,128)(2,1)} %bitcast.99), calls=%async_computation.2 | async-start | bytes 655360 | tf_op jit(solution)/shard_map/all_to_all | solution.py:451
  96.5 148.7 %reduce-scatter.2.cloned.1.call-start = ((), (), s32[]{:S(2)}) async-start(), calls=%async_computation.8 | async-start | bytes 7962624 | tf_op jit(solution)/shard_map/reduce_scatter | solution.py:480
  107.8 9.7 %collective-permute-start.5 = (bf16[160,1024]{1,0:T(8,128)(2,1)}, bf16[160,1024]{1,0:T(8,128)(2,1)}, u32[]{:S(2)}, u32[]{:S(2)}) collective-permute-start(bf16[160,1024]{1,0:T(8,128)(2,1)} %multiply_convert_fusion.refs_0_), channel_id=1, source_target_pairs={{0,2},{2,0},{4,6},{6,4},{1,3},{3,1},{5,7},{7,5},{8,10},{10,8},{12,... | collective-permute-start | bytes 983048 | tf_op jit(solution)/shard_map/ppermute | solution.py:36
  108.4 16.6 %collective-permute-start.6 = (bf16[160,1024]{1,0:T(8,128)(2,1)}, bf16[160,1024]{1,0:T(8,128)(2,1)}, u32[]{:S(2)}, u32[]{:S(2)}) collective-permute-start(bf16[160,1024]{1,0:T(8,128)(2,1)} %multiply_convert_fusion.refs_0_), channel_id=1, source_target_pairs={{0,4},{2,6},{4,0},{6,2},{1,5},{3,7},{5,1},{7,3},{8,12},{10,14},{12... | collective-permute-start | bytes 983048 | tf_op jit(solution)/shard_map/ppermute | solution.py:36
  111.1 13.9 %collective-permute-start.7 = (bf16[160,1024]{1,0:T(8,128)(2,1)}, bf16[160,1024]{1,0:T(8,128)(2,1)}, u32[]{:S(2)}, u32[]{:S(2)}) collective-permute-start(bf16[160,1024]{1,0:T(8,128)(2,1)} %multiply_convert_fusion.refs_0_), channel_id=1, source_target_pairs={{0,6},{2,4},{4,2},{6,0},{1,7},{3,5},{5,3},{7,1},{8,14},{10,12},{12... | collective-permute-start | bytes 983048 | tf_op jit(solution)/shard_map/ppermute | solution.py:36
  132.4 16.5 %collective-permute-start.10 = (bf16[160,1024]{1,0:T(8,128)(2,1)}, bf16[160,1024]{1,0:T(8,128)(2,1)}, u32[]{:S(2)}, u32[]{:S(2)}) collective-permute-start(bf16[160,1024]{1,0:T(8,128)(2,1)} %get-tuple-element.96), channel_id=1, source_target_pairs={{0,6},{2,4},{4,2},{6,0},{1,7},{3,5},{5,3},{7,1},{8,14},{10,12},{12... | collective-permute-start | bytes 983048 | tf_op jit(solution)/shard_map/ppermute | solution.py:36
  133.8 15.1 %collective-permute-start.9 = (bf16[160,1024]{1,0:T(8,128)(2,1)}, bf16[160,1024]{1,0:T(8,128)(2,1)}, u32[]{:S(2)}, u32[]{:S(2)}) collective-permute-start(bf16[160,1024]{1,0:T(8,128)(2,1)} %get-tuple-element.95), channel_id=1, source_target_pairs={{0,4},{2,6},{4,0},{6,2},{1,5},{3,7},{5,1},{7,3},{8,12},{10,14},{12... | collective-permute-start | bytes 983048 | tf_op jit(solution)/shard_map/ppermute | solution.py:36
  134.7 14.1 %collective-permute-start.8 = (bf16[160,1024]{1,0:T(8,128)(2,1)}, bf16[160,1024]{1,0:T(8,128)(2,1)}, u32[]{:S(2)}, u32[]{:S(2)}) collective-permute-start(bf16[160,1024]{1,0:T(8,128)(2,1)} %get-tuple-element.94), channel_id=1, source_target_pairs={{0,2},{2,0},{4,6},{6,4},{1,3},{3,1},{5,7},{7,5},{8,10},{10,8},{12,... | collective-permute-start | bytes 983048 | tf_op jit(solution)/shard_map/ppermute | solution.py:36
  157.1 15.5 %all-to-all-start.3 = ((bf16[8,160,128]{2,1,0:T(8,128)(2,1)}), bf16[8,160,128]{2,1,0:T(8,128)(2,1)S(1)}, u32[]{:S(2)}, u32[]{:S(2)}) async-start(bf16[8,160,128]{2,1,0:T(8,128)(2,1)} %bitcast_bitcast_fusion), calls=%async_computation.3 | async-start | bytes 655360 | tf_op jit(solution)/shard_map/all_to_all | solution.py:481
  172.6 19.6 %collective-permute-start.11 = (bf16[160,1024]{1,0:T(8,128)(2,1)S(1)}, bf16[160,1024]{1,0:T(8,128)(2,1)S(1)}, u32[]{:S(2)}, u32[]{:S(2)}) collective-permute-start(bf16[160,1024]{1,0:T(8,128)(2,1)S(1)} %copy-done.23), channel_id=1, source_target_pairs={{0,2},{2,0},{4,6},{6,4},{1,3},{3,1},{5,7},{7,5},{8,10},{10,8},{12,... | collective-permute-start | bytes 983048 | tf_op jit(solution)/shard_map/ppermute | solution.py:36
  173.2 19.1 %collective-permute-start.12 = (bf16[160,1024]{1,0:T(8,128)(2,1)S(1)}, bf16[160,1024]{1,0:T(8,128)(2,1)S(1)}, u32[]{:S(2)}, u32[]{:S(2)}) collective-permute-start(bf16[160,1024]{1,0:T(8,128)(2,1)S(1)} %copy-done.22), channel_id=1, source_target_pairs={{0,4},{2,6},{4,0},{6,2},{1,5},{3,7},{5,1},{7,3},{8,12},{10,14},{12... | collective-permute-start | bytes 983048 | tf_op jit(solution)/shard_map/ppermute | solution.py:36
  175.6 16.7 %collective-permute-start.13 = (bf16[160,1024]{1,0:T(8,128)(2,1)S(1)}, bf16[160,1024]{1,0:T(8,128)(2,1)S(1)}, u32[]{:S(2)}, u32[]{:S(2)}) collective-permute-start(bf16[160,1024]{1,0:T(8,128)(2,1)S(1)} %copy-done.21), channel_id=1, source_target_pairs={{0,6},{2,4},{4,2},{6,0},{1,7},{3,5},{5,3},{7,1},{8,14},{10,12},{12... | collective-permute-start | bytes 983048 | tf_op jit(solution)/shard_map/ppermute | solution.py:36
  192.3 15.1 %collective-permute-start.14 = (bf16[160,1024]{1,0:T(8,128)(2,1)}, bf16[160,1024]{1,0:T(8,128)(2,1)S(1)}, u32[]{:S(2)}, u32[]{:S(2)}) collective-permute-start(bf16[160,1024]{1,0:T(8,128)(2,1)} %get-tuple-element.120), channel_id=1, source_target_pairs={{0,1},{1,0},{2,3},{3,2},{4,5},{5,4},{6,7},{7,6},{8,9},{9,8},{10,11... | collective-permute-start | bytes 983048 | tf_op jit(solution)/shard_map/ppermute | solution.py:36
  193.9 14.6 %collective-permute-start.15 = (bf16[160,1024]{1,0:T(8,128)(2,1)}, bf16[160,1024]{1,0:T(8,128)(2,1)S(1)}, u32[]{:S(2)}, u32[]{:S(2)}) collective-permute-start(bf16[160,1024]{1,0:T(8,128)(2,1)} %get-tuple-element.121), channel_id=1, source_target_pairs={{0,2},{1,3},{2,0},{3,1},{4,6},{5,7},{6,4},{7,5},{8,10},{9,11},{10,... | collective-permute-start | bytes 983048 | tf_op jit(solution)/shard_map/ppermute | solution.py:36
  199.4 20.8 %collective-permute-start.16 = (bf16[160,1024]{1,0:T(8,128)(2,1)}, bf16[160,1024]{1,0:T(8,128)(2,1)}, u32[]{:S(2)}, u32[]{:S(2)}) collective-permute-start(bf16[160,1024]{1,0:T(8,128)(2,1)} %get-tuple-element.122), channel_id=1, source_target_pairs={{0,3},{1,2},{2,1},{3,0},{4,7},{5,6},{6,5},{7,4},{8,11},{9,10},{10,... | collective-permute-start | bytes 983048 | tf_op jit(solution)/shard_map/ppermute | solution.py:36
  203.1 17.1 %collective-permute-start.17 = (bf16[160,1024]{1,0:T(8,128)(2,1)}, bf16[160,1024]{1,0:T(8,128)(2,1)}, u32[]{:S(2)}, u32[]{:S(2)}) collective-permute-start(bf16[160,1024]{1,0:T(8,128)(2,1)} %get-tuple-element.123), channel_id=1, source_target_pairs={{0,4},{1,5},{2,6},{3,7},{4,0},{5,1},{6,2},{7,3},{8,12},{9,13},{10,... | collective-permute-start | bytes 983048 | tf_op jit(solution)/shard_map/ppermute | solution.py:36
  204.0 21.2 %collective-permute-start.18 = (bf16[160,1024]{1,0:T(8,128)(2,1)}, bf16[160,1024]{1,0:T(8,128)(2,1)}, u32[]{:S(2)}, u32[]{:S(2)}) collective-permute-start(bf16[160,1024]{1,0:T(8,128)(2,1)} %get-tuple-element.124), channel_id=1, source_target_pairs={{0,5},{1,4},{2,7},{3,6},{4,1},{5,0},{6,3},{7,2},{8,13},{9,12},{10,... | collective-permute-start | bytes 983048 | tf_op jit(solution)/shard_map/ppermute | solution.py:36
  207.4 22.5 %collective-permute-start.19 = (bf16[160,1024]{1,0:T(8,128)(2,1)}, bf16[160,1024]{1,0:T(8,128)(2,1)}, u32[]{:S(2)}, u32[]{:S(2)}) collective-permute-start(bf16[160,1024]{1,0:T(8,128)(2,1)} %get-tuple-element.125), channel_id=1, source_target_pairs={{0,6},{1,7},{2,4},{3,5},{4,2},{5,3},{6,0},{7,1},{8,14},{9,15},{10,... | collective-permute-start | bytes 983048 | tf_op jit(solution)/shard_map/ppermute | solution.py:36
  208.5 32.0 %collective-permute-start.20 = (bf16[160,1024]{1,0:T(8,128)(2,1)}, bf16[160,1024]{1,0:T(8,128)(2,1)}, u32[]{:S(2)}, u32[]{:S(2)}) collective-permute-start(bf16[160,1024]{1,0:T(8,128)(2,1)} %get-tuple-element.126), channel_id=1, source_target_pairs={{0,7},{1,6},{2,5},{3,4},{4,3},{5,2},{6,1},{7,0},{8,15},{9,14},{10,... | collective-permute-start | bytes 983048 | tf_op jit(solution)/shard_map/ppermute | solution.py:36
  214.5 29.3 %all-to-all-start.4 = ((bf16[16,80,384]{2,1,0:T(8,128)(2,1)}), bf16[16,80,384]{2,1,0:T(8,128)(2,1)S(1)}, u32[]{:S(2)}, u32[]{:S(2)}) async-start(bf16[16,80,384]{2,1,0:T(8,128)(2,1)} %pad_maximum_fusion), calls=%async_computation.4 | async-start | bytes 1966080 | tf_op jit(solution)/shard_map/all_to_all | solution.py:497
  246.3 18.8 %collective-permute-start.21 = (bf16[9,64,384]{2,1,0:T(8,128)(2,1)S(1)}, bf16[9,64,384]{2,1,0:T(8,128)(2,1)S(1)}, u32[]{:S(2)}, u32[]{:S(2)}) collective-permute-start(bf16[9,64,384]{2,1,0:T(8,128)(2,1)S(1)} %dynamic-slice_bitcast_fusion), channel_id=1, source_target_pairs={{0,16},{16,0},{1,17},{17,1},{2,18},{18,2},{3,19},{19,3},{4,20},{20... | collective-permute-start | bytes 1327112 | tf_op jit(solution)/shard_map/ppermute | solution.py:36
  248.2 16.1 %all-to-all-start.5 = ((f32[128,1,128]{2,1,0:T(1,128)}), f32[128,1,128]{2,1,0:T(1,128)}, u32[]{:S(2)}, u32[]{:S(2)}) async-start(f32[128,1,128]{2,1,0:T(1,128)} %broadcast_in_dim.17), calls=%async_computation.5 | async-start | bytes 131072 | tf_op jit(solution)/shard_map/all_to_all | solution.py:515
  265.4 15.0 %collective-permute-start.22 = (bf16[3,64,384]{2,1,0:T(8,128)(2,1)S(1)}, bf16[3,64,384]{2,1,0:T(8,128)(2,1)S(1)}, u32[]{:S(2)}, u32[]{:S(2)}) collective-permute-start(bf16[3,64,384]{2,1,0:T(8,128)(2,1)S(1)} %get-tuple-element.186), channel_id=1, source_target_pairs={{0,1},{1,0},{2,3},{3,2},{4,5},{5,4},{6,7},{7,6},{8,9},{9,8},{10,11... | collective-permute-start | bytes 442376 | tf_op jit(solution)/shard_map/ppermute | solution.py:36
  267.7 12.0 %all-to-all-start.6 = ((bf16[8,64,128]{2,1,0:T(8,128)(2,1)}), bf16[8,64,128]{2,1,0:T(8,128)(2,1)S(1)}, u32[]{:S(2)}, u32[]{:S(2)}) async-start(bf16[8,64,128]{2,1,0:T(8,128)(2,1)} %bitcast_bitcast_fusion.1), calls=%async_computation.7 | async-start | bytes 262144 | tf_op jit(solution)/shard_map/all_to_all | solution.py:516
  (25 other events, 748.5 us)
Sparse Core Ops, SparseCore 0:
  36.6 34.3 all-gather.4
  76.2 38.6 all-gather.6
  157.2 46.3 reduce-scatter.1

commit v6 on v5

--- a/solution.py
+++ b/solution.py
@@ -17,7 +17,7 @@
 WIDTH = 1024
 FFB = 328
 PAD = 384
-QB = 256
+QB = 320
 BACK_QB = 320
 VMEM = 60 * 1024 * 1024
 

time: 290 us -> 290 us (level)
  no operation moved by 1% of the time
where the time goes in v6:
time: 290 us; the launch traced here: 288 us
  waiting for transfers between devices  97.6 us (34%)
  starting transfers between devices  76.4 us (26%)
  Pallas kernels  63.1 us (22%)
  other arithmetic  21.7 us (7%)
  between operations  14.3 us (5%)
  local copies, waits for them, and re-layouts  13 us (4%)
    ppermute x23, waiting for transfers between devices, exchange(): return lax.ppermute(value, axes, [(i, i ^ mask) for i in range(count)])  40.2 us
    ppermute x23, starting transfers between devices, exchange(): return lax.ppermute(value, axes, [(i, i ^ mask) for i in range(count)])  40 us
    all_to_all x1, waiting for transfers between devices, on_device(): lax.all_to_all(jnp.broadcast_to(pair[None], (M, PRE, ROWS, WIDTH)), MLP_A...  21 us
    pallas_call x1, Pallas kernels, attend_back(): pl.pallas_call(attend_back_kernel, grid=(1,), in_specs=[pl.BlockSpec(memo...  14.9 us
    pallas_call x2, Pallas kernels, mlp(): pl.pallas_call(functools.partial(mlp_kernel, count), grid=(1,), in_specs=...  14.8 us
    pallas_call x1, Pallas kernels, mlp_grads(): pl.pallas_call(mlp_grads_kernel, grid=(PRE,), in_specs=[whole(ROWS, WIDTH...  12.4 us
    pallas_call x1, Pallas kernels, attend(): pl.pallas_call(attend_kernel, grid=(1,), in_specs=[ROWS_SPEC, QKV_SPEC, w...  12.1 us
    all_to_all x1, waiting for transfers between devices, on_device(): gm_own = lax.all_to_all(gm_parts, TP, 0, 0).reshape(LEN, 2 * HD)  8.62 us
  transfers between devices with their start and end apart: 33, of which 12 were waited for; matrix products, arithmetic and copies ran while one was open for 9% of the time, Pallas kernels for 18%

profile of v6, /device:TPU:0, one launch (start us, length us, event | category | flops | bytes accessed | tf_op | source)
XLA Modules:
  0.0 288.5 jit_solution(15636194331428727580)
XLA Ops:
  7.2 4.0 %collective-permute-start = (bf16[160,1024]{1,0:T(8,128)(2,1)}, bf16[160,1024]{1,0:T(8,128)(2,1)S(1)}, u32[]{:S(2)}, u32[]{:S(2)}) collective-permute-start(bf16[160,1024]{1,0:T(8,128)(2,1)} %param.10), channel_id=1, source_target_pairs={{0,1},{1,0},{2,3},{3,2},{4,5},{5,4},{6,7},{7,6},{8,9},{9,8},{10,11... | collective-permute-start | bytes 983048 | tf_op jit(solution)/shard_map/ppermute | solution.py:36
  11.3 7.9 %collective-permute-done = bf16[160,1024]{1,0:T(8,128)(2,1)S(1)} collective-permute-done((bf16[160,1024]{1,0:T(8,128)(2,1)}, bf16[160,1024]{1,0:T(8,128)(2,1)S(1)}, u32[]{:S(2)}, u32[]{:S(2)}) %collective-permute-start) | collective-permute-done | bytes 327712 | tf_op jit(solution)/shard_map/ppermute | solution.py:36
  20.6 7.1 %all-to-all-start = ((bf16[8,64,128]{2,1,0:T(8,128)(2,1)}), bf16[8,64,128]{2,1,0:T(8,128)(2,1)S(1)}, u32[]{:S(2)}, u32[]{:S(2)}) async-start(bf16[8,64,128]{2,1,0:T(8,128)(2,1)} %broadcast_in_dim.13), calls=%async_computation | async-start | bytes 262144 | tf_op jit(solution)/shard_map/all_to_all | solution.py:421
  27.8 7.8 %all-to-all-done = bf16[8,64,128]{2,1,0:T(8,128)(2,1)S(1)} async-done(((bf16[8,64,128]{2,1,0:T(8,128)(2,1)}), bf16[8,64,128]{2,1,0:T(8,128)(2,1)S(1)}, u32[]{:S(2)}, u32[]{:S(2)}) %all-to-all-start) | async-done | bytes 131104 | tf_op jit(solution)/shard_map/all_to_all | solution.py:421
  40.5 3.8 %all-to-all-start.1 = ((bf16[4,2,160,1024]{3,2,1,0:T(8,128)(2,1)}), bf16[4,2,160,1024]{3,2,1,0:T(8,128)(2,1)S(1)}, u32[]{:S(2)}, u32[]{:S(2)}) async-start(bf16[4,2,160,1024]{3,2,1,0:T(8,128)(2,1)} %broadcast_in_dim.15), calls=%async_computation.1 | async-start | bytes 5242880 | tf_op jit(solution)/shard_map/all_to_all | solution.py:442
  45.5 7.7 %collective-permute-done.1 = bf16[3,64,384]{2,1,0:T(8,128)(2,1)} collective-permute-done((bf16[3,64,384]{2,1,0:T(8,128)(2,1)S(1)}, bf16[3,64,384]{2,1,0:T(8,128)(2,1)}, u32[]{:S(2)}, u32[]{:S(2)}) %collective-permute-start.1) | collective-permute-done | bytes 147488 | tf_op jit(solution)/shard_map/ppermute | solution.py:36
  53.2 21.0 %all-to-all-done.1 = bf16[4,2,160,1024]{3,2,1,0:T(8,128)(2,1)S(1)} async-done(((bf16[4,2,160,1024]{3,2,1,0:T(8,128)(2,1)}), bf16[4,2,160,1024]{3,2,1,0:T(8,128)(2,1)S(1)}, u32[]{:S(2)}, u32[]{:S(2)}) %all-to-all-start.1) | async-done | bytes 2621472 | tf_op jit(solution)/shard_map/all_to_all | solution.py:442
  80.9 12.1 %attend.1 = (bf16[1280,128]{1,0:T(8,128)(2,1)}, bf16[1280,128]{1,0:T(8,128)(2,1)}, bf16[1280,128]{1,0:T(8,128)(2,1)}, bf16[1280,128]{1,0:T(8,128)(2,1)}, f32[1280,128]{1,0:T(8,128)}) custom-call(bf16[8,160,1024]{2,1,0:T(8,128)(2,1)} %bitcast.91, bf16[16,4,64,384]{3,2,1,0:T(8,128)(2,1)} %bitcast.93, f32[1280,128]{1,0:T(8,128)} %constant.67.clone.cos_ref.refs_5_, ...), custom_call_target="tpu_custom_call" | custom-call | flops 6000000000 | bytes 8000000 | tf_op jit(solution)/shard_map/attend/pallas_call | solution.py:147
  93.0 3.5 %all-to-all-start.2 = ((bf16[8,160,128]{2,1,0:T(8,128)(2,1)}), bf16[8,160,128]{2,1,0:T(8,128)(2,1)S(1)}, u32[]{:S(2)}, u32[]{:S(2)}) async-start(bf16[8,160,128]{2,1,0:T(8,128)(2,1)} %bitcast.99), calls=%async_computation.2 | async-start | bytes 655360 | tf_op jit(solution)/shard_map/all_to_all | solution.py:451
  98.5 6.8 %all-to-all-done.2 = bf16[8,160,128]{2,1,0:T(8,128)(2,1)S(1)} async-done(((bf16[8,160,128]{2,1,0:T(8,128)(2,1)}), bf16[8,160,128]{2,1,0:T(8,128)(2,1)S(1)}, u32[]{:S(2)}, u32[]{:S(2)}) %all-to-all-start.2) | async-done | bytes 327712 | tf_op jit(solution)/shard_map/all_to_all | solution.py:451
  108.4 2.7 collective-permute-start.6
  113.3 4.2 %collective-permute-done.5.refs_1_ = bf16[160,1024]{1,0:T(8,128)(2,1)} collective-permute-done((bf16[160,1024]{1,0:T(8,128)(2,1)}, bf16[160,1024]{1,0:T(8,128)(2,1)}, u32[]{:S(2)}, u32[]{:S(2)}) %collective-permute-start.5) | collective-permute-done | bytes 327712 | tf_op jit(solution)/shard_map/ppermute | solution.py:36
  117.6 7.4 %mlp.2 = (bf16[2,320,384]{2,1,0:T(8,128)(2,1)}, bf16[2,2,320,384]{3,2,1,0:T(8,128)(2,1)}, bf16[160,1024]{1,0:T(8,128)(2,1)}, bf16[160,1024]{1,0:T(8,128)(2,1)}) custom-call(bf16[160,1024]{1,0:T(8,128)(2,1)} %multiply_convert_fusion.refs_0_, bf16[160,1024]{1,0:T(8,128)(2,1)} %collective-permute-done.5.refs_1_, bf16[160,1024]{1,0:T(8,128)(2,1)} %refs_4_, ...), custom_call_target="tpu_custom_call" | custom-call | flops 5000000000 | bytes 8000000 | tf_op jit(solution)/shard_map/mlp/pallas_call | solution.py:304
  125.0 7.4 %mlp.3 = (bf16[2,320,384]{2,1,0:T(8,128)(2,1)}, bf16[2,2,320,384]{3,2,1,0:T(8,128)(2,1)}, bf16[160,1024]{1,0:T(8,128)(2,1)}, bf16[160,1024]{1,0:T(8,128)(2,1)}) custom-call(bf16[160,1024]{1,0:T(8,128)(2,1)} %collective-permute-done.6.refs_0_.refs_2_, bf16[160,1024]{1,0:T(8,128)(2,1)} %collective-permute-done.7.refs_1_.refs_3_, ...), custom_call_target="tpu_custom_call" | custom-call | flops 5000000000 | bytes 8000000 | tf_op jit(solution)/shard_map/mlp/pallas_call | solution.py:304
  136.5 12.4 %mlp_grads.1 = (bf16[8,2,9,64,384]{4,3,2,1,0:T(8,128)(2,1)}, bf16[160,1024]{1,0:T(8,128)(2,1)}, bf16[160,1024]{1,0:T(8,128)(2,1)}, bf16[160,1024]{1,0:T(8,128)(2,1)}, bf16[160,1024]{1,0:T(8,128)(2,1)}) custom-call(bf16[160,1024]{1,0:T(8,128)(2,1)} %multiply_convert_fusion.refs_0_, bf16[160,1024]{1,0:T(8,128)(2,1)} %collective-permute-done.5.refs_1_, ...), custom_call_target="tpu_custom_call" | custom-call | flops 8000000000 | bytes 12000000 | tf_op jit(solution)/shard_map/mlp_grads/pallas_call | solution.py:362
  153.5 3.5 %out_grads.1 = bf16[8,2,9,64,384]{4,3,2,1,0:T(8,128)(2,1)} custom-call(bf16[160,1024]{1,0:T(8,128)(2,1)} %copy-done.2, bf16[160,1152]{1,0:T(8,128)(2,1)} %pad.13.mixed_ref, bf16[8,2,9,64,384]{4,3,2,1,0:T(8,128)(2,1)} %get-tuple-element.129.held_ref), custom_call_target="tpu_custom_call", output_to_operand_aliasing={{}: (2, {})} | custom-call | flops 400000000 | bytes 4000000 | tf_op jit(solution)/shard_map/out_grads/pallas_call | solution.py:395
  157.1 6.9 %all-to-all-start.3 = ((bf16[8,160,128]{2,1,0:T(8,128)(2,1)}), bf16[8,160,128]{2,1,0:T(8,128)(2,1)S(1)}, u32[]{:S(2)}, u32[]{:S(2)}) async-start(bf16[8,160,128]{2,1,0:T(8,128)(2,1)} %bitcast_bitcast_fusion), calls=%async_computation.3 | async-start | bytes 655360 | tf_op jit(solution)/shard_map/all_to_all | solution.py:481
  164.0 8.6 %all-to-all-done.3 = bf16[8,160,128]{2,1,0:T(8,128)(2,1)S(1)} async-done(((bf16[8,160,128]{2,1,0:T(8,128)(2,1)}), bf16[8,160,128]{2,1,0:T(8,128)(2,1)S(1)}, u32[]{:S(2)}, u32[]{:S(2)}) %all-to-all-start.3) | async-done | bytes 327712 | tf_op jit(solution)/shard_map/all_to_all | solution.py:481
  173.2 2.4 collective-permute-start.12
  177.4 14.9 %attend_back.1 = (bf16[1280,384]{1,0:T(8,128)(2,1)}, bf16[160,1024]{1,0:T(8,128)(2,1)}, bf16[160,1024]{1,0:T(8,128)(2,1)}, bf16[160,1024]{1,0:T(8,128)(2,1)}, bf...) custom-call(s32[1]{0:T(128)} %bitcast.16.me_ref, ...), custom_call_target="tpu_custom_call" | custom-call | flops 12000000000 | bytes 8000000 | tf_op jit(solution)/shard_map/attend_back/pallas_call | solution.py:202
  194.0 5.4 %qkv_grads.1 = bf16[16,64,384]{2,1,0:T(8,128)(2,1)} custom-call(bf16[8,160,1024]{2,1,0:T(8,128)(2,1)} %bitcast.92, bf16[1280,384]{1,0:T(8,128)(2,1)} %get-tuple-element.127.g_ref), custom_call_target="tpu_custom_call" | custom-call | flops 2000000000 | bytes 5000000 | tf_op jit(solution)/shard_map/qkv_grads/pallas_call | solution.py:231
  199.4 3.7 %collective-permute-start.16 = (bf16[160,1024]{1,0:T(8,128)(2,1)}, bf16[160,1024]{1,0:T(8,128)(2,1)}, u32[]{:S(2)}, u32[]{:S(2)}) collective-permute-start(bf16[160,1024]{1,0:T(8,128)(2,1)} %get-tuple-element.122), channel_id=1, source_target_pairs={{0,3},{1,2},{2,1},{3,0},{4,7},{5,6},{6,5},{7,4},{8,11},{9,10},{10,... | collective-permute-start | bytes 983048 | tf_op jit(solution)/shard_map/ppermute | solution.py:36
  204.0 3.4 %collective-permute-start.18 = (bf16[160,1024]{1,0:T(8,128)(2,1)}, bf16[160,1024]{1,0:T(8,128)(2,1)}, u32[]{:S(2)}, u32[]{:S(2)}) collective-permute-start(bf16[160,1024]{1,0:T(8,128)(2,1)} %get-tuple-element.124), channel_id=1, source_target_pairs={{0,5},{1,4},{2,7},{3,6},{4,1},{5,0},{6,3},{7,2},{8,13},{9,12},{10,... | collective-permute-start | bytes 983048 | tf_op jit(solution)/shard_map/ppermute | solution.py:36
  208.5 3.7 %collective-permute-start.20 = (bf16[160,1024]{1,0:T(8,128)(2,1)}, bf16[160,1024]{1,0:T(8,128)(2,1)}, u32[]{:S(2)}, u32[]{:S(2)}) collective-permute-start(bf16[160,1024]{1,0:T(8,128)(2,1)} %get-tuple-element.126), channel_id=1, source_target_pairs={{0,7},{1,6},{2,5},{3,4},{4,3},{5,2},{6,1},{7,0},{8,15},{9,14},{10,... | collective-permute-start | bytes 983048 | tf_op jit(solution)/shard_map/ppermute | solution.py:36
  214.5 3.8 %all-to-all-start.4 = ((bf16[16,80,384]{2,1,0:T(8,128)(2,1)}), bf16[16,80,384]{2,1,0:T(8,128)(2,1)S(1)}, u32[]{:S(2)}, u32[]{:S(2)}) async-start(bf16[16,80,384]{2,1,0:T(8,128)(2,1)} %pad_maximum_fusion), calls=%async_computation.4 | async-start | bytes 1966080 | tf_op jit(solution)/shard_map/all_to_all | solution.py:497
  220.3 4.9 %collective-permute-done.18 = bf16[160,1024]{1,0:T(8,128)(2,1)} collective-permute-done((bf16[160,1024]{1,0:T(8,128)(2,1)}, bf16[160,1024]{1,0:T(8,128)(2,1)}, u32[]{:S(2)}, u32[]{:S(2)}) %collective-permute-start.18) | collective-permute-done | bytes 327712 | tf_op jit(solution)/shard_map/ppermute | solution.py:36
  225.2 4.7 %collective-permute-done.19 = bf16[160,1024]{1,0:T(8,128)(2,1)} collective-permute-done((bf16[160,1024]{1,0:T(8,128)(2,1)}, bf16[160,1024]{1,0:T(8,128)(2,1)}, u32[]{:S(2)}, u32[]{:S(2)}) %collective-permute-start.19) | collective-permute-done | bytes 327712 | tf_op jit(solution)/shard_map/ppermute | solution.py:36
  229.9 10.7 %collective-permute-done.20 = bf16[160,1024]{1,0:T(8,128)(2,1)} collective-permute-done((bf16[160,1024]{1,0:T(8,128)(2,1)}, bf16[160,1024]{1,0:T(8,128)(2,1)}, u32[]{:S(2)}, u32[]{:S(2)}) %collective-permute-start.20) | collective-permute-done | bytes 327712 | tf_op jit(solution)/shard_map/ppermute | solution.py:36
  248.2 7.1 %all-to-all-start.5 = ((f32[128,1,128]{2,1,0:T(1,128)}), f32[128,1,128]{2,1,0:T(1,128)}, u32[]{:S(2)}, u32[]{:S(2)}) async-start(f32[128,1,128]{2,1,0:T(1,128)} %broadcast_in_dim.17), calls=%async_computation.5 | async-start | bytes 131072 | tf_op jit(solution)/shard_map/all_to_all | solution.py:515
  257.7 6.6 %all-to-all-done.5 = f32[128,1,128]{2,1,0:T(1,128)} async-done(((f32[128,1,128]{2,1,0:T(1,128)}), f32[128,1,128]{2,1,0:T(1,128)}, u32[]{:S(2)}, u32[]{:S(2)}) %all-to-all-start.5) | async-done | bytes 65568 | tf_op jit(solution)/shard_map/all_to_all | solution.py:515
  267.8 4.1 %all-to-all-start.6 = ((bf16[8,64,128]{2,1,0:T(8,128)(2,1)}), bf16[8,64,128]{2,1,0:T(8,128)(2,1)S(1)}, u32[]{:S(2)}, u32[]{:S(2)}) async-start(bf16[8,64,128]{2,1,0:T(8,128)(2,1)} %bitcast_bitcast_fusion.1), calls=%async_computation.7 | async-start | bytes 262144 | tf_op jit(solution)/shard_map/all_to_all | solution.py:516
  273.2 6.5 %all-to-all-done.6 = bf16[8,64,128]{2,1,0:T(8,128)(2,1)S(1)} async-done(((bf16[8,64,128]{2,1,0:T(8,128)(2,1)}), bf16[8,64,128]{2,1,0:T(8,128)(2,1)S(1)}, u32[]{:S(2)}, u32[]{:S(2)}) %all-to-all-start.6) | async-done | bytes 131104 | tf_op jit(solution)/shard_map/all_to_all | solution.py:516
  (162 shorter events, 57.4 us)
Async XLA Ops:
  7.2 12.0 %collective-permute-start = (bf16[160,1024]{1,0:T(8,128)(2,1)}, bf16[160,1024]{1,0:T(8,128)(2,1)S(1)}, u32[]{:S(2)}, u32[]{:S(2)}) collective-permute-start(bf16[160,1024]{1,0:T(8,128)(2,1)} %param.10), channel_id=1, source_target_pairs={{0,1},{1,0},{2,3},{3,2},{4,5},{5,4},{6,7},{7,6},{8,9},{9,8},{10,11... | collective-permute-start | bytes 983048 | tf_op jit(solution)/shard_map/ppermute | solution.py:36
  20.6 15.1 %all-to-all-start = ((bf16[8,64,128]{2,1,0:T(8,128)(2,1)}), bf16[8,64,128]{2,1,0:T(8,128)(2,1)S(1)}, u32[]{:S(2)}, u32[]{:S(2)}) async-start(bf16[8,64,128]{2,1,0:T(8,128)(2,1)} %broadcast_in_dim.13), calls=%async_computation | async-start | bytes 262144 | tf_op jit(solution)/shard_map/all_to_all | solution.py:421
  27.7 53.2 %all-gather.5.cloned.1.call-start = ((), (), s32[]{:S(2)}) async-start(), calls=%async_computation.9 | async-start | bytes 3342336 | tf_op jit(solution)/shard_map/all_gather | solution.py:425
  40.5 33.8 %all-to-all-start.1 = ((bf16[4,2,160,1024]{3,2,1,0:T(8,128)(2,1)}), bf16[4,2,160,1024]{3,2,1,0:T(8,128)(2,1)S(1)}, u32[]{:S(2)}, u32[]{:S(2)}) async-start(bf16[4,2,160,1024]{3,2,1,0:T(8,128)(2,1)} %broadcast_in_dim.15), calls=%async_computation.1 | async-start | bytes 5242880 | tf_op jit(solution)/shard_map/all_to_all | solution.py:442
  44.3 73.3 %all-gather.7.cloned.1.call-start = ((), (), s32[]{:S(2)}) async-start(), calls=%async_computation.10 | async-start | bytes 5013504 | tf_op jit(solution)/shard_map/all_gather | solution.py:445
  76.1 16.9 %collective-permute-start.2 = (bf16[160,1024]{1,0:T(8,128)(2,1)S(1)}, bf16[160,1024]{1,0:T(8,128)(2,1)}, u32[]{:S(2)}, u32[]{:S(2)}) collective-permute-start(bf16[160,1024]{1,0:T(8,128)(2,1)S(1)} %copy-done.6), channel_id=1, source_target_pairs={{0,2},{2,0},{4,6},{6,4},{1,3},{3,1},{5,7},{7,5},{8,10},{10,8},{12,... | collective-permute-start | bytes 983048 | tf_op jit(solution)/shard_map/ppermute | solution.py:36
  76.8 16.3 %collective-permute-start.3 = (bf16[160,1024]{1,0:T(8,128)(2,1)S(1)}, bf16[160,1024]{1,0:T(8,128)(2,1)}, u32[]{:S(2)}, u32[]{:S(2)}) collective-permute-start(bf16[160,1024]{1,0:T(8,128)(2,1)S(1)} %copy-done.6), channel_id=1, source_target_pairs={{0,4},{2,6},{4,0},{6,2},{1,5},{3,7},{5,1},{7,3},{8,12},{10,14},{12... | collective-permute-start | bytes 983048 | tf_op jit(solution)/shard_map/ppermute | solution.py:36
  78.8 14.2 %collective-permute-start.4 = (bf16[160,1024]{1,0:T(8,128)(2,1)S(1)}, bf16[160,1024]{1,0:T(8,128)(2,1)}, u32[]{:S(2)}, u32[]{:S(2)}) collective-permute-start(bf16[160,1024]{1,0:T(8,128)(2,1)S(1)} %copy-done.6), channel_id=1, source_target_pairs={{0,6},{2,4},{4,2},{6,0},{1,7},{3,5},{5,3},{7,1},{8,14},{10,12},{12... | collective-permute-start | bytes 983048 | tf_op jit(solution)/shard_map/ppermute | solution.py:36
  93.0 12.2 %all-to-all-start.2 = ((bf16[8,160,128]{2,1,0:T(8,128)(2,1)}), bf16[8,160,128]{2,1,0:T(8,128)(2,1)S(1)}, u32[]{:S(2)}, u32[]{:S(2)}) async-start(bf16[8,160,128]{2,1,0:T(8,128)(2,1)} %bitcast.99), calls=%async_computation.2 | async-start | bytes 655360 | tf_op jit(solution)/shard_map/all_to_all | solution.py:451
  96.5 148.7 %reduce-scatter.2.cloned.1.call-start = ((), (), s32[]{:S(2)}) async-start(), calls=%async_computation.8 | async-start | bytes 7962624 | tf_op jit(solution)/shard_map/reduce_scatter | solution.py:480
  107.8 9.7 %collective-permute-start.5 = (bf16[160,1024]{1,0:T(8,128)(2,1)}, bf16[160,1024]{1,0:T(8,128)(2,1)}, u32[]{:S(2)}, u32[]{:S(2)}) collective-permute-start(bf16[160,1024]{1,0:T(8,128)(2,1)} %multiply_convert_fusion.refs_0_), channel_id=1, source_target_pairs={{0,2},{2,0},{4,6},{6,4},{1,3},{3,1},{5,7},{7,5},{8,10},{10,8},{12,... | collective-permute-start | bytes 983048 | tf_op jit(solution)/shard_map/ppermute | solution.py:36
  108.4 16.6 %collective-permute-start.6 = (bf16[160,1024]{1,0:T(8,128)(2,1)}, bf16[160,1024]{1,0:T(8,128)(2,1)}, u32[]{:S(2)}, u32[]{:S(2)}) collective-permute-start(bf16[160,1024]{1,0:T(8,128)(2,1)} %multiply_convert_fusion.refs_0_), channel_id=1, source_target_pairs={{0,4},{2,6},{4,0},{6,2},{1,5},{3,7},{5,1},{7,3},{8,12},{10,14},{12... | collective-permute-start | bytes 983048 | tf_op jit(solution)/shard_map/ppermute | solution.py:36
  111.1 13.9 %collective-permute-start.7 = (bf16[160,1024]{1,0:T(8,128)(2,1)}, bf16[160,1024]{1,0:T(8,128)(2,1)}, u32[]{:S(2)}, u32[]{:S(2)}) collective-permute-start(bf16[160,1024]{1,0:T(8,128)(2,1)} %multiply_convert_fusion.refs_0_), channel_id=1, source_target_pairs={{0,6},{2,4},{4,2},{6,0},{1,7},{3,5},{5,3},{7,1},{8,14},{10,12},{12... | collective-permute-start | bytes 983048 | tf_op jit(solution)/shard_map/ppermute | solution.py:36
  132.4 16.5 %collective-permute-start.10 = (bf16[160,1024]{1,0:T(8,128)(2,1)}, bf16[160,1024]{1,0:T(8,128)(2,1)}, u32[]{:S(2)}, u32[]{:S(2)}) collective-permute-start(bf16[160,1024]{1,0:T(8,128)(2,1)} %get-tuple-element.96), channel_id=1, source_target_pairs={{0,6},{2,4},{4,2},{6,0},{1,7},{3,5},{5,3},{7,1},{8,14},{10,12},{12... | collective-permute-start | bytes 983048 | tf_op jit(solution)/shard_map/ppermute | solution.py:36
  133.8 15.1 %collective-permute-start.9 = (bf16[160,1024]{1,0:T(8,128)(2,1)}, bf16[160,1024]{1,0:T(8,128)(2,1)}, u32[]{:S(2)}, u32[]{:S(2)}) collective-permute-start(bf16[160,1024]{1,0:T(8,128)(2,1)} %get-tuple-element.95), channel_id=1, source_target_pairs={{0,4},{2,6},{4,0},{6,2},{1,5},{3,7},{5,1},{7,3},{8,12},{10,14},{12... | collective-permute-start | bytes 983048 | tf_op jit(solution)/shard_map/ppermute | solution.py:36
  134.7 14.1 %collective-permute-start.8 = (bf16[160,1024]{1,0:T(8,128)(2,1)}, bf16[160,1024]{1,0:T(8,128)(2,1)}, u32[]{:S(2)}, u32[]{:S(2)}) collective-permute-start(bf16[160,1024]{1,0:T(8,128)(2,1)} %get-tuple-element.94), channel_id=1, source_target_pairs={{0,2},{2,0},{4,6},{6,4},{1,3},{3,1},{5,7},{7,5},{8,10},{10,8},{12,... | collective-permute-start | bytes 983048 | tf_op jit(solution)/shard_map/ppermute | solution.py:36
  157.1 15.6 %all-to-all-start.3 = ((bf16[8,160,128]{2,1,0:T(8,128)(2,1)}), bf16[8,160,128]{2,1,0:T(8,128)(2,1)S(1)}, u32[]{:S(2)}, u32[]{:S(2)}) async-start(bf16[8,160,128]{2,1,0:T(8,128)(2,1)} %bitcast_bitcast_fusion), calls=%async_computation.3 | async-start | bytes 655360 | tf_op jit(solution)/shard_map/all_to_all | solution.py:481
  172.7 19.6 %collective-permute-start.11 = (bf16[160,1024]{1,0:T(8,128)(2,1)S(1)}, bf16[160,1024]{1,0:T(8,128)(2,1)S(1)}, u32[]{:S(2)}, u32[]{:S(2)}) collective-permute-start(bf16[160,1024]{1,0:T(8,128)(2,1)S(1)} %copy-done.23), channel_id=1, source_target_pairs={{0,2},{2,0},{4,6},{6,4},{1,3},{3,1},{5,7},{7,5},{8,10},{10,8},{12,... | collective-permute-start | bytes 983048 | tf_op jit(solution)/shard_map/ppermute | solution.py:36
  173.2 19.1 %collective-permute-start.12 = (bf16[160,1024]{1,0:T(8,128)(2,1)S(1)}, bf16[160,1024]{1,0:T(8,128)(2,1)S(1)}, u32[]{:S(2)}, u32[]{:S(2)}) collective-permute-start(bf16[160,1024]{1,0:T(8,128)(2,1)S(1)} %copy-done.22), channel_id=1, source_target_pairs={{0,4},{2,6},{4,0},{6,2},{1,5},{3,7},{5,1},{7,3},{8,12},{10,14},{12... | collective-permute-start | bytes 983048 | tf_op jit(solution)/shard_map/ppermute | solution.py:36
  175.6 16.7 %collective-permute-start.13 = (bf16[160,1024]{1,0:T(8,128)(2,1)S(1)}, bf16[160,1024]{1,0:T(8,128)(2,1)S(1)}, u32[]{:S(2)}, u32[]{:S(2)}) collective-permute-start(bf16[160,1024]{1,0:T(8,128)(2,1)S(1)} %copy-done.21), channel_id=1, source_target_pairs={{0,6},{2,4},{4,2},{6,0},{1,7},{3,5},{5,3},{7,1},{8,14},{10,12},{12... | collective-permute-start | bytes 983048 | tf_op jit(solution)/shard_map/ppermute | solution.py:36
  192.3 15.1 %collective-permute-start.14 = (bf16[160,1024]{1,0:T(8,128)(2,1)}, bf16[160,1024]{1,0:T(8,128)(2,1)S(1)}, u32[]{:S(2)}, u32[]{:S(2)}) collective-permute-start(bf16[160,1024]{1,0:T(8,128)(2,1)} %get-tuple-element.120), channel_id=1, source_target_pairs={{0,1},{1,0},{2,3},{3,2},{4,5},{5,4},{6,7},{7,6},{8,9},{9,8},{10,11... | collective-permute-start | bytes 983048 | tf_op jit(solution)/shard_map/ppermute | solution.py:36
  193.9 14.6 %collective-permute-start.15 = (bf16[160,1024]{1,0:T(8,128)(2,1)}, bf16[160,1024]{1,0:T(8,128)(2,1)S(1)}, u32[]{:S(2)}, u32[]{:S(2)}) collective-permute-start(bf16[160,1024]{1,0:T(8,128)(2,1)} %get-tuple-element.121), channel_id=1, source_target_pairs={{0,2},{1,3},{2,0},{3,1},{4,6},{5,7},{6,4},{7,5},{8,10},{9,11},{10,... | collective-permute-start | bytes 983048 | tf_op jit(solution)/shard_map/ppermute | solution.py:36
  199.4 20.9 %collective-permute-start.16 = (bf16[160,1024]{1,0:T(8,128)(2,1)}, bf16[160,1024]{1,0:T(8,128)(2,1)}, u32[]{:S(2)}, u32[]{:S(2)}) collective-permute-start(bf16[160,1024]{1,0:T(8,128)(2,1)} %get-tuple-element.122), channel_id=1, source_target_pairs={{0,3},{1,2},{2,1},{3,0},{4,7},{5,6},{6,5},{7,4},{8,11},{9,10},{10,... | collective-permute-start | bytes 983048 | tf_op jit(solution)/shard_map/ppermute | solution.py:36
  203.1 17.2 %collective-permute-start.17 = (bf16[160,1024]{1,0:T(8,128)(2,1)}, bf16[160,1024]{1,0:T(8,128)(2,1)}, u32[]{:S(2)}, u32[]{:S(2)}) collective-permute-start(bf16[160,1024]{1,0:T(8,128)(2,1)} %get-tuple-element.123), channel_id=1, source_target_pairs={{0,4},{1,5},{2,6},{3,7},{4,0},{5,1},{6,2},{7,3},{8,12},{9,13},{10,... | collective-permute-start | bytes 983048 | tf_op jit(solution)/shard_map/ppermute | solution.py:36
  204.0 21.2 %collective-permute-start.18 = (bf16[160,1024]{1,0:T(8,128)(2,1)}, bf16[160,1024]{1,0:T(8,128)(2,1)}, u32[]{:S(2)}, u32[]{:S(2)}) collective-permute-start(bf16[160,1024]{1,0:T(8,128)(2,1)} %get-tuple-element.124), channel_id=1, source_target_pairs={{0,5},{1,4},{2,7},{3,6},{4,1},{5,0},{6,3},{7,2},{8,13},{9,12},{10,... | collective-permute-start | bytes 983048 | tf_op jit(solution)/shard_map/ppermute | solution.py:36
  207.4 22.5 %collective-permute-start.19 = (bf16[160,1024]{1,0:T(8,128)(2,1)}, bf16[160,1024]{1,0:T(8,128)(2,1)}, u32[]{:S(2)}, u32[]{:S(2)}) collective-permute-start(bf16[160,1024]{1,0:T(8,128)(2,1)} %get-tuple-element.125), channel_id=1, source_target_pairs={{0,6},{1,7},{2,4},{3,5},{4,2},{5,3},{6,0},{7,1},{8,14},{9,15},{10,... | collective-permute-start | bytes 983048 | tf_op jit(solution)/shard_map/ppermute | solution.py:36
  208.5 32.0 %collective-permute-start.20 = (bf16[160,1024]{1,0:T(8,128)(2,1)}, bf16[160,1024]{1,0:T(8,128)(2,1)}, u32[]{:S(2)}, u32[]{:S(2)}) collective-permute-start(bf16[160,1024]{1,0:T(8,128)(2,1)} %get-tuple-element.126), channel_id=1, source_target_pairs={{0,7},{1,6},{2,5},{3,4},{4,3},{5,2},{6,1},{7,0},{8,15},{9,14},{10,... | collective-permute-start | bytes 983048 | tf_op jit(solution)/shard_map/ppermute | solution.py:36
  214.5 29.3 %all-to-all-start.4 = ((bf16[16,80,384]{2,1,0:T(8,128)(2,1)}), bf16[16,80,384]{2,1,0:T(8,128)(2,1)S(1)}, u32[]{:S(2)}, u32[]{:S(2)}) async-start(bf16[16,80,384]{2,1,0:T(8,128)(2,1)} %pad_maximum_fusion), calls=%async_computation.4 | async-start | bytes 1966080 | tf_op jit(solution)/shard_map/all_to_all | solution.py:497
  246.4 18.8 %collective-permute-start.21 = (bf16[9,64,384]{2,1,0:T(8,128)(2,1)S(1)}, bf16[9,64,384]{2,1,0:T(8,128)(2,1)S(1)}, u32[]{:S(2)}, u32[]{:S(2)}) collective-permute-start(bf16[9,64,384]{2,1,0:T(8,128)(2,1)S(1)} %dynamic-slice_bitcast_fusion), channel_id=1, source_target_pairs={{0,16},{16,0},{1,17},{17,1},{2,18},{18,2},{3,19},{19,3},{4,20},{20... | collective-permute-start | bytes 1327112 | tf_op jit(solution)/shard_map/ppermute | solution.py:36
  248.2 16.1 %all-to-all-start.5 = ((f32[128,1,128]{2,1,0:T(1,128)}), f32[128,1,128]{2,1,0:T(1,128)}, u32[]{:S(2)}, u32[]{:S(2)}) async-start(f32[128,1,128]{2,1,0:T(1,128)} %broadcast_in_dim.17), calls=%async_computation.5 | async-start | bytes 131072 | tf_op jit(solution)/shard_map/all_to_all | solution.py:515
  265.4 15.0 %collective-permute-start.22 = (bf16[3,64,384]{2,1,0:T(8,128)(2,1)S(1)}, bf16[3,64,384]{2,1,0:T(8,128)(2,1)S(1)}, u32[]{:S(2)}, u32[]{:S(2)}) collective-permute-start(bf16[3,64,384]{2,1,0:T(8,128)(2,1)S(1)} %get-tuple-element.186), channel_id=1, source_target_pairs={{0,1},{1,0},{2,3},{3,2},{4,5},{5,4},{6,7},{7,6},{8,9},{9,8},{10,11... | collective-permute-start | bytes 442376 | tf_op jit(solution)/shard_map/ppermute | solution.py:36
  267.8 12.0 %all-to-all-start.6 = ((bf16[8,64,128]{2,1,0:T(8,128)(2,1)}), bf16[8,64,128]{2,1,0:T(8,128)(2,1)S(1)}, u32[]{:S(2)}, u32[]{:S(2)}) async-start(bf16[8,64,128]{2,1,0:T(8,128)(2,1)} %bitcast_bitcast_fusion.1), calls=%async_computation.7 | async-start | bytes 262144 | tf_op jit(solution)/shard_map/all_to_all | solution.py:516
  (25 other events, 748.6 us)
Sparse Core Ops, SparseCore 0:
  36.6 34.3 all-gather.4
  76.2 38.6 all-gather.6
  157.2 46.3 reduce-scatter.1
